TPU v7x, 32 devices: a whole 2x2x4 slice. The times are simulated.
32 devices in a mesh: slab: 8 (over z, x), hodlr: 4 (over y, core).
Axes of the slice: x: 2, y: 2, z: 4, core: 2. Of those that a mesh axis runs over, the one named last changes fastest.
Arguments:
- sources: bfloat16 [8, 32, 16384], P('slab', None, 'hodlr'), may hold values from -2 to 2
- leaves: bfloat16 [8, 16, 1024, 1024], P('slab', 'hodlr'), may hold values from -1 to 2
- v_rows: bfloat16 [8, 4, 64, 16384], P('slab', None, None, 'hodlr'), may hold values from -0.0625 to 0.0625
- u_rows: bfloat16 [8, 4, 64, 16384], P('slab', None, None, 'hodlr'), may hold values from -0.1875 to 0.1875
Outputs:
- fronts: bfloat16 [8, 32, 16384], P('slab', None, 'hodlr')
All inputs are finite; a program needn't handle non-finite values.
Results may differ from a plain program's by a relative error of at most 0.025.
Values may be sent and summed in bfloat16 or wider, within the bound.
No kernel may reach another device: no remote copies, remote signals or barrier semaphores. Data moves between devices by JAX's collectives and lax.ppermute only.
A program may use at most 64 MiB of HBM per device.

v0:
```python
import functools

import jax
import jax.numpy as jnp
from jax import lax
from jax.experimental import pallas as pl
from jax.experimental.pallas import tpu as pltpu
from jax.sharding import PartitionSpec as P

VMEM_LIMIT = 24 * 1024 * 1024
FIRST_SHARE = 2
IN_PLACE = 2
WHOLE_HOP = 3
OPEN_FLOPS = 4 * 10**9
ROWS_TIMES_COLUMNS = (((1,), (0,)), ((), ()))
ROWS_TIMES_ROWS = (((1,), (1,)), ((), ()))


def dot(a, b, dims=ROWS_TIMES_COLUMNS):
    return lax.dot_general(a, b, dims, preferred_element_type=jnp.float32)


def call(kernel, outs, args, aliases=None, scratch=(), from_hbm=(), flops=0):
    whole = pl.BlockSpec(memory_space=pltpu.VMEM)
    remote = pl.BlockSpec(memory_space=pl.ANY)
    placed = [
        pltpu.with_memory_space_constraint(a, pltpu.HBM if i in from_hbm else pltpu.VMEM)
        for i, a in enumerate(args)
    ]
    return pl.pallas_call(
        kernel,
        out_shape=outs,
        in_specs=[remote if i in from_hbm else whole for i in range(len(args))],
        out_specs=[whole] * len(outs),
        scratch_shapes=scratch,
        input_output_aliases=aliases or {},
        compiler_params=pltpu.CompilerParams(vmem_limit_bytes=VMEM_LIMIT),
        cost_estimate=pl.CostEstimate(flops=flops, bytes_accessed=0, transcendentals=0),
    )(*placed)


def on_factors(value, v_refs, columns, ranks):
    pieces = [dot(value, ref[:, columns], ROWS_TIMES_ROWS) for ref in v_refs]
    missing = ranks - sum(ref.shape[0] for ref in v_refs)
    if missing:
        pieces.append(jnp.zeros((value.shape[0], missing), jnp.float32))
    return jnp.concatenate(pieces, axis=1)


def fetch_kernel(spans, source_ref, v_ref, *refs):
    v_outs, w_outs, sems = refs[: -1 - len(spans)], refs[-1 - len(spans) : -1], refs[-1]
    copies, level = [], 0
    for out in v_outs[:-1]:
        copies.append((v_ref.at[pl.ds(level, out.shape[0])], out))
        level += out.shape[0]
    first = jnp.where(lax.axis_index("slab") == 1, 0, 1)
    copies.append((v_ref.at[pl.ds(first, v_outs[-1].shape[0])], v_outs[-1]))
    for out, (start, stop) in zip(w_outs, spans):
        copies.append((source_ref.at[:, pl.ds(start, stop - start)], out))
    copies = [pltpu.make_async_copy(a, b, sems.at[i]) for i, (a, b) in enumerate(copies)]
    for copy in copies:
        copy.start()
    for copy in copies:
        copy.wait()


def fetch(spans, cross, source, v):
    _, rank, width = v.shape
    shares = (cross - 1, 1, cross - 1)
    outs = [pltpu.VMEM((n, rank, width), v.dtype) for n in shares]
    outs += [pltpu.VMEM((source.shape[0], stop - start), source.dtype) for start, stop in spans]
    found = call(
        functools.partial(fetch_kernel, spans),
        outs,
        [source, v],
        scratch=[pltpu.SemaphoreType.DMA((len(outs),))],
        from_hbm=(0, 1),
    )
    return [f.reshape(-1, width) for f in found[: len(shares)]], list(found[len(shares) :])


def behind_kernel(x_ref, other_ref, out_ref):
    out_ref[...] = x_ref[...]


def put_behind(x, other):
    return call(behind_kernel, [pltpu.VMEM(x.shape, x.dtype)], [x, other], flops=OPEN_FLOPS)[0]


def project_kernel(spans, factors, *refs):
    v_refs, parts, p_ref = refs[:factors], refs[factors:-1], refs[-1]
    total = None
    for ref, (start, stop) in zip(parts, spans):
        term = on_factors(ref[...], v_refs, slice(start, stop), p_ref.shape[1])
        total = term if total is None else total + term
    p_ref[...] = total.astype(p_ref.dtype)


def project(spans, w, far_v, ranks, flops=0):
    outs = [pltpu.VMEM((w[0].shape[0], ranks), jnp.bfloat16)]
    return call(functools.partial(project_kernel, spans, len(far_v)), outs, [*far_v, *w], flops=flops)[0]


def turn_kernel(size, *refs):
    v_refs, out_ref = refs[:-1], refs[-1]
    for c in range(out_ref.shape[0] // size):
        rows = slice(c * size, (c + 1) * size)
        out_ref[rows, :] = jnp.concatenate([ref[:, rows] for ref in v_refs], axis=0).T


def turn(size, v):
    outs = [pltpu.VMEM((v[0].shape[1], sum(x.shape[0] for x in v)), v[0].dtype)]
    return call(functools.partial(turn_kernel, size), outs, v)[0]


def project_turned_kernel(spans, v_ref, *refs):
    parts, p_ref = refs[:-1], refs[-1]
    total = None
    for ref, (start, stop) in zip(parts, spans):
        term = dot(ref[...], v_ref[start:stop, :])
        total = term if total is None else total + term
    p_ref[...] = total.astype(p_ref.dtype)


def project_turned(spans, w, v):
    outs = [pltpu.VMEM((w[0].shape[0], v.shape[1]), jnp.bfloat16)]
    return call(functools.partial(project_turned_kernel, spans), outs, [v, *w])[0]


def leaves_of(span, size):
    return range(span[0] // size, span[1] // size)


def first_kernel(spans, cross, *refs):
    n = len(spans)
    w_refs, (leaf_ref, v_ref), near_out = refs[:n], refs[n : n + 2], refs[n + 2]
    sum_refs, p_refs = refs[n + 3 : 2 * n + 3], refs[2 * n + 3 :]
    size = leaf_ref.shape[1]
    near = p_refs[0].shape[2]
    for i, span in enumerate(spans):
        for j, c in enumerate(leaves_of(span, size)):
            columns = slice(j * size, (j + 1) * size)
            turned = v_ref[cross:, :, c * size : (c + 1) * size].reshape(near, size).T
            group = near_out.shape[2] // near
            near_out[c // group, :, c % group * near : (c % group + 1) * near] = turned
            p_refs[i][j] = dot(w_refs[i][:, columns], turned)
            sum_refs[i][:, columns] = dot(w_refs[i][:, columns], leaf_ref[c])


def first_part(spans, cross, w, leaf, v):
    levels, rank, width = v.shape
    size = leaf.shape[1]
    rows = w[0].shape[0]
    near = (levels - cross) * rank
    group = 2 if all((stop - start) // size % 2 == 0 for start, stop in spans) else 1
    outs = [pltpu.VMEM((width // size // group, size, group * near), v.dtype)]
    outs += [pltpu.VMEM(x.shape, jnp.float32) for x in w]
    outs += [pltpu.VMEM((x.shape[1] // size, rows, near), jnp.float32) for x in w]
    n = len(w)
    found = call(functools.partial(first_kernel, spans, cross), outs, [*w, leaf, v])
    return found[0], list(found[1 : 1 + n]), list(found[1 + n :])


def nearby_kernel(rank, levels_of, front_ref, v_ref, *refs):
    part_refs, p_ref = refs[: len(levels_of)], refs[-1]
    term = dot(front_ref[...], v_ref[...], ROWS_TIMES_ROWS)
    rows, ranks = p_ref.shape
    before = ranks - term.shape[1]
    if before:
        term = jnp.concatenate([jnp.zeros((rows, before), jnp.float32), term], axis=1)
    lane = lax.broadcasted_iota(jnp.int32, (rows, ranks), 1) // rank
    for ref, level in zip(part_refs, levels_of):
        term = term + jnp.where(lane == level, ref[...].astype(jnp.float32), 0.0)
    p_ref[...] = term.astype(p_ref.dtype)


def nearby_part(rank, front, v, ranks, parts, levels_of, behind, flops=0):
    outs = [pltpu.VMEM((front.shape[0], ranks), jnp.bfloat16)]
    return call(functools.partial(nearby_kernel, rank, tuple(levels_of)), outs, [front, v, *parts, *behind], flops=flops)[0]


def near_kernel(span, start, w_ref, front_ref, leaf_ref, v_ref, *refs):
    w_out, sum_out, p_out = refs[-3:]
    size = leaf_ref.shape[1]
    rows = w_ref.shape[0]
    near = p_out.shape[2]
    group = v_ref.shape[2] // near
    members = []
    for j, c in enumerate(leaves_of(span, size)):
        columns = slice(j * size, (j + 1) * size)
        w = w_ref[:, columns] + front_ref[:, start + j * size : start + (j + 1) * size]
        w_out[:, columns] = w
        members.append(w)
        if len(members) == group:
            both = dot(jnp.concatenate(members, axis=0), v_ref[c // group])
            for i in range(group):
                p_out[j - group + 1 + i] = both[i * rows : (i + 1) * rows, i * near : (i + 1) * near]
            members = []
        sum_out[:, columns] = dot(w, leaf_ref[c])


def near_part(span, start, near, w, front, leaf, near_v, behind):
    outs = [
        pltpu.VMEM(w.shape, w.dtype),
        pltpu.VMEM(w.shape, jnp.float32),
        pltpu.VMEM((w.shape[1] // leaf.shape[1], w.shape[0], near), jnp.float32),
    ]
    return call(functools.partial(near_kernel, span, start), outs, [w, front, leaf, near_v, *behind], {0: 0})


def far_kernel(rank, size, spans, chosen, levels_of, *refs):
    refs = list(refs)
    sum_refs = [refs.pop(0) for _ in chosen]
    p_refs = [refs.pop(0) for _ in spans]
    q_ref = refs.pop(0)
    part_refs = [refs.pop(0) for _ in levels_of]
    u_ref = refs.pop(0)
    out_ref, q_out = refs[:2]
    rows, far = q_ref.shape
    near = u_ref.shape[0] - far

    q = q_ref[...]
    lane = lax.broadcasted_iota(jnp.int32, (rows, far), 1) // rank
    for ref, level in zip(part_refs, levels_of):
        part = ref[...].astype(jnp.float32)
        q = q + (part if level is None else jnp.where(lane == level, part, 0.0))
    q_out[...] = q

    projected = [ref[j] for ref in p_refs for j in range(ref.shape[0])]
    nleaf = len(projected)
    lane = lax.broadcasted_iota(jnp.int32, (rows, near), 1) // rank
    sums = []
    for level in range(near // rank):
        block = nleaf >> (level + 1)
        sums.append(
            [
                functools.reduce(jnp.add, projected[b * block : (b + 1) * block])
                for b in range(nleaf // block)
            ]
        )
    place = 0
    for i, ref in zip(chosen, sum_refs):
        for j, c in enumerate(leaves_of(spans[i], size)):
            swapped = sums[0][(c // (nleaf >> 1)) ^ 1]
            for level in range(1, near // rank):
                swapped = jnp.where(lane == level, sums[level][(c // (nleaf >> (level + 1))) ^ 1], swapped)
            columns = slice(c * size, (c + 1) * size)
            value = ref[:, j * size : (j + 1) * size]
            value = value + dot(q.astype(jnp.bfloat16), u_ref[:far, columns])
            value = value + dot(swapped.astype(jnp.bfloat16), u_ref[far:, columns])
            out_ref[:, place : place + size] = value.astype(jnp.bfloat16)
            place += size


def far_part(rank, size, spans, chosen, sums, projected, q, parts, levels_of, u, last):
    args = [*[sums[i] for i in chosen], *projected, q, *parts, u]
    width = sum(sums[i].shape[1] for i in chosen)
    space = jax.ShapeDtypeStruct if last else pltpu.VMEM
    outs = [space((q.shape[0], width), jnp.bfloat16), pltpu.VMEM(q.shape, jnp.float32)]
    kernel = functools.partial(far_kernel, rank, size, spans, chosen, tuple(levels_of) if parts else ())
    return call(kernel, outs, args, {len(chosen) + len(projected): 1})


def local(sources, leaves, v_rows, u_rows):
    devices = lax.axis_size("hodlr")
    chain = lax.axis_size("slab")
    cross = devices.bit_length() - 1
    source, right = sources[0], v_rows[0]
    levels, rank, width = right.shape
    nleaf, size = leaves.shape[1:3]
    cut = max(nleaf * FIRST_SHARE // 4, 1) * size
    spans = ((0, cut), (cut, width))
    offsets = list(range(1, devices))
    levels_of = [cross - x.bit_length() for x in offsets]

    def moved(x, moves, offset=0):
        route = [(a * devices + h, b * devices + (h ^ offset)) for a, b in moves for h in range(devices)]
        return lax.ppermute(x, ("slab", "hodlr"), route)

    def exchanged(p, moves):
        return [moved(p, moves, x) for x in offsets]

    (coarse_v, fine_v, ahead_v), w = fetch(spans, cross, source, right)
    later = [(k, k - 1) for k in range(IN_PLACE + 1, chain)]
    early = moved(ahead_v, [(1, 0)] + later)
    coarse = moved(coarse_v, later)
    ranks = cross * rank
    whole = ((0, width),)
    p = project(spans, w, [coarse_v, fine_v], ranks, OPEN_FLOPS)
    parts = exchanged(p, [(k, k) for k in range(chain)])
    leaf, u = leaves[0], u_rows[0].reshape(levels * rank, width)
    near_v, sums, projected = first_part(spans, cross, w, leaf, right)

    q = jnp.zeros(p.shape, jnp.float32)
    every = tuple(range(len(spans)))
    far = functools.partial(far_part, rank, size, spans)
    out, q = far(every, sums, projected, q, parts, levels_of, u, False)
    front = [moved(out, [(0, 1)])]
    ahead = [project(whole, [out], [early], ranks)]
    relayed = offsets[1::2]
    parts = [moved(ahead[0], [(0, 1)], x) for x in relayed]
    second = moved(put_behind(coarse_v, ahead[0]), [(2, 1)])
    levels_relayed = [cross - x.bit_length() for x in relayed]
    for k in range(1, chain):
        levels_now = levels_of[::-1]
        if k <= IN_PLACE:
            if k == IN_PLACE:
                turned = turn(size, [coarse, early[-rank:]])
            behind = ahead if k == 1 else [turned]
            nearby = nearby_part(rank, front[0], fine_v, ranks, parts, levels_relayed, behind, OPEN_FLOPS)
            parts = [moved(nearby, [(k, k)], offsets[0])] + parts
            levels_now = [None] + levels_relayed
        for i, span in enumerate(spans):
            behind = projected[i - 1 : i] if i else []
            given, start = (front[0], span[0]) if len(front) == 1 else (front[i], 0)
            w[i], sums[i], projected[i] = near_part(span, start, (levels - cross) * rank, w[i], given, leaf, near_v, behind)
        if k == chain - 1:
            out, _ = far(every, sums, projected, q, parts, levels_now, u, True)
            return out[None]
        split = k >= IN_PLACE and k != WHOLE_HOP
        outs, front = [], []
        for chosen in [(i,) for i in every] if split else [every]:
            out, q = far(chosen, sums, projected, q, [] if front else parts, levels_now, u, False)
            outs.append(out)
            front.append(moved(out, [(k, k + 1)]))
        if k < IN_PLACE:
            p = project(whole, outs, [second], ranks)
        else:
            p = project_turned(spans if split else whole, outs, turned)
        sent = relayed if k < IN_PLACE else offsets[::-1]
        parts = [moved(p, [(k, k + 1)], x) for x in sent]


def solution(mesh):
    in_specs = (
        P("slab", None, "hodlr"),
        P("slab", "hodlr", None, None),
        P("slab", None, None, "hodlr"),
        P("slab", None, None, "hodlr"),
    )
    out_specs = P("slab", None, "hodlr")
    return jax.shard_map(local, mesh=mesh, in_specs=in_specs, out_specs=out_specs, check_vma=False)
```

profile of v0, /device:TPU:26, one launch (start us, length us, event | category | flops | bytes accessed | tf_op | source)
XLA Modules:
  0.0 94.5 jit_solution(2368878801134412572)
XLA Ops:
  0.0 1.6 %shard_map.46 = (bf16[1,64,4096]{2,1,0:T(8,128)(2,1)S(1)}, bf16[1,64,4096]{2,1,0:T(8,128)(2,1)S(1)}, bf16[1,64,4096]{2,1,0:T(8,128)(2,1)S(1)}, bf16[32,2048]{1,0:T(8,128)(2,1)S(1)}, bf16[32,2048]{1,0:T(8,128)(2,1)S(1)}) custom-call(bf16[32,4096]{1,0:T(8,128)(2,1)} %bitcast.46, bf16[4,64,4096]{2,1,0:T(8,128)(2,1)} %bitcast.37), custom_call_target="tpu_custom_call" | custom-call | tf_op jit(solution)/shard_map/pallas_call | solution.py:30
  1.6 2.6 %collective-permute-start.4 = (bf16[64,4096]{1,0:T(8,128)(2,1)S(1)}, bf16[64,4096]{1,0:T(8,128)(2,1)S(1)}, u32[]{:S(2)}, u32[]{:S(2)}) collective-permute-start(bf16[64,4096]{1,0:T(8,128)(2,1)S(1)} %bitcast.45), channel_id=1, source_target_pairs={{4,0},{5,1},{6,2},{7,3},{12,8},{13,9},{14,10},{15,11},{16,12},{17,... | collective-permute-start | bytes 1572872 | tf_op jit(solution)/shard_map/ppermute | solution.py:278
  4.3 0.4 shard_map.48
  4.8 1.6 %collective-permute-start.1 = (bf16[32,128]{1,0:T(8,128)(2,1)S(1)}, bf16[32,128]{1,0:T(8,128)(2,1)S(1)}, u32[]{:S(2)}, u32[]{:S(2)}) collective-permute-start(bf16[32,128]{1,0:T(8,128)(2,1)S(1)} %shard_map.48), channel_id=1, source_target_pairs={{0,2},{1,3},{2,0},{3,1},{4,6},{5,7},{6,4},{7,5},{8,10},{9,11},{10,... | collective-permute-start | bytes 24584 | tf_op jit(solution)/shard_map/ppermute | solution.py:278
  6.3 0.3 collective-permute-start.2
  6.6 3.3 %collective-permute-start.10 = (bf16[64,4096]{1,0:T(8,128)(2,1)S(1)}, bf16[64,4096]{1,0:T(8,128)(2,1)S(1)}, u32[]{:S(2)}, u32[]{:S(2)}) collective-permute-start(bf16[64,4096]{1,0:T(8,128)(2,1)S(1)} %bitcast.43), channel_id=1, source_target_pairs={{12,8},{13,9},{14,10},{15,11},{16,12},{17,13},{18,14},{19,15},{20,... | collective-permute-start | bytes 1572872 | tf_op jit(solution)/shard_map/ppermute | solution.py:278
  9.9 1.8 %shard_map.47 = (bf16[2,1024,256]{2,1,0:T(8,128)(2,1)S(1)}, f32[32,2048]{1,0:T(8,128)S(1)}, f32[32,2048]{1,0:T(8,128)S(1)}, f32[2,32,128]{2,1,0:T(8,128)S(1)}, f32[2,32,128]{2,1,0:T(8,128)S(1)}) custom-call(bf16[32,2048]{1,0:T(8,128)(2,1)S(1)} %get-tuple-element.78.refs_0_.refs_2_.w_ref, bf16[32,2048]{1,0:T(8,128)(2,1)S(1)} %get-tuple-element.79.refs_1_.refs_3_.w_ref, ...), custom_call_target="tpu_custom_call" | custom-call | tf_op jit(solution)/shard_map/pallas_call | solution.py:30
  11.8 0.4 shard_map.49
  12.2 0.7 collective-permute-start.3
  12.9 3.6 %collective-permute-done.4.refs_0_.refs_1_ = bf16[64,4096]{1,0:T(8,128)(2,1)S(1)} collective-permute-done((bf16[64,4096]{1,0:T(8,128)(2,1)S(1)}, bf16[64,4096]{1,0:T(8,128)(2,1)S(1)}, u32[]{:S(2)}, u32[]{:S(2)}) %collective-permute-start.4) | collective-permute-done | bytes 524320 | tf_op jit(solution)/shard_map/ppermute | solution.py:278
  16.8 0.7 collective-permute-start.5
  17.5 0.7 collective-permute-start.8
  18.2 0.3 shard_map.53
  18.5 0.7 collective-permute-start.6
  19.2 0.9 shard_map.50
  20.1 0.9 shard_map.51
  21.1 0.4 shard_map.54
  21.5 0.7 collective-permute-start.7
  22.4 0.7 collective-permute-start.9
  23.1 3.5 %collective-permute-done.10.refs_0_ = bf16[64,4096]{1,0:T(8,128)(2,1)S(1)} collective-permute-done((bf16[64,4096]{1,0:T(8,128)(2,1)S(1)}, bf16[64,4096]{1,0:T(8,128)(2,1)S(1)}, u32[]{:S(2)}, u32[]{:S(2)}) %collective-permute-start.10) | collective-permute-done | bytes 524320 | tf_op jit(solution)/shard_map/ppermute | solution.py:278
  26.6 0.3 shard_map.59.refs_1_.v_ref
  26.9 0.3 shard_map.60
  27.3 0.7 collective-permute-start.11
  27.9 0.9 shard_map.55
  28.9 0.9 shard_map.56
  30.1 0.7 collective-permute-start.12
  31.0 0.7 collective-permute-start.13
  32.0 0.7 collective-permute-start.14
  32.6 0.7 collective-permute-start.15
  33.3 0.7 collective-permute-start.16
  34.0 0.9 shard_map.62
  34.9 0.9 shard_map.64
  35.9 0.4 shard_map.66
  36.3 0.7 collective-permute-start.17
  37.0 0.3 shard_map.69
  37.3 0.7 collective-permute-start.18
  37.9 0.7 collective-permute-start.19
  38.6 0.7 collective-permute-start.20
  39.3 0.9 shard_map.67
  40.2 0.9 shard_map.68
  41.4 0.7 collective-permute-start.21
  42.4 0.7 collective-permute-start.22
  43.3 0.7 collective-permute-start.23
  44.0 0.7 collective-permute-start.24
  44.7 0.8 collective-permute-start.25
  45.5 0.9 shard_map.71
  46.5 0.9 shard_map.73
  47.7 0.7 collective-permute-start.26
  48.6 0.7 collective-permute-start.27
  49.6 0.7 collective-permute-start.28
  50.3 0.7 collective-permute-start.29
  50.9 0.7 collective-permute-start.30
  51.6 0.9 shard_map.76
  52.5 0.9 shard_map.78
  53.8 1.3 %collective-permute-start.31 = (bf16[32,2048]{1,0:T(8,128)(2,1)S(1)}, bf16[32,2048]{1,0:T(8,128)(2,1)S(1)}, u32[]{:S(2)}, u32[]{:S(2)}) collective-permute-start(bf16[32,2048]{1,0:T(8,128)(2,1)S(1)} %get-tuple-element.140.refs_0_), channel_id=1, source_target_pairs={{24,28},{25,29},{26,30},{27,31}} | collective-permute-start | bytes 393224 | tf_op jit(solution)/shard_map/ppermute | solution.py:278
  55.3 1.3 %collective-permute-start.32 = (bf16[32,2048]{1,0:T(8,128)(2,1)S(1)}, bf16[32,2048]{1,0:T(8,128)(2,1)S(1)}, u32[]{:S(2)}, u32[]{:S(2)}) collective-permute-start(bf16[32,2048]{1,0:T(8,128)(2,1)S(1)} %get-tuple-element.145.refs_1_), channel_id=1, source_target_pairs={{24,28},{25,29},{26,30},{27,31}} | collective-permute-start | bytes 393224 | tf_op jit(solution)/shard_map/ppermute | solution.py:278
  56.9 1.3 %collective-permute-start.33 = (bf16[32,128]{1,0:T(8,128)(2,1)S(1)}, bf16[32,128]{1,0:T(8,128)(2,1)S(1)}, u32[]{:S(2)}, u32[]{:S(2)}) collective-permute-start(bf16[32,128]{1,0:T(8,128)(2,1)S(1)} %shard_map.84), channel_id=1, source_target_pairs={{24,31},{25,30},{26,29},{27,28}} | collective-permute-start | bytes 24584 | tf_op jit(solution)/shard_map/ppermute | solution.py:278
  58.2 1.3 %collective-permute-start.34 = (bf16[32,128]{1,0:T(8,128)(2,1)S(1)}, bf16[32,128]{1,0:T(8,128)(2,1)S(1)}, u32[]{:S(2)}, u32[]{:S(2)}) collective-permute-start(bf16[32,128]{1,0:T(8,128)(2,1)S(1)} %shard_map.84), channel_id=1, source_target_pairs={{24,30},{25,31},{26,28},{27,29}} | collective-permute-start | bytes 24584 | tf_op jit(solution)/shard_map/ppermute | solution.py:278
  59.5 1.3 %collective-permute-start.35 = (bf16[32,128]{1,0:T(8,128)(2,1)S(1)}, bf16[32,128]{1,0:T(8,128)(2,1)S(1)}, u32[]{:S(2)}, u32[]{:S(2)}) collective-permute-start(bf16[32,128]{1,0:T(8,128)(2,1)S(1)} %shard_map.84), channel_id=1, source_target_pairs={{24,29},{25,28},{26,31},{27,30}} | collective-permute-start | bytes 24584 | tf_op jit(solution)/shard_map/ppermute | solution.py:278
  60.8 29.6 %collective-permute-done.31.front_ref = bf16[32,2048]{1,0:T(8,128)(2,1)S(1)} collective-permute-done((bf16[32,2048]{1,0:T(8,128)(2,1)S(1)}, bf16[32,2048]{1,0:T(8,128)(2,1)S(1)}, u32[]{:S(2)}, u32[]{:S(2)}) %collective-permute-start.31) | collective-permute-done | bytes 131104 | tf_op jit(solution)/shard_map/ppermute | solution.py:278
  90.4 0.9 shard_map.81
  91.3 1.1 %collective-permute-done.32.front_ref = bf16[32,2048]{1,0:T(8,128)(2,1)S(1)} collective-permute-done((bf16[32,2048]{1,0:T(8,128)(2,1)S(1)}, bf16[32,2048]{1,0:T(8,128)(2,1)S(1)}, u32[]{:S(2)}, u32[]{:S(2)}) %collective-permute-start.32) | collective-permute-done | bytes 131104 | tf_op jit(solution)/shard_map/ppermute | solution.py:278
  92.4 0.9 shard_map.83
  93.3 1.1 %shard_map.85 = (bf16[32,4096]{1,0:T(8,128)(2,1)}, f32[32,128]{1,0:T(8,128)S(1)}) custom-call(f32[32,2048]{1,0:T(8,128)S(1)} %get-tuple-element.141.refs_0_, f32[32,2048]{1,0:T(8,128)S(1)} %get-tuple-element.147.refs_1_, f32[2,32,128]{2,1,0:T(8,128)S(1)} %get-tuple-element.146.refs_0_.refs_2_, ...), custom_call_target="tpu_custom_call", output_to_operand_aliasing={{1}: (4, {})} | custom-call | tf_op jit(solution)/shard_map/pallas_call | solution.py:30
  (58 shorter events, 4.0 us)
Async XLA Ops:
  0.0 9.9 %slice-start = ((s8[8388608]{0:T(1024)(128)(4,1)}), s8[4194304]{0:T(1024)(128)(4,1)S(1)}, s32[]{:S(2)}) async-start(s8[8388608]{0:T(1024)(128)(4,1)} %bitcast.8), calls=%async_computation | async-start | bytes 8388608
  1.6 14.9 %collective-permute-start.4 = (bf16[64,4096]{1,0:T(8,128)(2,1)S(1)}, bf16[64,4096]{1,0:T(8,128)(2,1)S(1)}, u32[]{:S(2)}, u32[]{:S(2)}) collective-permute-start(bf16[64,4096]{1,0:T(8,128)(2,1)S(1)} %bitcast.45), channel_id=1, source_target_pairs={{4,0},{5,1},{6,2},{7,3},{12,8},{13,9},{14,10},{15,11},{16,12},{17,... | collective-permute-start | bytes 1572872 | tf_op jit(solution)/shard_map/ppermute | solution.py:278
  4.2 5.7 %slice-start.1 = ((s8[8388608]{0:T(1024)(128)(4,1)}), s8[4194304]{0:T(1024)(128)(4,1)S(1)}, s32[]{:S(2)}) async-start(s8[8388608]{0:T(1024)(128)(4,1)} %bitcast.8), calls=%async_computation.1 | async-start | bytes 8388608
  4.2 5.7 %copy-start.1 = (bf16[1,4,64,4096]{3,2,1,0:T(8,128)(2,1)S(1)}, bf16[1,4,64,4096]{3,2,1,0:T(8,128)(2,1)}, u32[]{:S(2)}) copy-start(bf16[1,4,64,4096]{3,2,1,0:T(8,128)(2,1)} %param.6) | copy-start | bytes 6291460
  4.7 7.1 %collective-permute-start = (bf16[32,128]{1,0:T(8,128)(2,1)S(1)}, bf16[32,128]{1,0:T(8,128)(2,1)S(1)}, u32[]{:S(2)}, u32[]{:S(2)}) collective-permute-start(bf16[32,128]{1,0:T(8,128)(2,1)S(1)} %shard_map.48), channel_id=1, source_target_pairs={{0,1},{1,0},{2,3},{3,2},{4,5},{5,4},{6,7},{7,6},{8,9},{9,8},{10,11... | collective-permute-start | bytes 24584 | tf_op jit(solution)/shard_map/ppermute | solution.py:278
  4.8 7.0 %collective-permute-start.1 = (bf16[32,128]{1,0:T(8,128)(2,1)S(1)}, bf16[32,128]{1,0:T(8,128)(2,1)S(1)}, u32[]{:S(2)}, u32[]{:S(2)}) collective-permute-start(bf16[32,128]{1,0:T(8,128)(2,1)S(1)} %shard_map.48), channel_id=1, source_target_pairs={{0,2},{1,3},{2,0},{3,1},{4,6},{5,7},{6,4},{7,5},{8,10},{9,11},{10,... | collective-permute-start | bytes 24584 | tf_op jit(solution)/shard_map/ppermute | solution.py:278
  6.3 5.4 %collective-permute-start.2 = (bf16[32,128]{1,0:T(8,128)(2,1)S(1)}, bf16[32,128]{1,0:T(8,128)(2,1)S(1)}, u32[]{:S(2)}, u32[]{:S(2)}) collective-permute-start(bf16[32,128]{1,0:T(8,128)(2,1)S(1)} %shard_map.48), channel_id=1, source_target_pairs={{0,3},{1,2},{2,1},{3,0},{4,7},{5,6},{6,5},{7,4},{8,11},{9,10},{10,... | collective-permute-start | bytes 24584 | tf_op jit(solution)/shard_map/ppermute | solution.py:278
  6.6 20.0 %collective-permute-start.10 = (bf16[64,4096]{1,0:T(8,128)(2,1)S(1)}, bf16[64,4096]{1,0:T(8,128)(2,1)S(1)}, u32[]{:S(2)}, u32[]{:S(2)}) collective-permute-start(bf16[64,4096]{1,0:T(8,128)(2,1)S(1)} %bitcast.43), channel_id=1, source_target_pairs={{12,8},{13,9},{14,10},{15,11},{16,12},{17,13},{18,14},{19,15},{20,... | collective-permute-start | bytes 1572872 | tf_op jit(solution)/shard_map/ppermute | solution.py:278
  9.9 1.9 %copy-start = (bf16[1,4,64,4096]{3,2,1,0:T(8,128)(2,1)S(1)}, bf16[1,4,64,4096]{3,2,1,0:T(8,128)(2,1)}, u32[]{:S(2)}) copy-start(bf16[1,4,64,4096]{3,2,1,0:T(8,128)(2,1)} %param.7) | copy-start | bytes 6291460
  12.2 6.0 %collective-permute-start.3 = (bf16[32,4096]{1,0:T(8,128)(2,1)S(1)}, bf16[32,4096]{1,0:T(8,128)(2,1)S(1)}, u32[]{:S(2)}, u32[]{:S(2)}) collective-permute-start(bf16[32,4096]{1,0:T(8,128)(2,1)S(1)} %get-tuple-element.86.refs_1_), channel_id=1, source_target_pairs={{0,4},{1,5},{2,6},{3,7}} | collective-permute-start | bytes 786440 | tf_op jit(solution)/shard_map/ppermute | solution.py:278
  16.8 1.4 %collective-permute-start.5 = (bf16[32,128]{1,0:T(8,128)(2,1)S(1)}, bf16[32,128]{1,0:T(8,128)(2,1)S(1)}, u32[]{:S(2)}, u32[]{:S(2)}) collective-permute-start(bf16[32,128]{1,0:T(8,128)(2,1)S(1)} %shard_map.52.refs_1_.other_ref), channel_id=1, source_target_pairs={{0,6},{1,7},{2,4},{3,5}} | collective-permute-start | bytes 24584 | tf_op jit(solution)/shard_map/ppermute | solution.py:278
  17.5 4.7 %collective-permute-start.8 = (bf16[64,4096]{1,0:T(8,128)(2,1)S(1)}, bf16[64,4096]{1,0:T(8,128)(2,1)S(1)}, u32[]{:S(2)}, u32[]{:S(2)}) collective-permute-start(bf16[64,4096]{1,0:T(8,128)(2,1)S(1)} %shard_map.57), channel_id=1, source_target_pairs={{8,4},{9,5},{10,6},{11,7}} | collective-permute-start | bytes 1572872 | tf_op jit(solution)/shard_map/ppermute | solution.py:278
  18.5 2.5 %collective-permute-start.6 = (bf16[32,128]{1,0:T(8,128)(2,1)S(1)}, bf16[32,128]{1,0:T(8,128)(2,1)S(1)}, u32[]{:S(2)}, u32[]{:S(2)}) collective-permute-start(bf16[32,128]{1,0:T(8,128)(2,1)S(1)} %shard_map.53), channel_id=1, source_target_pairs={{4,5},{5,4},{6,7},{7,6}} | collective-permute-start | bytes 24584 | tf_op jit(solution)/shard_map/ppermute | solution.py:278
  21.5 5.5 %collective-permute-start.7 = (bf16[32,4096]{1,0:T(8,128)(2,1)S(1)}, bf16[32,4096]{1,0:T(8,128)(2,1)S(1)}, u32[]{:S(2)}, u32[]{:S(2)}) collective-permute-start(bf16[32,4096]{1,0:T(8,128)(2,1)S(1)} %get-tuple-element.95.refs_1_), channel_id=1, source_target_pairs={{4,8},{5,9},{6,10},{7,11}} | collective-permute-start | bytes 786440 | tf_op jit(solution)/shard_map/ppermute | solution.py:278
  22.4 4.5 %collective-permute-start.9 = (bf16[32,128]{1,0:T(8,128)(2,1)S(1)}, bf16[32,128]{1,0:T(8,128)(2,1)S(1)}, u32[]{:S(2)}, u32[]{:S(2)}) collective-permute-start(bf16[32,128]{1,0:T(8,128)(2,1)S(1)} %shard_map.58), channel_id=1, source_target_pairs={{4,10},{5,11},{6,8},{7,9}} | collective-permute-start | bytes 24584 | tf_op jit(solution)/shard_map/ppermute | solution.py:278
  27.3 2.5 %collective-permute-start.11 = (bf16[32,128]{1,0:T(8,128)(2,1)S(1)}, bf16[32,128]{1,0:T(8,128)(2,1)S(1)}, u32[]{:S(2)}, u32[]{:S(2)}) collective-permute-start(bf16[32,128]{1,0:T(8,128)(2,1)S(1)} %shard_map.60), channel_id=1, source_target_pairs={{8,9},{9,8},{10,11},{11,10}} | collective-permute-start | bytes 24584 | tf_op jit(solution)/shard_map/ppermute | solution.py:278
  30.1 3.9 %collective-permute-start.12 = (bf16[32,2048]{1,0:T(8,128)(2,1)S(1)}, bf16[32,2048]{1,0:T(8,128)(2,1)S(1)}, u32[]{:S(2)}, u32[]{:S(2)}) collective-permute-start(bf16[32,2048]{1,0:T(8,128)(2,1)S(1)} %get-tuple-element.102.refs_0_), channel_id=1, source_target_pairs={{8,12},{9,13},{10,14},{11,15}} | collective-permute-start | bytes 393224 | tf_op jit(solution)/shard_map/ppermute | solution.py:278
  31.0 3.9 %collective-permute-start.13 = (bf16[32,2048]{1,0:T(8,128)(2,1)S(1)}, bf16[32,2048]{1,0:T(8,128)(2,1)S(1)}, u32[]{:S(2)}, u32[]{:S(2)}) collective-permute-start(bf16[32,2048]{1,0:T(8,128)(2,1)S(1)} %get-tuple-element.108.refs_1_), channel_id=1, source_target_pairs={{8,12},{9,13},{10,14},{11,15}} | collective-permute-start | bytes 393224 | tf_op jit(solution)/shard_map/ppermute | solution.py:278
  32.0 3.9 %collective-permute-start.14 = (bf16[32,128]{1,0:T(8,128)(2,1)S(1)}, bf16[32,128]{1,0:T(8,128)(2,1)S(1)}, u32[]{:S(2)}, u32[]{:S(2)}) collective-permute-start(bf16[32,128]{1,0:T(8,128)(2,1)S(1)} %shard_map.65), channel_id=1, source_target_pairs={{8,15},{9,14},{10,13},{11,12}} | collective-permute-start | bytes 24584 | tf_op jit(solution)/shard_map/ppermute | solution.py:278
  32.6 3.2 %collective-permute-start.15 = (bf16[32,128]{1,0:T(8,128)(2,1)S(1)}, bf16[32,128]{1,0:T(8,128)(2,1)S(1)}, u32[]{:S(2)}, u32[]{:S(2)}) collective-permute-start(bf16[32,128]{1,0:T(8,128)(2,1)S(1)} %shard_map.65), channel_id=1, source_target_pairs={{8,14},{9,15},{10,12},{11,13}} | collective-permute-start | bytes 24584 | tf_op jit(solution)/shard_map/ppermute | solution.py:278
  33.3 2.5 %collective-permute-start.16 = (bf16[32,128]{1,0:T(8,128)(2,1)S(1)}, bf16[32,128]{1,0:T(8,128)(2,1)S(1)}, u32[]{:S(2)}, u32[]{:S(2)}) collective-permute-start(bf16[32,128]{1,0:T(8,128)(2,1)S(1)} %shard_map.65), channel_id=1, source_target_pairs={{8,13},{9,12},{10,15},{11,14}} | collective-permute-start | bytes 24584 | tf_op jit(solution)/shard_map/ppermute | solution.py:278
  36.3 3.0 %collective-permute-start.17 = (bf16[32,4096]{1,0:T(8,128)(2,1)S(1)}, bf16[32,4096]{1,0:T(8,128)(2,1)S(1)}, u32[]{:S(2)}, u32[]{:S(2)}) collective-permute-start(bf16[32,4096]{1,0:T(8,128)(2,1)S(1)} %get-tuple-element.113.refs_0_), channel_id=1, source_target_pairs={{12,16},{13,17},{14,18},{15,19}} | collective-permute-start | bytes 786440 | tf_op jit(solution)/shard_map/ppermute | solution.py:278
  37.3 3.9 %collective-permute-start.18 = (bf16[32,128]{1,0:T(8,128)(2,1)S(1)}, bf16[32,128]{1,0:T(8,128)(2,1)S(1)}, u32[]{:S(2)}, u32[]{:S(2)}) collective-permute-start(bf16[32,128]{1,0:T(8,128)(2,1)S(1)} %shard_map.69), channel_id=1, source_target_pairs={{12,19},{13,18},{14,17},{15,16}} | collective-permute-start | bytes 24584 | tf_op jit(solution)/shard_map/ppermute | solution.py:278
  37.9 3.2 %collective-permute-start.19 = (bf16[32,128]{1,0:T(8,128)(2,1)S(1)}, bf16[32,128]{1,0:T(8,128)(2,1)S(1)}, u32[]{:S(2)}, u32[]{:S(2)}) collective-permute-start(bf16[32,128]{1,0:T(8,128)(2,1)S(1)} %shard_map.69), channel_id=1, source_target_pairs={{12,18},{13,19},{14,16},{15,17}} | collective-permute-start | bytes 24584 | tf_op jit(solution)/shard_map/ppermute | solution.py:278
  38.6 2.5 %collective-permute-start.20 = (bf16[32,128]{1,0:T(8,128)(2,1)S(1)}, bf16[32,128]{1,0:T(8,128)(2,1)S(1)}, u32[]{:S(2)}, u32[]{:S(2)}) collective-permute-start(bf16[32,128]{1,0:T(8,128)(2,1)S(1)} %shard_map.69), channel_id=1, source_target_pairs={{12,17},{13,16},{14,19},{15,18}} | collective-permute-start | bytes 24584 | tf_op jit(solution)/shard_map/ppermute | solution.py:278
  41.4 4.1 %collective-permute-start.21 = (bf16[32,2048]{1,0:T(8,128)(2,1)S(1)}, bf16[32,2048]{1,0:T(8,128)(2,1)S(1)}, u32[]{:S(2)}, u32[]{:S(2)}) collective-permute-start(bf16[32,2048]{1,0:T(8,128)(2,1)S(1)} %get-tuple-element.120.refs_0_), channel_id=1, source_target_pairs={{16,20},{17,21},{18,22},{19,23}} | collective-permute-start | bytes 393224 | tf_op jit(solution)/shard_map/ppermute | solution.py:278
  42.4 4.1 %collective-permute-start.22 = (bf16[32,2048]{1,0:T(8,128)(2,1)S(1)}, bf16[32,2048]{1,0:T(8,128)(2,1)S(1)}, u32[]{:S(2)}, u32[]{:S(2)}) collective-permute-start(bf16[32,2048]{1,0:T(8,128)(2,1)S(1)} %get-tuple-element.127.refs_1_), channel_id=1, source_target_pairs={{16,20},{17,21},{18,22},{19,23}} | collective-permute-start | bytes 393224 | tf_op jit(solution)/shard_map/ppermute | solution.py:278
  43.3 4.0 %collective-permute-start.23 = (bf16[32,128]{1,0:T(8,128)(2,1)S(1)}, bf16[32,128]{1,0:T(8,128)(2,1)S(1)}, u32[]{:S(2)}, u32[]{:S(2)}) collective-permute-start(bf16[32,128]{1,0:T(8,128)(2,1)S(1)} %shard_map.74), channel_id=1, source_target_pairs={{16,23},{17,22},{18,21},{19,20}} | collective-permute-start | bytes 24584 | tf_op jit(solution)/shard_map/ppermute | solution.py:278
  44.0 3.4 %collective-permute-start.24 = (bf16[32,128]{1,0:T(8,128)(2,1)S(1)}, bf16[32,128]{1,0:T(8,128)(2,1)S(1)}, u32[]{:S(2)}, u32[]{:S(2)}) collective-permute-start(bf16[32,128]{1,0:T(8,128)(2,1)S(1)} %shard_map.74), channel_id=1, source_target_pairs={{16,22},{17,23},{18,20},{19,21}} | collective-permute-start | bytes 24584 | tf_op jit(solution)/shard_map/ppermute | solution.py:278
  44.7 2.7 %collective-permute-start.25 = (bf16[32,128]{1,0:T(8,128)(2,1)S(1)}, bf16[32,128]{1,0:T(8,128)(2,1)S(1)}, u32[]{:S(2)}, u32[]{:S(2)}) collective-permute-start(bf16[32,128]{1,0:T(8,128)(2,1)S(1)} %shard_map.74), channel_id=1, source_target_pairs={{16,21},{17,20},{18,23},{19,22}} | collective-permute-start | bytes 24584 | tf_op jit(solution)/shard_map/ppermute | solution.py:278
  47.7 3.9 %collective-permute-start.26 = (bf16[32,2048]{1,0:T(8,128)(2,1)S(1)}, bf16[32,2048]{1,0:T(8,128)(2,1)S(1)}, u32[]{:S(2)}, u32[]{:S(2)}) collective-permute-start(bf16[32,2048]{1,0:T(8,128)(2,1)S(1)} %get-tuple-element.130.refs_0_), channel_id=1, source_target_pairs={{20,24},{21,25},{22,26},{23,27}} | collective-permute-start | bytes 393224 | tf_op jit(solution)/shard_map/ppermute | solution.py:278
  48.6 3.9 %collective-permute-start.27 = (bf16[32,2048]{1,0:T(8,128)(2,1)S(1)}, bf16[32,2048]{1,0:T(8,128)(2,1)S(1)}, u32[]{:S(2)}, u32[]{:S(2)}) collective-permute-start(bf16[32,2048]{1,0:T(8,128)(2,1)S(1)} %get-tuple-element.137.refs_1_), channel_id=1, source_target_pairs={{20,24},{21,25},{22,26},{23,27}} | collective-permute-start | bytes 393224 | tf_op jit(solution)/shard_map/ppermute | solution.py:278
  49.6 3.9 %collective-permute-start.28 = (bf16[32,128]{1,0:T(8,128)(2,1)S(1)}, bf16[32,128]{1,0:T(8,128)(2,1)S(1)}, u32[]{:S(2)}, u32[]{:S(2)}) collective-permute-start(bf16[32,128]{1,0:T(8,128)(2,1)S(1)} %shard_map.79), channel_id=1, source_target_pairs={{20,27},{21,26},{22,25},{23,24}} | collective-permute-start | bytes 24584 | tf_op jit(solution)/shard_map/ppermute | solution.py:278
  50.3 3.2 %collective-permute-start.29 = (bf16[32,128]{1,0:T(8,128)(2,1)S(1)}, bf16[32,128]{1,0:T(8,128)(2,1)S(1)}, u32[]{:S(2)}, u32[]{:S(2)}) collective-permute-start(bf16[32,128]{1,0:T(8,128)(2,1)S(1)} %shard_map.79), channel_id=1, source_target_pairs={{20,26},{21,27},{22,24},{23,25}} | collective-permute-start | bytes 24584 | tf_op jit(solution)/shard_map/ppermute | solution.py:278
  50.9 2.5 %collective-permute-start.30 = (bf16[32,128]{1,0:T(8,128)(2,1)S(1)}, bf16[32,128]{1,0:T(8,128)(2,1)S(1)}, u32[]{:S(2)}, u32[]{:S(2)}) collective-permute-start(bf16[32,128]{1,0:T(8,128)(2,1)S(1)} %shard_map.79), channel_id=1, source_target_pairs={{20,25},{21,24},{22,27},{23,26}} | collective-permute-start | bytes 24584 | tf_op jit(solution)/shard_map/ppermute | solution.py:278
  53.8 36.6 %collective-permute-start.31 = (bf16[32,2048]{1,0:T(8,128)(2,1)S(1)}, bf16[32,2048]{1,0:T(8,128)(2,1)S(1)}, u32[]{:S(2)}, u32[]{:S(2)}) collective-permute-start(bf16[32,2048]{1,0:T(8,128)(2,1)S(1)} %get-tuple-element.140.refs_0_), channel_id=1, source_target_pairs={{24,28},{25,29},{26,30},{27,31}} | collective-permute-start | bytes 393224 | tf_op jit(solution)/shard_map/ppermute | solution.py:278
  55.3 37.1 %collective-permute-start.32 = (bf16[32,2048]{1,0:T(8,128)(2,1)S(1)}, bf16[32,2048]{1,0:T(8,128)(2,1)S(1)}, u32[]{:S(2)}, u32[]{:S(2)}) collective-permute-start(bf16[32,2048]{1,0:T(8,128)(2,1)S(1)} %get-tuple-element.145.refs_1_), channel_id=1, source_target_pairs={{24,28},{25,29},{26,30},{27,31}} | collective-permute-start | bytes 393224 | tf_op jit(solution)/shard_map/ppermute | solution.py:278
  56.9 36.4 %collective-permute-start.33 = (bf16[32,128]{1,0:T(8,128)(2,1)S(1)}, bf16[32,128]{1,0:T(8,128)(2,1)S(1)}, u32[]{:S(2)}, u32[]{:S(2)}) collective-permute-start(bf16[32,128]{1,0:T(8,128)(2,1)S(1)} %shard_map.84), channel_id=1, source_target_pairs={{24,31},{25,30},{26,29},{27,28}} | collective-permute-start | bytes 24584 | tf_op jit(solution)/shard_map/ppermute | solution.py:278
  58.2 35.1 %collective-permute-start.34 = (bf16[32,128]{1,0:T(8,128)(2,1)S(1)}, bf16[32,128]{1,0:T(8,128)(2,1)S(1)}, u32[]{:S(2)}, u32[]{:S(2)}) collective-permute-start(bf16[32,128]{1,0:T(8,128)(2,1)S(1)} %shard_map.84), channel_id=1, source_target_pairs={{24,30},{25,31},{26,28},{27,29}} | collective-permute-start | bytes 24584 | tf_op jit(solution)/shard_map/ppermute | solution.py:278
  59.5 33.8 %collective-permute-start.35 = (bf16[32,128]{1,0:T(8,128)(2,1)S(1)}, bf16[32,128]{1,0:T(8,128)(2,1)S(1)}, u32[]{:S(2)}, u32[]{:S(2)}) collective-permute-start(bf16[32,128]{1,0:T(8,128)(2,1)S(1)} %shard_map.84), channel_id=1, source_target_pairs={{24,29},{25,28},{26,31},{27,30}} | collective-permute-start | bytes 24584 | tf_op jit(solution)/shard_map/ppermute | solution.py:278
where the time goes:
time: 95.2 us; the launch traced here: 94.5 us
  waiting for transfers between devices  37.9 us (40%)
  starting transfers between devices  31.8 us (33%)
  Pallas kernels  24 us (25%)
    ppermute x36, waiting for transfers between devices, moved(): return lax.ppermute(x, ('slab', 'hodlr'), route)  37.9 us
    ppermute x36, starting transfers between devices, moved(): return lax.ppermute(x, ('slab', 'hodlr'), route)  31.8 us
    pallas_call x40, Pallas kernels, call(): pl.pallas_call(kernel, out_shape=outs, in_specs=[remote if i in from_hbm...  24 us
  transfers between devices with their start and end apart: 36, of which 4 were waited for; matrix products, arithmetic and copies ran while one was open for 0% of the time, Pallas kernels for 21%

commit v1 on v0

--- a/solution.py
+++ b/solution.py
@@ -303,15 +303,24 @@
     levels_relayed = [cross - x.bit_length() for x in relayed]
     for k in range(1, chain):
         levels_now = levels_of[::-1]
-        if k <= IN_PLACE:
-            if k == IN_PLACE:
-                turned = turn(size, [coarse, early[-rank:]])
-            behind = ahead if k == 1 else [turned]
-            nearby = nearby_part(rank, front[0], fine_v, ranks, parts, levels_relayed, behind, OPEN_FLOPS)
-            parts = [moved(nearby, [(k, k)], offsets[0])] + parts
-            levels_now = [None] + levels_relayed
         for i, span in enumerate(spans):
-            behind = projected[i - 1 : i] if i else []
+            behind = projected[i - 1 : i] if i else ahead if k == 1 else []
+            if i == 1 and k <= IN_PLACE:
+                if k == IN_PLACE:
+                    turned = turn(size, [coarse, early[-rank:]])
+                nearby = nearby_part(
+                    rank,
+                    front[0],
+                    fine_v,
+                    ranks,
+                    parts,
+                    levels_relayed,
+                    behind + (ahead if k == 1 else [turned]),
+                    OPEN_FLOPS,
+                )
+                parts = [moved(nearby, [(k, k)], offsets[0])] + parts
+                levels_now = [None] + levels_relayed
+                behind = [nearby]
             given, start = (front[0], span[0]) if len(front) == 1 else (front[i], 0)
             w[i], sums[i], projected[i] = near_part(span, start, (levels - cross) * rank, w[i], given, leaf, near_v, behind)
         if k == chain - 1:

time: 95.2 us -> 94.3 us (level)
  no operation moved by 1% of the time
where the time goes in v1:
time: 94.3 us; the launch traced here: 93.5 us
  waiting for transfers between devices  37 us (39%)
  starting transfers between devices  31.8 us (34%)
  Pallas kernels  24 us (25%)
    ppermute x36, waiting for transfers between devices, moved(): return lax.ppermute(x, ('slab', 'hodlr'), route)  37 us
    ppermute x36, starting transfers between devices, moved(): return lax.ppermute(x, ('slab', 'hodlr'), route)  31.8 us
    pallas_call x40, Pallas kernels, call(): pl.pallas_call(kernel, out_shape=outs, in_specs=[remote if i in from_hbm...  24 us
  transfers between devices with their start and end apart: 36, of which 4 were waited for; matrix products, arithmetic and copies ran while one was open for 0% of the time, Pallas kernels for 21%

profile of v1, /device:TPU:26, one launch (start us, length us, event | category | flops | bytes accessed | tf_op | source)
XLA Modules:
  0.0 93.5 jit_solution(15496797968707769805)
XLA Ops:
  0.0 1.6 %shard_map.46 = (bf16[1,64,4096]{2,1,0:T(8,128)(2,1)S(1)}, bf16[1,64,4096]{2,1,0:T(8,128)(2,1)S(1)}, bf16[1,64,4096]{2,1,0:T(8,128)(2,1)S(1)}, bf16[32,2048]{1,0:T(8,128)(2,1)S(1)}, bf16[32,2048]{1,0:T(8,128)(2,1)S(1)}) custom-call(bf16[32,4096]{1,0:T(8,128)(2,1)} %bitcast.46, bf16[4,64,4096]{2,1,0:T(8,128)(2,1)} %bitcast.37), custom_call_target="tpu_custom_call" | custom-call | tf_op jit(solution)/shard_map/pallas_call | solution.py:30
  1.6 2.6 %collective-permute-start.4 = (bf16[64,4096]{1,0:T(8,128)(2,1)S(1)}, bf16[64,4096]{1,0:T(8,128)(2,1)S(1)}, u32[]{:S(2)}, u32[]{:S(2)}) collective-permute-start(bf16[64,4096]{1,0:T(8,128)(2,1)S(1)} %bitcast.45), channel_id=1, source_target_pairs={{4,0},{5,1},{6,2},{7,3},{12,8},{13,9},{14,10},{15,11},{16,12},{17,... | collective-permute-start | bytes 1572872 | tf_op jit(solution)/shard_map/ppermute | solution.py:278
  4.3 0.4 shard_map.48
  4.8 1.6 %collective-permute-start.1 = (bf16[32,128]{1,0:T(8,128)(2,1)S(1)}, bf16[32,128]{1,0:T(8,128)(2,1)S(1)}, u32[]{:S(2)}, u32[]{:S(2)}) collective-permute-start(bf16[32,128]{1,0:T(8,128)(2,1)S(1)} %shard_map.48), channel_id=1, source_target_pairs={{0,2},{1,3},{2,0},{3,1},{4,6},{5,7},{6,4},{7,5},{8,10},{9,11},{10,... | collective-permute-start | bytes 24584 | tf_op jit(solution)/shard_map/ppermute | solution.py:278
  6.3 0.3 collective-permute-start.2
  6.6 3.3 %collective-permute-start.10 = (bf16[64,4096]{1,0:T(8,128)(2,1)S(1)}, bf16[64,4096]{1,0:T(8,128)(2,1)S(1)}, u32[]{:S(2)}, u32[]{:S(2)}) collective-permute-start(bf16[64,4096]{1,0:T(8,128)(2,1)S(1)} %bitcast.43), channel_id=1, source_target_pairs={{12,8},{13,9},{14,10},{15,11},{16,12},{17,13},{18,14},{19,15},{20,... | collective-permute-start | bytes 1572872 | tf_op jit(solution)/shard_map/ppermute | solution.py:278
  9.9 1.8 %shard_map.47 = (bf16[2,1024,256]{2,1,0:T(8,128)(2,1)S(1)}, f32[32,2048]{1,0:T(8,128)S(1)}, f32[32,2048]{1,0:T(8,128)S(1)}, f32[2,32,128]{2,1,0:T(8,128)S(1)}, f32[2,32,128]{2,1,0:T(8,128)S(1)}) custom-call(bf16[32,2048]{1,0:T(8,128)(2,1)S(1)} %get-tuple-element.78.refs_0_.refs_2_.w_ref, bf16[32,2048]{1,0:T(8,128)(2,1)S(1)} %get-tuple-element.79.refs_1_.refs_3_.w_ref, ...), custom_call_target="tpu_custom_call" | custom-call | tf_op jit(solution)/shard_map/pallas_call | solution.py:30
  11.8 0.4 shard_map.49
  12.2 0.7 collective-permute-start.3
  12.9 3.6 %collective-permute-done.4.refs_0_.refs_1_ = bf16[64,4096]{1,0:T(8,128)(2,1)S(1)} collective-permute-done((bf16[64,4096]{1,0:T(8,128)(2,1)S(1)}, bf16[64,4096]{1,0:T(8,128)(2,1)S(1)}, u32[]{:S(2)}, u32[]{:S(2)}) %collective-permute-start.4) | collective-permute-done | bytes 524320 | tf_op jit(solution)/shard_map/ppermute | solution.py:278
  16.8 0.7 collective-permute-start.5
  17.5 0.7 collective-permute-start.8
  18.2 0.9 shard_map.51
  19.1 0.3 shard_map.52.refs_0_
  19.5 0.7 collective-permute-start.6
  20.1 0.9 shard_map.53
  21.1 0.4 shard_map.54
  21.5 0.7 collective-permute-start.7
  22.4 0.7 collective-permute-start.9
  23.1 3.5 %collective-permute-done.10.refs_0_ = bf16[64,4096]{1,0:T(8,128)(2,1)S(1)} collective-permute-done((bf16[64,4096]{1,0:T(8,128)(2,1)S(1)}, bf16[64,4096]{1,0:T(8,128)(2,1)S(1)}, u32[]{:S(2)}, u32[]{:S(2)}) %collective-permute-start.10) | collective-permute-done | bytes 524320 | tf_op jit(solution)/shard_map/ppermute | solution.py:278
  26.6 0.3 shard_map.58.refs_2_.v_ref
  26.9 0.9 shard_map.55
  27.9 0.3 shard_map.59.refs_0_
  28.2 0.7 collective-permute-start.11
  28.9 0.9 shard_map.60
  30.1 0.7 collective-permute-start.12
  31.0 0.7 collective-permute-start.13
  32.0 0.7 collective-permute-start.14
  32.6 0.7 collective-permute-start.15
  33.3 0.7 collective-permute-start.16
  34.0 0.9 shard_map.62
  34.9 0.9 shard_map.64
  35.9 0.4 shard_map.66
  36.3 0.7 collective-permute-start.17
  37.0 0.3 shard_map.69
  37.3 0.7 collective-permute-start.18
  37.9 0.7 collective-permute-start.19
  38.6 0.7 collective-permute-start.20
  39.3 0.9 shard_map.67
  40.2 0.9 shard_map.68
  41.4 0.7 collective-permute-start.21
  42.4 0.7 collective-permute-start.22
  43.3 0.7 collective-permute-start.23
  44.0 0.7 collective-permute-start.24
  44.7 0.8 collective-permute-start.25
  45.5 0.9 shard_map.71
  46.4 0.9 shard_map.73
  47.7 0.7 collective-permute-start.26
  48.6 0.7 collective-permute-start.27
  49.6 0.7 collective-permute-start.28
  50.2 0.7 collective-permute-start.29
  50.9 0.7 collective-permute-start.30
  51.6 0.9 shard_map.76
  52.5 0.9 shard_map.78
  53.8 1.3 %collective-permute-start.31 = (bf16[32,2048]{1,0:T(8,128)(2,1)S(1)}, bf16[32,2048]{1,0:T(8,128)(2,1)S(1)}, u32[]{:S(2)}, u32[]{:S(2)}) collective-permute-start(bf16[32,2048]{1,0:T(8,128)(2,1)S(1)} %get-tuple-element.140.refs_0_), channel_id=1, source_target_pairs={{24,28},{25,29},{26,30},{27,31}} | collective-permute-start | bytes 393224 | tf_op jit(solution)/shard_map/ppermute | solution.py:278
  55.3 1.3 %collective-permute-start.32 = (bf16[32,2048]{1,0:T(8,128)(2,1)S(1)}, bf16[32,2048]{1,0:T(8,128)(2,1)S(1)}, u32[]{:S(2)}, u32[]{:S(2)}) collective-permute-start(bf16[32,2048]{1,0:T(8,128)(2,1)S(1)} %get-tuple-element.145.refs_1_), channel_id=1, source_target_pairs={{24,28},{25,29},{26,30},{27,31}} | collective-permute-start | bytes 393224 | tf_op jit(solution)/shard_map/ppermute | solution.py:278
  56.9 1.3 %collective-permute-start.33 = (bf16[32,128]{1,0:T(8,128)(2,1)S(1)}, bf16[32,128]{1,0:T(8,128)(2,1)S(1)}, u32[]{:S(2)}, u32[]{:S(2)}) collective-permute-start(bf16[32,128]{1,0:T(8,128)(2,1)S(1)} %shard_map.84), channel_id=1, source_target_pairs={{24,31},{25,30},{26,29},{27,28}} | collective-permute-start | bytes 24584 | tf_op jit(solution)/shard_map/ppermute | solution.py:278
  58.2 1.3 %collective-permute-start.34 = (bf16[32,128]{1,0:T(8,128)(2,1)S(1)}, bf16[32,128]{1,0:T(8,128)(2,1)S(1)}, u32[]{:S(2)}, u32[]{:S(2)}) collective-permute-start(bf16[32,128]{1,0:T(8,128)(2,1)S(1)} %shard_map.84), channel_id=1, source_target_pairs={{24,30},{25,31},{26,28},{27,29}} | collective-permute-start | bytes 24584 | tf_op jit(solution)/shard_map/ppermute | solution.py:278
  59.5 1.3 %collective-permute-start.35 = (bf16[32,128]{1,0:T(8,128)(2,1)S(1)}, bf16[32,128]{1,0:T(8,128)(2,1)S(1)}, u32[]{:S(2)}, u32[]{:S(2)}) collective-permute-start(bf16[32,128]{1,0:T(8,128)(2,1)S(1)} %shard_map.84), channel_id=1, source_target_pairs={{24,29},{25,28},{26,31},{27,30}} | collective-permute-start | bytes 24584 | tf_op jit(solution)/shard_map/ppermute | solution.py:278
  60.8 28.6 %collective-permute-done.31.front_ref = bf16[32,2048]{1,0:T(8,128)(2,1)S(1)} collective-permute-done((bf16[32,2048]{1,0:T(8,128)(2,1)S(1)}, bf16[32,2048]{1,0:T(8,128)(2,1)S(1)}, u32[]{:S(2)}, u32[]{:S(2)}) %collective-permute-start.31) | collective-permute-done | bytes 131104 | tf_op jit(solution)/shard_map/ppermute | solution.py:278
  89.4 0.9 shard_map.81
  90.3 1.1 %collective-permute-done.32.front_ref = bf16[32,2048]{1,0:T(8,128)(2,1)S(1)} collective-permute-done((bf16[32,2048]{1,0:T(8,128)(2,1)S(1)}, bf16[32,2048]{1,0:T(8,128)(2,1)S(1)}, u32[]{:S(2)}, u32[]{:S(2)}) %collective-permute-start.32) | collective-permute-done | bytes 131104 | tf_op jit(solution)/shard_map/ppermute | solution.py:278
  91.4 0.9 shard_map.83
  92.4 1.1 %shard_map.85 = (bf16[32,4096]{1,0:T(8,128)(2,1)}, f32[32,128]{1,0:T(8,128)S(1)}) custom-call(f32[32,2048]{1,0:T(8,128)S(1)} %get-tuple-element.141.refs_0_, f32[32,2048]{1,0:T(8,128)S(1)} %get-tuple-element.147.refs_1_, f32[2,32,128]{2,1,0:T(8,128)S(1)} %get-tuple-element.146.refs_0_.refs_2_, ...), custom_call_target="tpu_custom_call", output_to_operand_aliasing={{1}: (4, {})} | custom-call | tf_op jit(solution)/shard_map/pallas_call | solution.py:30
  (58 shorter events, 4.0 us)
Async XLA Ops:
  0.0 9.9 %slice-start = ((s8[8388608]{0:T(1024)(128)(4,1)}), s8[4194304]{0:T(1024)(128)(4,1)S(1)}, s32[]{:S(2)}) async-start(s8[8388608]{0:T(1024)(128)(4,1)} %bitcast.8), calls=%async_computation | async-start | bytes 8388608
  1.6 14.9 %collective-permute-start.4 = (bf16[64,4096]{1,0:T(8,128)(2,1)S(1)}, bf16[64,4096]{1,0:T(8,128)(2,1)S(1)}, u32[]{:S(2)}, u32[]{:S(2)}) collective-permute-start(bf16[64,4096]{1,0:T(8,128)(2,1)S(1)} %bitcast.45), channel_id=1, source_target_pairs={{4,0},{5,1},{6,2},{7,3},{12,8},{13,9},{14,10},{15,11},{16,12},{17,... | collective-permute-start | bytes 1572872 | tf_op jit(solution)/shard_map/ppermute | solution.py:278
  4.2 5.7 %slice-start.1 = ((s8[8388608]{0:T(1024)(128)(4,1)}), s8[4194304]{0:T(1024)(128)(4,1)S(1)}, s32[]{:S(2)}) async-start(s8[8388608]{0:T(1024)(128)(4,1)} %bitcast.8), calls=%async_computation.1 | async-start | bytes 8388608
  4.2 5.7 %copy-start.1 = (bf16[1,4,64,4096]{3,2,1,0:T(8,128)(2,1)S(1)}, bf16[1,4,64,4096]{3,2,1,0:T(8,128)(2,1)}, u32[]{:S(2)}) copy-start(bf16[1,4,64,4096]{3,2,1,0:T(8,128)(2,1)} %param.6) | copy-start | bytes 6291460
  4.7 7.1 %collective-permute-start = (bf16[32,128]{1,0:T(8,128)(2,1)S(1)}, bf16[32,128]{1,0:T(8,128)(2,1)S(1)}, u32[]{:S(2)}, u32[]{:S(2)}) collective-permute-start(bf16[32,128]{1,0:T(8,128)(2,1)S(1)} %shard_map.48), channel_id=1, source_target_pairs={{0,1},{1,0},{2,3},{3,2},{4,5},{5,4},{6,7},{7,6},{8,9},{9,8},{10,11... | collective-permute-start | bytes 24584 | tf_op jit(solution)/shard_map/ppermute | solution.py:278
  4.8 7.0 %collective-permute-start.1 = (bf16[32,128]{1,0:T(8,128)(2,1)S(1)}, bf16[32,128]{1,0:T(8,128)(2,1)S(1)}, u32[]{:S(2)}, u32[]{:S(2)}) collective-permute-start(bf16[32,128]{1,0:T(8,128)(2,1)S(1)} %shard_map.48), channel_id=1, source_target_pairs={{0,2},{1,3},{2,0},{3,1},{4,6},{5,7},{6,4},{7,5},{8,10},{9,11},{10,... | collective-permute-start | bytes 24584 | tf_op jit(solution)/shard_map/ppermute | solution.py:278
  6.3 5.4 %collective-permute-start.2 = (bf16[32,128]{1,0:T(8,128)(2,1)S(1)}, bf16[32,128]{1,0:T(8,128)(2,1)S(1)}, u32[]{:S(2)}, u32[]{:S(2)}) collective-permute-start(bf16[32,128]{1,0:T(8,128)(2,1)S(1)} %shard_map.48), channel_id=1, source_target_pairs={{0,3},{1,2},{2,1},{3,0},{4,7},{5,6},{6,5},{7,4},{8,11},{9,10},{10,... | collective-permute-start | bytes 24584 | tf_op jit(solution)/shard_map/ppermute | solution.py:278
  6.6 20.0 %collective-permute-start.10 = (bf16[64,4096]{1,0:T(8,128)(2,1)S(1)}, bf16[64,4096]{1,0:T(8,128)(2,1)S(1)}, u32[]{:S(2)}, u32[]{:S(2)}) collective-permute-start(bf16[64,4096]{1,0:T(8,128)(2,1)S(1)} %bitcast.43), channel_id=1, source_target_pairs={{12,8},{13,9},{14,10},{15,11},{16,12},{17,13},{18,14},{19,15},{20,... | collective-permute-start | bytes 1572872 | tf_op jit(solution)/shard_map/ppermute | solution.py:278
  9.9 1.9 %copy-start = (bf16[1,4,64,4096]{3,2,1,0:T(8,128)(2,1)S(1)}, bf16[1,4,64,4096]{3,2,1,0:T(8,128)(2,1)}, u32[]{:S(2)}) copy-start(bf16[1,4,64,4096]{3,2,1,0:T(8,128)(2,1)} %param.7) | copy-start | bytes 6291460
  12.2 6.0 %collective-permute-start.3 = (bf16[32,4096]{1,0:T(8,128)(2,1)S(1)}, bf16[32,4096]{1,0:T(8,128)(2,1)S(1)}, u32[]{:S(2)}, u32[]{:S(2)}) collective-permute-start(bf16[32,4096]{1,0:T(8,128)(2,1)S(1)} %get-tuple-element.86.refs_1_), channel_id=1, source_target_pairs={{0,4},{1,5},{2,6},{3,7}} | collective-permute-start | bytes 786440 | tf_op jit(solution)/shard_map/ppermute | solution.py:278
  16.8 2.4 %collective-permute-start.5 = (bf16[32,128]{1,0:T(8,128)(2,1)S(1)}, bf16[32,128]{1,0:T(8,128)(2,1)S(1)}, u32[]{:S(2)}, u32[]{:S(2)}) collective-permute-start(bf16[32,128]{1,0:T(8,128)(2,1)S(1)} %shard_map.50.refs_0_.refs_2_.other_ref), channel_id=1, source_target_pairs={{0,6},{1,7},{2,4},{3,5}} | collective-permute-start | bytes 24584 | tf_op jit(solution)/shard_map/ppermute | solution.py:278
  17.5 4.7 %collective-permute-start.8 = (bf16[64,4096]{1,0:T(8,128)(2,1)S(1)}, bf16[64,4096]{1,0:T(8,128)(2,1)S(1)}, u32[]{:S(2)}, u32[]{:S(2)}) collective-permute-start(bf16[64,4096]{1,0:T(8,128)(2,1)S(1)} %shard_map.56), channel_id=1, source_target_pairs={{8,4},{9,5},{10,6},{11,7}} | collective-permute-start | bytes 1572872 | tf_op jit(solution)/shard_map/ppermute | solution.py:278
  19.5 1.6 %collective-permute-start.6 = (bf16[32,128]{1,0:T(8,128)(2,1)S(1)}, bf16[32,128]{1,0:T(8,128)(2,1)S(1)}, u32[]{:S(2)}, u32[]{:S(2)}) collective-permute-start(bf16[32,128]{1,0:T(8,128)(2,1)S(1)} %shard_map.52.refs_0_), channel_id=1, source_target_pairs={{4,5},{5,4},{6,7},{7,6}} | collective-permute-start | bytes 24584 | tf_op jit(solution)/shard_map/ppermute | solution.py:278
  21.5 5.5 %collective-permute-start.7 = (bf16[32,4096]{1,0:T(8,128)(2,1)S(1)}, bf16[32,4096]{1,0:T(8,128)(2,1)S(1)}, u32[]{:S(2)}, u32[]{:S(2)}) collective-permute-start(bf16[32,4096]{1,0:T(8,128)(2,1)S(1)} %get-tuple-element.95.refs_1_), channel_id=1, source_target_pairs={{4,8},{5,9},{6,10},{7,11}} | collective-permute-start | bytes 786440 | tf_op jit(solution)/shard_map/ppermute | solution.py:278
  22.4 5.4 %collective-permute-start.9 = (bf16[32,128]{1,0:T(8,128)(2,1)S(1)}, bf16[32,128]{1,0:T(8,128)(2,1)S(1)}, u32[]{:S(2)}, u32[]{:S(2)}) collective-permute-start(bf16[32,128]{1,0:T(8,128)(2,1)S(1)} %shard_map.57), channel_id=1, source_target_pairs={{4,10},{5,11},{6,8},{7,9}} | collective-permute-start | bytes 24584 | tf_op jit(solution)/shard_map/ppermute | solution.py:278
  28.2 1.6 %collective-permute-start.11 = (bf16[32,128]{1,0:T(8,128)(2,1)S(1)}, bf16[32,128]{1,0:T(8,128)(2,1)S(1)}, u32[]{:S(2)}, u32[]{:S(2)}) collective-permute-start(bf16[32,128]{1,0:T(8,128)(2,1)S(1)} %shard_map.59.refs_0_), channel_id=1, source_target_pairs={{8,9},{9,8},{10,11},{11,10}} | collective-permute-start | bytes 24584 | tf_op jit(solution)/shard_map/ppermute | solution.py:278
  30.1 3.9 %collective-permute-start.12 = (bf16[32,2048]{1,0:T(8,128)(2,1)S(1)}, bf16[32,2048]{1,0:T(8,128)(2,1)S(1)}, u32[]{:S(2)}, u32[]{:S(2)}) collective-permute-start(bf16[32,2048]{1,0:T(8,128)(2,1)S(1)} %get-tuple-element.102.refs_0_), channel_id=1, source_target_pairs={{8,12},{9,13},{10,14},{11,15}} | collective-permute-start | bytes 393224 | tf_op jit(solution)/shard_map/ppermute | solution.py:278
  31.0 3.9 %collective-permute-start.13 = (bf16[32,2048]{1,0:T(8,128)(2,1)S(1)}, bf16[32,2048]{1,0:T(8,128)(2,1)S(1)}, u32[]{:S(2)}, u32[]{:S(2)}) collective-permute-start(bf16[32,2048]{1,0:T(8,128)(2,1)S(1)} %get-tuple-element.108.refs_1_), channel_id=1, source_target_pairs={{8,12},{9,13},{10,14},{11,15}} | collective-permute-start | bytes 393224 | tf_op jit(solution)/shard_map/ppermute | solution.py:278
  32.0 3.9 %collective-permute-start.14 = (bf16[32,128]{1,0:T(8,128)(2,1)S(1)}, bf16[32,128]{1,0:T(8,128)(2,1)S(1)}, u32[]{:S(2)}, u32[]{:S(2)}) collective-permute-start(bf16[32,128]{1,0:T(8,128)(2,1)S(1)} %shard_map.65), channel_id=1, source_target_pairs={{8,15},{9,14},{10,13},{11,12}} | collective-permute-start | bytes 24584 | tf_op jit(solution)/shard_map/ppermute | solution.py:278
  32.6 3.2 %collective-permute-start.15 = (bf16[32,128]{1,0:T(8,128)(2,1)S(1)}, bf16[32,128]{1,0:T(8,128)(2,1)S(1)}, u32[]{:S(2)}, u32[]{:S(2)}) collective-permute-start(bf16[32,128]{1,0:T(8,128)(2,1)S(1)} %shard_map.65), channel_id=1, source_target_pairs={{8,14},{9,15},{10,12},{11,13}} | collective-permute-start | bytes 24584 | tf_op jit(solution)/shard_map/ppermute | solution.py:278
  33.3 2.5 %collective-permute-start.16 = (bf16[32,128]{1,0:T(8,128)(2,1)S(1)}, bf16[32,128]{1,0:T(8,128)(2,1)S(1)}, u32[]{:S(2)}, u32[]{:S(2)}) collective-permute-start(bf16[32,128]{1,0:T(8,128)(2,1)S(1)} %shard_map.65), channel_id=1, source_target_pairs={{8,13},{9,12},{10,15},{11,14}} | collective-permute-start | bytes 24584 | tf_op jit(solution)/shard_map/ppermute | solution.py:278
  36.3 3.0 %collective-permute-start.17 = (bf16[32,4096]{1,0:T(8,128)(2,1)S(1)}, bf16[32,4096]{1,0:T(8,128)(2,1)S(1)}, u32[]{:S(2)}, u32[]{:S(2)}) collective-permute-start(bf16[32,4096]{1,0:T(8,128)(2,1)S(1)} %get-tuple-element.113.refs_0_), channel_id=1, source_target_pairs={{12,16},{13,17},{14,18},{15,19}} | collective-permute-start | bytes 786440 | tf_op jit(solution)/shard_map/ppermute | solution.py:278
  37.3 3.9 %collective-permute-start.18 = (bf16[32,128]{1,0:T(8,128)(2,1)S(1)}, bf16[32,128]{1,0:T(8,128)(2,1)S(1)}, u32[]{:S(2)}, u32[]{:S(2)}) collective-permute-start(bf16[32,128]{1,0:T(8,128)(2,1)S(1)} %shard_map.69), channel_id=1, source_target_pairs={{12,19},{13,18},{14,17},{15,16}} | collective-permute-start | bytes 24584 | tf_op jit(solution)/shard_map/ppermute | solution.py:278
  37.9 3.2 %collective-permute-start.19 = (bf16[32,128]{1,0:T(8,128)(2,1)S(1)}, bf16[32,128]{1,0:T(8,128)(2,1)S(1)}, u32[]{:S(2)}, u32[]{:S(2)}) collective-permute-start(bf16[32,128]{1,0:T(8,128)(2,1)S(1)} %shard_map.69), channel_id=1, source_target_pairs={{12,18},{13,19},{14,16},{15,17}} | collective-permute-start | bytes 24584 | tf_op jit(solution)/shard_map/ppermute | solution.py:278
  38.6 2.5 %collective-permute-start.20 = (bf16[32,128]{1,0:T(8,128)(2,1)S(1)}, bf16[32,128]{1,0:T(8,128)(2,1)S(1)}, u32[]{:S(2)}, u32[]{:S(2)}) collective-permute-start(bf16[32,128]{1,0:T(8,128)(2,1)S(1)} %shard_map.69), channel_id=1, source_target_pairs={{12,17},{13,16},{14,19},{15,18}} | collective-permute-start | bytes 24584 | tf_op jit(solution)/shard_map/ppermute | solution.py:278
  41.4 4.1 %collective-permute-start.21 = (bf16[32,2048]{1,0:T(8,128)(2,1)S(1)}, bf16[32,2048]{1,0:T(8,128)(2,1)S(1)}, u32[]{:S(2)}, u32[]{:S(2)}) collective-permute-start(bf16[32,2048]{1,0:T(8,128)(2,1)S(1)} %get-tuple-element.120.refs_0_), channel_id=1, source_target_pairs={{16,20},{17,21},{18,22},{19,23}} | collective-permute-start | bytes 393224 | tf_op jit(solution)/shard_map/ppermute | solution.py:278
  42.4 4.1 %collective-permute-start.22 = (bf16[32,2048]{1,0:T(8,128)(2,1)S(1)}, bf16[32,2048]{1,0:T(8,128)(2,1)S(1)}, u32[]{:S(2)}, u32[]{:S(2)}) collective-permute-start(bf16[32,2048]{1,0:T(8,128)(2,1)S(1)} %get-tuple-element.127.refs_1_), channel_id=1, source_target_pairs={{16,20},{17,21},{18,22},{19,23}} | collective-permute-start | bytes 393224 | tf_op jit(solution)/shard_map/ppermute | solution.py:278
  43.3 4.0 %collective-permute-start.23 = (bf16[32,128]{1,0:T(8,128)(2,1)S(1)}, bf16[32,128]{1,0:T(8,128)(2,1)S(1)}, u32[]{:S(2)}, u32[]{:S(2)}) collective-permute-start(bf16[32,128]{1,0:T(8,128)(2,1)S(1)} %shard_map.74), channel_id=1, source_target_pairs={{16,23},{17,22},{18,21},{19,20}} | collective-permute-start | bytes 24584 | tf_op jit(solution)/shard_map/ppermute | solution.py:278
  44.0 3.4 %collective-permute-start.24 = (bf16[32,128]{1,0:T(8,128)(2,1)S(1)}, bf16[32,128]{1,0:T(8,128)(2,1)S(1)}, u32[]{:S(2)}, u32[]{:S(2)}) collective-permute-start(bf16[32,128]{1,0:T(8,128)(2,1)S(1)} %shard_map.74), channel_id=1, source_target_pairs={{16,22},{17,23},{18,20},{19,21}} | collective-permute-start | bytes 24584 | tf_op jit(solution)/shard_map/ppermute | solution.py:278
  44.7 2.7 %collective-permute-start.25 = (bf16[32,128]{1,0:T(8,128)(2,1)S(1)}, bf16[32,128]{1,0:T(8,128)(2,1)S(1)}, u32[]{:S(2)}, u32[]{:S(2)}) collective-permute-start(bf16[32,128]{1,0:T(8,128)(2,1)S(1)} %shard_map.74), channel_id=1, source_target_pairs={{16,21},{17,20},{18,23},{19,22}} | collective-permute-start | bytes 24584 | tf_op jit(solution)/shard_map/ppermute | solution.py:278
  47.7 3.9 %collective-permute-start.26 = (bf16[32,2048]{1,0:T(8,128)(2,1)S(1)}, bf16[32,2048]{1,0:T(8,128)(2,1)S(1)}, u32[]{:S(2)}, u32[]{:S(2)}) collective-permute-start(bf16[32,2048]{1,0:T(8,128)(2,1)S(1)} %get-tuple-element.130.refs_0_), channel_id=1, source_target_pairs={{20,24},{21,25},{22,26},{23,27}} | collective-permute-start | bytes 393224 | tf_op jit(solution)/shard_map/ppermute | solution.py:278
  48.6 3.9 %collective-permute-start.27 = (bf16[32,2048]{1,0:T(8,128)(2,1)S(1)}, bf16[32,2048]{1,0:T(8,128)(2,1)S(1)}, u32[]{:S(2)}, u32[]{:S(2)}) collective-permute-start(bf16[32,2048]{1,0:T(8,128)(2,1)S(1)} %get-tuple-element.137.refs_1_), channel_id=1, source_target_pairs={{20,24},{21,25},{22,26},{23,27}} | collective-permute-start | bytes 393224 | tf_op jit(solution)/shard_map/ppermute | solution.py:278
  49.6 3.9 %collective-permute-start.28 = (bf16[32,128]{1,0:T(8,128)(2,1)S(1)}, bf16[32,128]{1,0:T(8,128)(2,1)S(1)}, u32[]{:S(2)}, u32[]{:S(2)}) collective-permute-start(bf16[32,128]{1,0:T(8,128)(2,1)S(1)} %shard_map.79), channel_id=1, source_target_pairs={{20,27},{21,26},{22,25},{23,24}} | collective-permute-start | bytes 24584 | tf_op jit(solution)/shard_map/ppermute | solution.py:278
  50.2 3.2 %collective-permute-start.29 = (bf16[32,128]{1,0:T(8,128)(2,1)S(1)}, bf16[32,128]{1,0:T(8,128)(2,1)S(1)}, u32[]{:S(2)}, u32[]{:S(2)}) collective-permute-start(bf16[32,128]{1,0:T(8,128)(2,1)S(1)} %shard_map.79), channel_id=1, source_target_pairs={{20,26},{21,27},{22,24},{23,25}} | collective-permute-start | bytes 24584 | tf_op jit(solution)/shard_map/ppermute | solution.py:278
  50.9 2.5 %collective-permute-start.30 = (bf16[32,128]{1,0:T(8,128)(2,1)S(1)}, bf16[32,128]{1,0:T(8,128)(2,1)S(1)}, u32[]{:S(2)}, u32[]{:S(2)}) collective-permute-start(bf16[32,128]{1,0:T(8,128)(2,1)S(1)} %shard_map.79), channel_id=1, source_target_pairs={{20,25},{21,24},{22,27},{23,26}} | collective-permute-start | bytes 24584 | tf_op jit(solution)/shard_map/ppermute | solution.py:278
  53.8 35.7 %collective-permute-start.31 = (bf16[32,2048]{1,0:T(8,128)(2,1)S(1)}, bf16[32,2048]{1,0:T(8,128)(2,1)S(1)}, u32[]{:S(2)}, u32[]{:S(2)}) collective-permute-start(bf16[32,2048]{1,0:T(8,128)(2,1)S(1)} %get-tuple-element.140.refs_0_), channel_id=1, source_target_pairs={{24,28},{25,29},{26,30},{27,31}} | collective-permute-start | bytes 393224 | tf_op jit(solution)/shard_map/ppermute | solution.py:278
  55.3 36.1 %collective-permute-start.32 = (bf16[32,2048]{1,0:T(8,128)(2,1)S(1)}, bf16[32,2048]{1,0:T(8,128)(2,1)S(1)}, u32[]{:S(2)}, u32[]{:S(2)}) collective-permute-start(bf16[32,2048]{1,0:T(8,128)(2,1)S(1)} %get-tuple-element.145.refs_1_), channel_id=1, source_target_pairs={{24,28},{25,29},{26,30},{27,31}} | collective-permute-start | bytes 393224 | tf_op jit(solution)/shard_map/ppermute | solution.py:278
  56.9 35.5 %collective-permute-start.33 = (bf16[32,128]{1,0:T(8,128)(2,1)S(1)}, bf16[32,128]{1,0:T(8,128)(2,1)S(1)}, u32[]{:S(2)}, u32[]{:S(2)}) collective-permute-start(bf16[32,128]{1,0:T(8,128)(2,1)S(1)} %shard_map.84), channel_id=1, source_target_pairs={{24,31},{25,30},{26,29},{27,28}} | collective-permute-start | bytes 24584 | tf_op jit(solution)/shard_map/ppermute | solution.py:278
  58.2 34.2 %collective-permute-start.34 = (bf16[32,128]{1,0:T(8,128)(2,1)S(1)}, bf16[32,128]{1,0:T(8,128)(2,1)S(1)}, u32[]{:S(2)}, u32[]{:S(2)}) collective-permute-start(bf16[32,128]{1,0:T(8,128)(2,1)S(1)} %shard_map.84), channel_id=1, source_target_pairs={{24,30},{25,31},{26,28},{27,29}} | collective-permute-start | bytes 24584 | tf_op jit(solution)/shard_map/ppermute | solution.py:278
  59.5 32.9 %collective-permute-start.35 = (bf16[32,128]{1,0:T(8,128)(2,1)S(1)}, bf16[32,128]{1,0:T(8,128)(2,1)S(1)}, u32[]{:S(2)}, u32[]{:S(2)}) collective-permute-start(bf16[32,128]{1,0:T(8,128)(2,1)S(1)} %shard_map.84), channel_id=1, source_target_pairs={{24,29},{25,28},{26,31},{27,30}} | collective-permute-start | bytes 24584 | tf_op jit(solution)/shard_map/ppermute | solution.py:278

commit v2 on v1

--- a/solution.py
+++ b/solution.py
@@ -79,12 +79,21 @@
     return [f.reshape(-1, width) for f in found[: len(shares)]], list(found[len(shares) :])
 
 
-def behind_kernel(x_ref, other_ref, out_ref):
-    out_ref[...] = x_ref[...]
-
-
-def put_behind(x, other):
-    return call(behind_kernel, [pltpu.VMEM(x.shape, x.dtype)], [x, other], flops=OPEN_FLOPS)[0]
+def turn_near_kernel(cross, near, x_ref, v_ref, other_ref, x_out, near_out):
+    size = near_out.shape[1]
+    group = near_out.shape[2] // near
+    for c in range(near_out.shape[0] * group):
+        turned = v_ref[cross:, :, c * size : (c + 1) * size].reshape(near, size).T
+        near_out[c // group, :, c % group * near : (c % group + 1) * near] = turned
+    x_out[...] = x_ref[...]
+
+
+def turn_near(spans, cross, size, x, v, other):
+    levels, rank, width = v.shape
+    near = (levels - cross) * rank
+    group = 2 if all((stop - start) // size % 2 == 0 for start, stop in spans) else 1
+    outs = [pltpu.VMEM(x.shape, x.dtype), pltpu.VMEM((width // size // group, size, group * near), v.dtype)]
+    return call(functools.partial(turn_near_kernel, cross, near), outs, [x, v, other], flops=OPEN_FLOPS)
 
 
 def project_kernel(spans, factors, *refs):
@@ -133,17 +142,15 @@
 
 def first_kernel(spans, cross, *refs):
     n = len(spans)
-    w_refs, (leaf_ref, v_ref), near_out = refs[:n], refs[n : n + 2], refs[n + 2]
-    sum_refs, p_refs = refs[n + 3 : 2 * n + 3], refs[2 * n + 3 :]
+    w_refs, (leaf_ref, v_ref) = refs[:n], refs[n : n + 2]
+    sum_refs, p_refs = refs[n + 2 : 2 * n + 2], refs[2 * n + 2 :]
     size = leaf_ref.shape[1]
     near = p_refs[0].shape[2]
     for i, span in enumerate(spans):
         for j, c in enumerate(leaves_of(span, size)):
             columns = slice(j * size, (j + 1) * size)
-            turned = v_ref[cross:, :, c * size : (c + 1) * size].reshape(near, size).T
-            group = near_out.shape[2] // near
-            near_out[c // group, :, c % group * near : (c % group + 1) * near] = turned
-            p_refs[i][j] = dot(w_refs[i][:, columns], turned)
+            rows = v_ref[cross:, :, c * size : (c + 1) * size].reshape(near, size)
+            p_refs[i][j] = dot(w_refs[i][:, columns], rows, ROWS_TIMES_ROWS)
             sum_refs[i][:, columns] = dot(w_refs[i][:, columns], leaf_ref[c])
 
 
@@ -152,13 +159,11 @@
     size = leaf.shape[1]
     rows = w[0].shape[0]
     near = (levels - cross) * rank
-    group = 2 if all((stop - start) // size % 2 == 0 for start, stop in spans) else 1
-    outs = [pltpu.VMEM((width // size // group, size, group * near), v.dtype)]
-    outs += [pltpu.VMEM(x.shape, jnp.float32) for x in w]
+    outs = [pltpu.VMEM(x.shape, jnp.float32) for x in w]
     outs += [pltpu.VMEM((x.shape[1] // size, rows, near), jnp.float32) for x in w]
     n = len(w)
     found = call(functools.partial(first_kernel, spans, cross), outs, [*w, leaf, v])
-    return found[0], list(found[1 : 1 + n]), list(found[1 + n :])
+    return list(found[:n]), list(found[n:])
 
 
 def nearby_kernel(rank, levels_of, front_ref, v_ref, *refs):
@@ -289,7 +294,7 @@
     p = project(spans, w, [coarse_v, fine_v], ranks, OPEN_FLOPS)
     parts = exchanged(p, [(k, k) for k in range(chain)])
     leaf, u = leaves[0], u_rows[0].reshape(levels * rank, width)
-    near_v, sums, projected = first_part(spans, cross, w, leaf, right)
+    sums, projected = first_part(spans, cross, w, leaf, right)
 
     q = jnp.zeros(p.shape, jnp.float32)
     every = tuple(range(len(spans)))
@@ -299,7 +304,8 @@
     ahead = [project(whole, [out], [early], ranks)]
     relayed = offsets[1::2]
     parts = [moved(ahead[0], [(0, 1)], x) for x in relayed]
-    second = moved(put_behind(coarse_v, ahead[0]), [(2, 1)])
+    late, near_v = turn_near(spans, cross, size, coarse_v, right, ahead[0])
+    second = moved(late, [(2, 1)])
     levels_relayed = [cross - x.bit_length() for x in relayed]
     for k in range(1, chain):
         levels_now = levels_of[::-1]

time: 94.3 us -> 94.9 us (level)
  transfers between devices with their start and end apart: 36 -> 36, of which waited for: 4 -> 5; matrix products, arithmetic and copies ran while one was open for 0% -> 0% of each run, Pallas kernels for 21% -> 21%
where the time goes in v2:
time: 94.9 us; the launch traced here: 94.2 us
  waiting for transfers between devices  37.1 us (39%)
  starting transfers between devices  31.8 us (34%)
  Pallas kernels  24.5 us (26%)
    ppermute x36, waiting for transfers between devices, moved(): return lax.ppermute(x, ('slab', 'hodlr'), route)  37.1 us
    ppermute x36, starting transfers between devices, moved(): return lax.ppermute(x, ('slab', 'hodlr'), route)  31.8 us
    pallas_call x40, Pallas kernels, call(): pl.pallas_call(kernel, out_shape=outs, in_specs=[remote if i in from_hbm...  24.5 us
  transfers between devices with their start and end apart: 36, of which 5 were waited for; matrix products, arithmetic and copies ran while one was open for 0% of the time, Pallas kernels for 21%

profile of v2, /device:TPU:26, one launch (start us, length us, event | category | flops | bytes accessed | tf_op | source)
XLA Modules:
  0.0 94.2 jit_solution(3854084993723322214)
XLA Ops:
  0.0 1.6 %shard_map.46 = (bf16[1,64,4096]{2,1,0:T(8,128)(2,1)S(1)}, bf16[1,64,4096]{2,1,0:T(8,128)(2,1)S(1)}, bf16[1,64,4096]{2,1,0:T(8,128)(2,1)S(1)}, bf16[32,2048]{1,0:T(8,128)(2,1)S(1)}, bf16[32,2048]{1,0:T(8,128)(2,1)S(1)}) custom-call(bf16[32,4096]{1,0:T(8,128)(2,1)} %bitcast.47, bf16[4,64,4096]{2,1,0:T(8,128)(2,1)} %bitcast.37), custom_call_target="tpu_custom_call" | custom-call | tf_op jit(solution)/shard_map/pallas_call | solution.py:30
  1.6 2.6 %collective-permute-start.4 = (bf16[64,4096]{1,0:T(8,128)(2,1)S(1)}, bf16[64,4096]{1,0:T(8,128)(2,1)S(1)}, u32[]{:S(2)}, u32[]{:S(2)}) collective-permute-start(bf16[64,4096]{1,0:T(8,128)(2,1)S(1)} %bitcast.46), channel_id=1, source_target_pairs={{4,0},{5,1},{6,2},{7,3},{12,8},{13,9},{14,10},{15,11},{16,12},{17,... | collective-permute-start | bytes 1572872 | tf_op jit(solution)/shard_map/ppermute | solution.py:283
  4.3 0.4 shard_map.48
  4.8 1.6 %collective-permute-start.1 = (bf16[32,128]{1,0:T(8,128)(2,1)S(1)}, bf16[32,128]{1,0:T(8,128)(2,1)S(1)}, u32[]{:S(2)}, u32[]{:S(2)}) collective-permute-start(bf16[32,128]{1,0:T(8,128)(2,1)S(1)} %shard_map.48), channel_id=1, source_target_pairs={{0,2},{1,3},{2,0},{3,1},{4,6},{5,7},{6,4},{7,5},{8,10},{9,11},{10,... | collective-permute-start | bytes 24584 | tf_op jit(solution)/shard_map/ppermute | solution.py:283
  6.6 3.3 %collective-permute-start.10 = (bf16[64,4096]{1,0:T(8,128)(2,1)S(1)}, bf16[64,4096]{1,0:T(8,128)(2,1)S(1)}, u32[]{:S(2)}, u32[]{:S(2)}) collective-permute-start(bf16[64,4096]{1,0:T(8,128)(2,1)S(1)} %bitcast.44), channel_id=1, source_target_pairs={{12,8},{13,9},{14,10},{15,11},{16,12},{17,13},{18,14},{19,15},{20,... | collective-permute-start | bytes 1572872 | tf_op jit(solution)/shard_map/ppermute | solution.py:283
  9.9 1.9 %shard_map.47 = (f32[32,2048]{1,0:T(8,128)S(1)}, f32[32,2048]{1,0:T(8,128)S(1)}, f32[2,32,128]{2,1,0:T(8,128)S(1)}, f32[2,32,128]{2,1,0:T(8,128)S(1)}) custom-call(bf16[32,2048]{1,0:T(8,128)(2,1)S(1)} %get-tuple-element.79.refs_0_.refs_2_.w_ref, bf16[32,2048]{1,0:T(8,128)(2,1)S(1)} %get-tuple-element.80.refs_1_.refs_3_.w_ref, ...), custom_call_target="tpu_custom_call" | custom-call | tf_op jit(solution)/shard_map/pallas_call | solution.py:30
  11.9 0.4 shard_map.49
  12.3 0.7 collective-permute-start.3
  13.0 3.5 %collective-permute-done.4.refs_0_.refs_1_ = bf16[64,4096]{1,0:T(8,128)(2,1)S(1)} collective-permute-done((bf16[64,4096]{1,0:T(8,128)(2,1)S(1)}, bf16[64,4096]{1,0:T(8,128)(2,1)S(1)}, u32[]{:S(2)}, u32[]{:S(2)}) %collective-permute-start.4) | collective-permute-done | bytes 524320 | tf_op jit(solution)/shard_map/ppermute | solution.py:283
  16.8 0.7 collective-permute-start.5
  17.4 0.3 shard_map.51
  17.8 0.7 collective-permute-start.8
  18.5 0.9 shard_map.52
  19.4 0.3 shard_map.53.refs_0_
  19.8 0.7 collective-permute-start.6
  20.4 0.9 shard_map.54
  21.4 0.4 shard_map.55
  21.8 0.7 collective-permute-start.7
  22.7 0.7 collective-permute-start.9
  23.4 3.2 %collective-permute-done.10.refs_0_ = bf16[64,4096]{1,0:T(8,128)(2,1)S(1)} collective-permute-done((bf16[64,4096]{1,0:T(8,128)(2,1)S(1)}, bf16[64,4096]{1,0:T(8,128)(2,1)S(1)}, u32[]{:S(2)}, u32[]{:S(2)}) %collective-permute-start.10) | collective-permute-done | bytes 524320 | tf_op jit(solution)/shard_map/ppermute | solution.py:283
  26.6 0.3 shard_map.58.refs_2_.v_ref
  26.9 0.9 shard_map.56
  27.9 0.3 shard_map.59.refs_0_
  28.2 0.7 collective-permute-start.11
  28.9 0.9 shard_map.60
  30.1 0.7 collective-permute-start.12
  31.0 0.7 collective-permute-start.13
  32.0 0.7 collective-permute-start.14
  32.6 0.7 collective-permute-start.15
  33.3 0.7 collective-permute-start.16
  34.0 0.9 shard_map.62
  34.9 0.9 shard_map.64
  35.9 0.4 shard_map.66
  36.3 0.7 collective-permute-start.17
  37.3 0.7 collective-permute-start.18
  37.9 0.7 collective-permute-start.19
  38.6 0.7 collective-permute-start.20
  39.3 0.9 shard_map.67
  40.2 0.9 shard_map.68
  41.4 0.7 collective-permute-start.21
  42.4 0.8 collective-permute-start.22
  43.5 0.7 collective-permute-start.23
  44.2 0.7 collective-permute-start.24
  44.9 0.7 collective-permute-start.25
  45.6 0.9 shard_map.71
  46.5 0.9 shard_map.73
  47.7 0.7 collective-permute-start.26
  48.7 0.7 collective-permute-start.27
  49.6 0.7 collective-permute-start.28
  50.3 0.7 collective-permute-start.29
  51.0 0.7 collective-permute-start.30
  51.7 0.9 shard_map.76
  52.6 0.9 shard_map.78
  53.8 1.3 %collective-permute-start.31 = (bf16[32,2048]{1,0:T(8,128)(2,1)S(1)}, bf16[32,2048]{1,0:T(8,128)(2,1)S(1)}, u32[]{:S(2)}, u32[]{:S(2)}) collective-permute-start(bf16[32,2048]{1,0:T(8,128)(2,1)S(1)} %get-tuple-element.142.refs_0_), channel_id=1, source_target_pairs={{24,28},{25,29},{26,30},{27,31}} | collective-permute-start | bytes 393224 | tf_op jit(solution)/shard_map/ppermute | solution.py:283
  55.4 1.3 %collective-permute-start.32 = (bf16[32,2048]{1,0:T(8,128)(2,1)S(1)}, bf16[32,2048]{1,0:T(8,128)(2,1)S(1)}, u32[]{:S(2)}, u32[]{:S(2)}) collective-permute-start(bf16[32,2048]{1,0:T(8,128)(2,1)S(1)} %get-tuple-element.147.refs_1_), channel_id=1, source_target_pairs={{24,28},{25,29},{26,30},{27,31}} | collective-permute-start | bytes 393224 | tf_op jit(solution)/shard_map/ppermute | solution.py:283
  56.7 0.3 shard_map.84
  57.0 1.3 %collective-permute-start.33 = (bf16[32,128]{1,0:T(8,128)(2,1)S(1)}, bf16[32,128]{1,0:T(8,128)(2,1)S(1)}, u32[]{:S(2)}, u32[]{:S(2)}) collective-permute-start(bf16[32,128]{1,0:T(8,128)(2,1)S(1)} %shard_map.84), channel_id=1, source_target_pairs={{24,31},{25,30},{26,29},{27,28}} | collective-permute-start | bytes 24584 | tf_op jit(solution)/shard_map/ppermute | solution.py:283
  58.3 1.3 %collective-permute-start.34 = (bf16[32,128]{1,0:T(8,128)(2,1)S(1)}, bf16[32,128]{1,0:T(8,128)(2,1)S(1)}, u32[]{:S(2)}, u32[]{:S(2)}) collective-permute-start(bf16[32,128]{1,0:T(8,128)(2,1)S(1)} %shard_map.84), channel_id=1, source_target_pairs={{24,30},{25,31},{26,28},{27,29}} | collective-permute-start | bytes 24584 | tf_op jit(solution)/shard_map/ppermute | solution.py:283
  59.6 1.3 %collective-permute-start.35 = (bf16[32,128]{1,0:T(8,128)(2,1)S(1)}, bf16[32,128]{1,0:T(8,128)(2,1)S(1)}, u32[]{:S(2)}, u32[]{:S(2)}) collective-permute-start(bf16[32,128]{1,0:T(8,128)(2,1)S(1)} %shard_map.84), channel_id=1, source_target_pairs={{24,29},{25,28},{26,31},{27,30}} | collective-permute-start | bytes 24584 | tf_op jit(solution)/shard_map/ppermute | solution.py:283
  60.9 29.0 %collective-permute-done.31.front_ref = bf16[32,2048]{1,0:T(8,128)(2,1)S(1)} collective-permute-done((bf16[32,2048]{1,0:T(8,128)(2,1)S(1)}, bf16[32,2048]{1,0:T(8,128)(2,1)S(1)}, u32[]{:S(2)}, u32[]{:S(2)}) %collective-permute-start.31) | collective-permute-done | bytes 131104 | tf_op jit(solution)/shard_map/ppermute | solution.py:283
  89.9 0.9 shard_map.81
  90.9 1.1 %collective-permute-done.32.front_ref = bf16[32,2048]{1,0:T(8,128)(2,1)S(1)} collective-permute-done((bf16[32,2048]{1,0:T(8,128)(2,1)S(1)}, bf16[32,2048]{1,0:T(8,128)(2,1)S(1)}, u32[]{:S(2)}, u32[]{:S(2)}) %collective-permute-start.32) | collective-permute-done | bytes 131104 | tf_op jit(solution)/shard_map/ppermute | solution.py:283
  92.0 0.9 shard_map.83
  93.0 1.1 %shard_map.85 = (bf16[32,4096]{1,0:T(8,128)(2,1)}, f32[32,128]{1,0:T(8,128)S(1)}) custom-call(f32[32,2048]{1,0:T(8,128)S(1)} %get-tuple-element.143.refs_0_, f32[32,2048]{1,0:T(8,128)S(1)} %get-tuple-element.149.refs_1_, f32[2,32,128]{2,1,0:T(8,128)S(1)} %get-tuple-element.148.refs_0_.refs_2_, ...), custom_call_target="tpu_custom_call", output_to_operand_aliasing={{1}: (4, {})} | custom-call | tf_op jit(solution)/shard_map/pallas_call | solution.py:30
  (58 shorter events, 4.3 us)
Async XLA Ops:
  0.0 9.9 %slice-start = ((s8[8388608]{0:T(1024)(128)(4,1)}), s8[4194304]{0:T(1024)(128)(4,1)S(1)}, s32[]{:S(2)}) async-start(s8[8388608]{0:T(1024)(128)(4,1)} %bitcast.8), calls=%async_computation | async-start | bytes 8388608
  1.6 14.9 %collective-permute-start.4 = (bf16[64,4096]{1,0:T(8,128)(2,1)S(1)}, bf16[64,4096]{1,0:T(8,128)(2,1)S(1)}, u32[]{:S(2)}, u32[]{:S(2)}) collective-permute-start(bf16[64,4096]{1,0:T(8,128)(2,1)S(1)} %bitcast.46), channel_id=1, source_target_pairs={{4,0},{5,1},{6,2},{7,3},{12,8},{13,9},{14,10},{15,11},{16,12},{17,... | collective-permute-start | bytes 1572872 | tf_op jit(solution)/shard_map/ppermute | solution.py:283
  4.2 5.7 %slice-start.1 = ((s8[8388608]{0:T(1024)(128)(4,1)}), s8[4194304]{0:T(1024)(128)(4,1)S(1)}, s32[]{:S(2)}) async-start(s8[8388608]{0:T(1024)(128)(4,1)} %bitcast.8), calls=%async_computation.1 | async-start | bytes 8388608
  4.2 5.7 %copy-start.1 = (bf16[1,4,64,4096]{3,2,1,0:T(8,128)(2,1)S(1)}, bf16[1,4,64,4096]{3,2,1,0:T(8,128)(2,1)}, u32[]{:S(2)}) copy-start(bf16[1,4,64,4096]{3,2,1,0:T(8,128)(2,1)} %param.6) | copy-start | bytes 6291460
  4.7 7.1 %collective-permute-start = (bf16[32,128]{1,0:T(8,128)(2,1)S(1)}, bf16[32,128]{1,0:T(8,128)(2,1)S(1)}, u32[]{:S(2)}, u32[]{:S(2)}) collective-permute-start(bf16[32,128]{1,0:T(8,128)(2,1)S(1)} %shard_map.48), channel_id=1, source_target_pairs={{0,1},{1,0},{2,3},{3,2},{4,5},{5,4},{6,7},{7,6},{8,9},{9,8},{10,11... | collective-permute-start | bytes 24584 | tf_op jit(solution)/shard_map/ppermute | solution.py:283
  4.8 7.1 %collective-permute-start.1 = (bf16[32,128]{1,0:T(8,128)(2,1)S(1)}, bf16[32,128]{1,0:T(8,128)(2,1)S(1)}, u32[]{:S(2)}, u32[]{:S(2)}) collective-permute-start(bf16[32,128]{1,0:T(8,128)(2,1)S(1)} %shard_map.48), channel_id=1, source_target_pairs={{0,2},{1,3},{2,0},{3,1},{4,6},{5,7},{6,4},{7,5},{8,10},{9,11},{10,... | collective-permute-start | bytes 24584 | tf_op jit(solution)/shard_map/ppermute | solution.py:283
  6.3 5.5 %collective-permute-start.2 = (bf16[32,128]{1,0:T(8,128)(2,1)S(1)}, bf16[32,128]{1,0:T(8,128)(2,1)S(1)}, u32[]{:S(2)}, u32[]{:S(2)}) collective-permute-start(bf16[32,128]{1,0:T(8,128)(2,1)S(1)} %shard_map.48), channel_id=1, source_target_pairs={{0,3},{1,2},{2,1},{3,0},{4,7},{5,6},{6,5},{7,4},{8,11},{9,10},{10,... | collective-permute-start | bytes 24584 | tf_op jit(solution)/shard_map/ppermute | solution.py:283
  6.6 20.0 %collective-permute-start.10 = (bf16[64,4096]{1,0:T(8,128)(2,1)S(1)}, bf16[64,4096]{1,0:T(8,128)(2,1)S(1)}, u32[]{:S(2)}, u32[]{:S(2)}) collective-permute-start(bf16[64,4096]{1,0:T(8,128)(2,1)S(1)} %bitcast.44), channel_id=1, source_target_pairs={{12,8},{13,9},{14,10},{15,11},{16,12},{17,13},{18,14},{19,15},{20,... | collective-permute-start | bytes 1572872 | tf_op jit(solution)/shard_map/ppermute | solution.py:283
  9.9 1.9 %copy-start = (bf16[1,4,64,4096]{3,2,1,0:T(8,128)(2,1)S(1)}, bf16[1,4,64,4096]{3,2,1,0:T(8,128)(2,1)}, u32[]{:S(2)}) copy-start(bf16[1,4,64,4096]{3,2,1,0:T(8,128)(2,1)} %param.7) | copy-start | bytes 6291460
  12.3 6.2 %collective-permute-start.3 = (bf16[32,4096]{1,0:T(8,128)(2,1)S(1)}, bf16[32,4096]{1,0:T(8,128)(2,1)S(1)}, u32[]{:S(2)}, u32[]{:S(2)}) collective-permute-start(bf16[32,4096]{1,0:T(8,128)(2,1)S(1)} %get-tuple-element.87.refs_1_), channel_id=1, source_target_pairs={{0,4},{1,5},{2,6},{3,7}} | collective-permute-start | bytes 786440 | tf_op jit(solution)/shard_map/ppermute | solution.py:283
  16.8 2.7 %collective-permute-start.5 = (bf16[32,128]{1,0:T(8,128)(2,1)S(1)}, bf16[32,128]{1,0:T(8,128)(2,1)S(1)}, u32[]{:S(2)}, u32[]{:S(2)}) collective-permute-start(bf16[32,128]{1,0:T(8,128)(2,1)S(1)} %shard_map.50.other_ref.refs_0_.refs_2_), channel_id=1, source_target_pairs={{0,6},{1,7},{2,4},{3,5}} | collective-permute-start | bytes 24584 | tf_op jit(solution)/shard_map/ppermute | solution.py:283
  17.8 4.7 %collective-permute-start.8 = (bf16[64,4096]{1,0:T(8,128)(2,1)S(1)}, bf16[64,4096]{1,0:T(8,128)(2,1)S(1)}, u32[]{:S(2)}, u32[]{:S(2)}) collective-permute-start(bf16[64,4096]{1,0:T(8,128)(2,1)S(1)} %get-tuple-element.101), channel_id=1, source_target_pairs={{8,4},{9,5},{10,6},{11,7}} | collective-permute-start | bytes 1572872 | tf_op jit(solution)/shard_map/ppermute | solution.py:283
  19.8 1.6 %collective-permute-start.6 = (bf16[32,128]{1,0:T(8,128)(2,1)S(1)}, bf16[32,128]{1,0:T(8,128)(2,1)S(1)}, u32[]{:S(2)}, u32[]{:S(2)}) collective-permute-start(bf16[32,128]{1,0:T(8,128)(2,1)S(1)} %shard_map.53.refs_0_), channel_id=1, source_target_pairs={{4,5},{5,4},{6,7},{7,6}} | collective-permute-start | bytes 24584 | tf_op jit(solution)/shard_map/ppermute | solution.py:283
  21.8 5.2 %collective-permute-start.7 = (bf16[32,4096]{1,0:T(8,128)(2,1)S(1)}, bf16[32,4096]{1,0:T(8,128)(2,1)S(1)}, u32[]{:S(2)}, u32[]{:S(2)}) collective-permute-start(bf16[32,4096]{1,0:T(8,128)(2,1)S(1)} %get-tuple-element.96.refs_1_), channel_id=1, source_target_pairs={{4,8},{5,9},{6,10},{7,11}} | collective-permute-start | bytes 786440 | tf_op jit(solution)/shard_map/ppermute | solution.py:283
  22.7 5.1 %collective-permute-start.9 = (bf16[32,128]{1,0:T(8,128)(2,1)S(1)}, bf16[32,128]{1,0:T(8,128)(2,1)S(1)}, u32[]{:S(2)}, u32[]{:S(2)}) collective-permute-start(bf16[32,128]{1,0:T(8,128)(2,1)S(1)} %shard_map.57), channel_id=1, source_target_pairs={{4,10},{5,11},{6,8},{7,9}} | collective-permute-start | bytes 24584 | tf_op jit(solution)/shard_map/ppermute | solution.py:283
  28.2 1.6 %collective-permute-start.11 = (bf16[32,128]{1,0:T(8,128)(2,1)S(1)}, bf16[32,128]{1,0:T(8,128)(2,1)S(1)}, u32[]{:S(2)}, u32[]{:S(2)}) collective-permute-start(bf16[32,128]{1,0:T(8,128)(2,1)S(1)} %shard_map.59.refs_0_), channel_id=1, source_target_pairs={{8,9},{9,8},{10,11},{11,10}} | collective-permute-start | bytes 24584 | tf_op jit(solution)/shard_map/ppermute | solution.py:283
  30.1 3.9 %collective-permute-start.12 = (bf16[32,2048]{1,0:T(8,128)(2,1)S(1)}, bf16[32,2048]{1,0:T(8,128)(2,1)S(1)}, u32[]{:S(2)}, u32[]{:S(2)}) collective-permute-start(bf16[32,2048]{1,0:T(8,128)(2,1)S(1)} %get-tuple-element.104.refs_0_), channel_id=1, source_target_pairs={{8,12},{9,13},{10,14},{11,15}} | collective-permute-start | bytes 393224 | tf_op jit(solution)/shard_map/ppermute | solution.py:283
  31.0 3.9 %collective-permute-start.13 = (bf16[32,2048]{1,0:T(8,128)(2,1)S(1)}, bf16[32,2048]{1,0:T(8,128)(2,1)S(1)}, u32[]{:S(2)}, u32[]{:S(2)}) collective-permute-start(bf16[32,2048]{1,0:T(8,128)(2,1)S(1)} %get-tuple-element.110.refs_1_), channel_id=1, source_target_pairs={{8,12},{9,13},{10,14},{11,15}} | collective-permute-start | bytes 393224 | tf_op jit(solution)/shard_map/ppermute | solution.py:283
  32.0 3.9 %collective-permute-start.14 = (bf16[32,128]{1,0:T(8,128)(2,1)S(1)}, bf16[32,128]{1,0:T(8,128)(2,1)S(1)}, u32[]{:S(2)}, u32[]{:S(2)}) collective-permute-start(bf16[32,128]{1,0:T(8,128)(2,1)S(1)} %shard_map.65), channel_id=1, source_target_pairs={{8,15},{9,14},{10,13},{11,12}} | collective-permute-start | bytes 24584 | tf_op jit(solution)/shard_map/ppermute | solution.py:283
  32.6 3.2 %collective-permute-start.15 = (bf16[32,128]{1,0:T(8,128)(2,1)S(1)}, bf16[32,128]{1,0:T(8,128)(2,1)S(1)}, u32[]{:S(2)}, u32[]{:S(2)}) collective-permute-start(bf16[32,128]{1,0:T(8,128)(2,1)S(1)} %shard_map.65), channel_id=1, source_target_pairs={{8,14},{9,15},{10,12},{11,13}} | collective-permute-start | bytes 24584 | tf_op jit(solution)/shard_map/ppermute | solution.py:283
  33.3 2.6 %collective-permute-start.16 = (bf16[32,128]{1,0:T(8,128)(2,1)S(1)}, bf16[32,128]{1,0:T(8,128)(2,1)S(1)}, u32[]{:S(2)}, u32[]{:S(2)}) collective-permute-start(bf16[32,128]{1,0:T(8,128)(2,1)S(1)} %shard_map.65), channel_id=1, source_target_pairs={{8,13},{9,12},{10,15},{11,14}} | collective-permute-start | bytes 24584 | tf_op jit(solution)/shard_map/ppermute | solution.py:283
  36.3 3.0 %collective-permute-start.17 = (bf16[32,4096]{1,0:T(8,128)(2,1)S(1)}, bf16[32,4096]{1,0:T(8,128)(2,1)S(1)}, u32[]{:S(2)}, u32[]{:S(2)}) collective-permute-start(bf16[32,4096]{1,0:T(8,128)(2,1)S(1)} %get-tuple-element.115.refs_0_), channel_id=1, source_target_pairs={{12,16},{13,17},{14,18},{15,19}} | collective-permute-start | bytes 786440 | tf_op jit(solution)/shard_map/ppermute | solution.py:283
  37.3 3.9 %collective-permute-start.18 = (bf16[32,128]{1,0:T(8,128)(2,1)S(1)}, bf16[32,128]{1,0:T(8,128)(2,1)S(1)}, u32[]{:S(2)}, u32[]{:S(2)}) collective-permute-start(bf16[32,128]{1,0:T(8,128)(2,1)S(1)} %shard_map.69), channel_id=1, source_target_pairs={{12,19},{13,18},{14,17},{15,16}} | collective-permute-start | bytes 24584 | tf_op jit(solution)/shard_map/ppermute | solution.py:283
  37.9 3.2 %collective-permute-start.19 = (bf16[32,128]{1,0:T(8,128)(2,1)S(1)}, bf16[32,128]{1,0:T(8,128)(2,1)S(1)}, u32[]{:S(2)}, u32[]{:S(2)}) collective-permute-start(bf16[32,128]{1,0:T(8,128)(2,1)S(1)} %shard_map.69), channel_id=1, source_target_pairs={{12,18},{13,19},{14,16},{15,17}} | collective-permute-start | bytes 24584 | tf_op jit(solution)/shard_map/ppermute | solution.py:283
  38.6 2.6 %collective-permute-start.20 = (bf16[32,128]{1,0:T(8,128)(2,1)S(1)}, bf16[32,128]{1,0:T(8,128)(2,1)S(1)}, u32[]{:S(2)}, u32[]{:S(2)}) collective-permute-start(bf16[32,128]{1,0:T(8,128)(2,1)S(1)} %shard_map.69), channel_id=1, source_target_pairs={{12,17},{13,16},{14,19},{15,18}} | collective-permute-start | bytes 24584 | tf_op jit(solution)/shard_map/ppermute | solution.py:283
  41.4 4.1 %collective-permute-start.21 = (bf16[32,2048]{1,0:T(8,128)(2,1)S(1)}, bf16[32,2048]{1,0:T(8,128)(2,1)S(1)}, u32[]{:S(2)}, u32[]{:S(2)}) collective-permute-start(bf16[32,2048]{1,0:T(8,128)(2,1)S(1)} %get-tuple-element.122.refs_0_), channel_id=1, source_target_pairs={{16,20},{17,21},{18,22},{19,23}} | collective-permute-start | bytes 393224 | tf_op jit(solution)/shard_map/ppermute | solution.py:283
  42.4 4.1 %collective-permute-start.22 = (bf16[32,2048]{1,0:T(8,128)(2,1)S(1)}, bf16[32,2048]{1,0:T(8,128)(2,1)S(1)}, u32[]{:S(2)}, u32[]{:S(2)}) collective-permute-start(bf16[32,2048]{1,0:T(8,128)(2,1)S(1)} %get-tuple-element.129.refs_1_), channel_id=1, source_target_pairs={{16,20},{17,21},{18,22},{19,23}} | collective-permute-start | bytes 393224 | tf_op jit(solution)/shard_map/ppermute | solution.py:283
  43.5 3.9 %collective-permute-start.23 = (bf16[32,128]{1,0:T(8,128)(2,1)S(1)}, bf16[32,128]{1,0:T(8,128)(2,1)S(1)}, u32[]{:S(2)}, u32[]{:S(2)}) collective-permute-start(bf16[32,128]{1,0:T(8,128)(2,1)S(1)} %shard_map.74), channel_id=1, source_target_pairs={{16,23},{17,22},{18,21},{19,20}} | collective-permute-start | bytes 24584 | tf_op jit(solution)/shard_map/ppermute | solution.py:283
  44.2 3.2 %collective-permute-start.24 = (bf16[32,128]{1,0:T(8,128)(2,1)S(1)}, bf16[32,128]{1,0:T(8,128)(2,1)S(1)}, u32[]{:S(2)}, u32[]{:S(2)}) collective-permute-start(bf16[32,128]{1,0:T(8,128)(2,1)S(1)} %shard_map.74), channel_id=1, source_target_pairs={{16,22},{17,23},{18,20},{19,21}} | collective-permute-start | bytes 24584 | tf_op jit(solution)/shard_map/ppermute | solution.py:283
  44.9 2.6 %collective-permute-start.25 = (bf16[32,128]{1,0:T(8,128)(2,1)S(1)}, bf16[32,128]{1,0:T(8,128)(2,1)S(1)}, u32[]{:S(2)}, u32[]{:S(2)}) collective-permute-start(bf16[32,128]{1,0:T(8,128)(2,1)S(1)} %shard_map.74), channel_id=1, source_target_pairs={{16,21},{17,20},{18,23},{19,22}} | collective-permute-start | bytes 24584 | tf_op jit(solution)/shard_map/ppermute | solution.py:283
  47.7 3.9 %collective-permute-start.26 = (bf16[32,2048]{1,0:T(8,128)(2,1)S(1)}, bf16[32,2048]{1,0:T(8,128)(2,1)S(1)}, u32[]{:S(2)}, u32[]{:S(2)}) collective-permute-start(bf16[32,2048]{1,0:T(8,128)(2,1)S(1)} %get-tuple-element.132.refs_0_), channel_id=1, source_target_pairs={{20,24},{21,25},{22,26},{23,27}} | collective-permute-start | bytes 393224 | tf_op jit(solution)/shard_map/ppermute | solution.py:283
  48.7 3.9 %collective-permute-start.27 = (bf16[32,2048]{1,0:T(8,128)(2,1)S(1)}, bf16[32,2048]{1,0:T(8,128)(2,1)S(1)}, u32[]{:S(2)}, u32[]{:S(2)}) collective-permute-start(bf16[32,2048]{1,0:T(8,128)(2,1)S(1)} %get-tuple-element.139.refs_1_), channel_id=1, source_target_pairs={{20,24},{21,25},{22,26},{23,27}} | collective-permute-start | bytes 393224 | tf_op jit(solution)/shard_map/ppermute | solution.py:283
  49.6 3.9 %collective-permute-start.28 = (bf16[32,128]{1,0:T(8,128)(2,1)S(1)}, bf16[32,128]{1,0:T(8,128)(2,1)S(1)}, u32[]{:S(2)}, u32[]{:S(2)}) collective-permute-start(bf16[32,128]{1,0:T(8,128)(2,1)S(1)} %shard_map.79), channel_id=1, source_target_pairs={{20,27},{21,26},{22,25},{23,24}} | collective-permute-start | bytes 24584 | tf_op jit(solution)/shard_map/ppermute | solution.py:283
  50.3 3.2 %collective-permute-start.29 = (bf16[32,128]{1,0:T(8,128)(2,1)S(1)}, bf16[32,128]{1,0:T(8,128)(2,1)S(1)}, u32[]{:S(2)}, u32[]{:S(2)}) collective-permute-start(bf16[32,128]{1,0:T(8,128)(2,1)S(1)} %shard_map.79), channel_id=1, source_target_pairs={{20,26},{21,27},{22,24},{23,25}} | collective-permute-start | bytes 24584 | tf_op jit(solution)/shard_map/ppermute | solution.py:283
  51.0 2.6 %collective-permute-start.30 = (bf16[32,128]{1,0:T(8,128)(2,1)S(1)}, bf16[32,128]{1,0:T(8,128)(2,1)S(1)}, u32[]{:S(2)}, u32[]{:S(2)}) collective-permute-start(bf16[32,128]{1,0:T(8,128)(2,1)S(1)} %shard_map.79), channel_id=1, source_target_pairs={{20,25},{21,24},{22,27},{23,26}} | collective-permute-start | bytes 24584 | tf_op jit(solution)/shard_map/ppermute | solution.py:283
  53.8 36.1 %collective-permute-start.31 = (bf16[32,2048]{1,0:T(8,128)(2,1)S(1)}, bf16[32,2048]{1,0:T(8,128)(2,1)S(1)}, u32[]{:S(2)}, u32[]{:S(2)}) collective-permute-start(bf16[32,2048]{1,0:T(8,128)(2,1)S(1)} %get-tuple-element.142.refs_0_), channel_id=1, source_target_pairs={{24,28},{25,29},{26,30},{27,31}} | collective-permute-start | bytes 393224 | tf_op jit(solution)/shard_map/ppermute | solution.py:283
  55.4 36.6 %collective-permute-start.32 = (bf16[32,2048]{1,0:T(8,128)(2,1)S(1)}, bf16[32,2048]{1,0:T(8,128)(2,1)S(1)}, u32[]{:S(2)}, u32[]{:S(2)}) collective-permute-start(bf16[32,2048]{1,0:T(8,128)(2,1)S(1)} %get-tuple-element.147.refs_1_), channel_id=1, source_target_pairs={{24,28},{25,29},{26,30},{27,31}} | collective-permute-start | bytes 393224 | tf_op jit(solution)/shard_map/ppermute | solution.py:283
  57.0 35.9 %collective-permute-start.33 = (bf16[32,128]{1,0:T(8,128)(2,1)S(1)}, bf16[32,128]{1,0:T(8,128)(2,1)S(1)}, u32[]{:S(2)}, u32[]{:S(2)}) collective-permute-start(bf16[32,128]{1,0:T(8,128)(2,1)S(1)} %shard_map.84), channel_id=1, source_target_pairs={{24,31},{25,30},{26,29},{27,28}} | collective-permute-start | bytes 24584 | tf_op jit(solution)/shard_map/ppermute | solution.py:283
  58.3 34.7 %collective-permute-start.34 = (bf16[32,128]{1,0:T(8,128)(2,1)S(1)}, bf16[32,128]{1,0:T(8,128)(2,1)S(1)}, u32[]{:S(2)}, u32[]{:S(2)}) collective-permute-start(bf16[32,128]{1,0:T(8,128)(2,1)S(1)} %shard_map.84), channel_id=1, source_target_pairs={{24,30},{25,31},{26,28},{27,29}} | collective-permute-start | bytes 24584 | tf_op jit(solution)/shard_map/ppermute | solution.py:283
  59.6 33.5 %collective-permute-start.35 = (bf16[32,128]{1,0:T(8,128)(2,1)S(1)}, bf16[32,128]{1,0:T(8,128)(2,1)S(1)}, u32[]{:S(2)}, u32[]{:S(2)}) collective-permute-start(bf16[32,128]{1,0:T(8,128)(2,1)S(1)} %shard_map.84), channel_id=1, source_target_pairs={{24,29},{25,28},{26,31},{27,30}} | collective-permute-start | bytes 24584 | tf_op jit(solution)/shard_map/ppermute | solution.py:283

commit v3 on v2

--- a/solution.py
+++ b/solution.py
@@ -277,6 +277,7 @@
     spans = ((0, cut), (cut, width))
     offsets = list(range(1, devices))
     levels_of = [cross - x.bit_length() for x in offsets]
+    other_core_first = sorted(offsets, key=lambda x: (x % 2 == 0, -x))
 
     def moved(x, moves, offset=0):
         route = [(a * devices + h, b * devices + (h ^ offset)) for a, b in moves for h in range(devices)]
@@ -308,7 +309,7 @@
     second = moved(late, [(2, 1)])
     levels_relayed = [cross - x.bit_length() for x in relayed]
     for k in range(1, chain):
-        levels_now = levels_of[::-1]
+        levels_now = [cross - x.bit_length() for x in other_core_first]
         for i, span in enumerate(spans):
             behind = projected[i - 1 : i] if i else ahead if k == 1 else []
             if i == 1 and k <= IN_PLACE:
@@ -342,7 +343,7 @@
             p = project(whole, outs, [second], ranks)
         else:
             p = project_turned(spans if split else whole, outs, turned)
-        sent = relayed if k < IN_PLACE else offsets[::-1]
+        sent = relayed if k < IN_PLACE else other_core_first
         parts = [moved(p, [(k, k + 1)], x) for x in sent]
 
 

time: 94.9 us -> 96 us (1.012)
  waiting for transfers between devices: 37.1 us -> 38.5 us
    ppermute x36, waiting for transfers between devices: 37.1 us -> 38.5 us  [moved(): return lax.ppermute(x, ('slab', 'hodlr'), route)]
where the time goes in v3:
time: 96 us; the launch traced here: 95.6 us
  waiting for transfers between devices  38.5 us (40%)
  starting transfers between devices  31.8 us (33%)
  Pallas kernels  24.5 us (26%)
    ppermute x36, waiting for transfers between devices, moved(): return lax.ppermute(x, ('slab', 'hodlr'), route)  38.5 us
    ppermute x36, starting transfers between devices, moved(): return lax.ppermute(x, ('slab', 'hodlr'), route)  31.8 us
    pallas_call x40, Pallas kernels, call(): pl.pallas_call(kernel, out_shape=outs, in_specs=[remote if i in from_hbm...  24.5 us
  transfers between devices with their start and end apart: 36, of which 5 were waited for; matrix products, arithmetic and copies ran while one was open for 0% of the time, Pallas kernels for 21%

profile of v3, /device:TPU:26, one launch (start us, length us, event | category | flops | bytes accessed | tf_op | source)
XLA Modules:
  0.0 95.6 jit_solution(13589393844371276473)
XLA Ops:
  0.0 1.6 %shard_map.46 = (bf16[1,64,4096]{2,1,0:T(8,128)(2,1)S(1)}, bf16[1,64,4096]{2,1,0:T(8,128)(2,1)S(1)}, bf16[1,64,4096]{2,1,0:T(8,128)(2,1)S(1)}, bf16[32,2048]{1,0:T(8,128)(2,1)S(1)}, bf16[32,2048]{1,0:T(8,128)(2,1)S(1)}) custom-call(bf16[32,4096]{1,0:T(8,128)(2,1)} %bitcast.47, bf16[4,64,4096]{2,1,0:T(8,128)(2,1)} %bitcast.37), custom_call_target="tpu_custom_call" | custom-call | tf_op jit(solution)/shard_map/pallas_call | solution.py:30
  1.6 2.6 %collective-permute-start.4 = (bf16[64,4096]{1,0:T(8,128)(2,1)S(1)}, bf16[64,4096]{1,0:T(8,128)(2,1)S(1)}, u32[]{:S(2)}, u32[]{:S(2)}) collective-permute-start(bf16[64,4096]{1,0:T(8,128)(2,1)S(1)} %bitcast.46), channel_id=1, source_target_pairs={{4,0},{5,1},{6,2},{7,3},{12,8},{13,9},{14,10},{15,11},{16,12},{17,... | collective-permute-start | bytes 1572872 | tf_op jit(solution)/shard_map/ppermute | solution.py:284
  4.3 0.4 shard_map.48
  4.8 1.6 %collective-permute-start.1 = (bf16[32,128]{1,0:T(8,128)(2,1)S(1)}, bf16[32,128]{1,0:T(8,128)(2,1)S(1)}, u32[]{:S(2)}, u32[]{:S(2)}) collective-permute-start(bf16[32,128]{1,0:T(8,128)(2,1)S(1)} %shard_map.48), channel_id=1, source_target_pairs={{0,2},{1,3},{2,0},{3,1},{4,6},{5,7},{6,4},{7,5},{8,10},{9,11},{10,... | collective-permute-start | bytes 24584 | tf_op jit(solution)/shard_map/ppermute | solution.py:284
  6.6 3.3 %collective-permute-start.10 = (bf16[64,4096]{1,0:T(8,128)(2,1)S(1)}, bf16[64,4096]{1,0:T(8,128)(2,1)S(1)}, u32[]{:S(2)}, u32[]{:S(2)}) collective-permute-start(bf16[64,4096]{1,0:T(8,128)(2,1)S(1)} %bitcast.44), channel_id=1, source_target_pairs={{12,8},{13,9},{14,10},{15,11},{16,12},{17,13},{18,14},{19,15},{20,... | collective-permute-start | bytes 1572872 | tf_op jit(solution)/shard_map/ppermute | solution.py:284
  9.9 1.9 %shard_map.47 = (f32[32,2048]{1,0:T(8,128)S(1)}, f32[32,2048]{1,0:T(8,128)S(1)}, f32[2,32,128]{2,1,0:T(8,128)S(1)}, f32[2,32,128]{2,1,0:T(8,128)S(1)}) custom-call(bf16[32,2048]{1,0:T(8,128)(2,1)S(1)} %get-tuple-element.79.refs_0_.refs_2_.w_ref, bf16[32,2048]{1,0:T(8,128)(2,1)S(1)} %get-tuple-element.80.refs_1_.refs_3_.w_ref, ...), custom_call_target="tpu_custom_call" | custom-call | tf_op jit(solution)/shard_map/pallas_call | solution.py:30
  11.9 0.4 shard_map.49
  12.3 0.7 collective-permute-start.3
  13.0 3.5 %collective-permute-done.4.refs_0_.refs_1_ = bf16[64,4096]{1,0:T(8,128)(2,1)S(1)} collective-permute-done((bf16[64,4096]{1,0:T(8,128)(2,1)S(1)}, bf16[64,4096]{1,0:T(8,128)(2,1)S(1)}, u32[]{:S(2)}, u32[]{:S(2)}) %collective-permute-start.4) | collective-permute-done | bytes 524320 | tf_op jit(solution)/shard_map/ppermute | solution.py:284
  16.8 0.7 collective-permute-start.5
  17.4 0.3 shard_map.51
  17.8 0.7 collective-permute-start.8
  18.5 0.9 shard_map.52
  19.4 0.3 shard_map.53.refs_0_
  19.8 0.7 collective-permute-start.6
  20.4 0.9 shard_map.54
  21.4 0.4 shard_map.55
  21.8 0.7 collective-permute-start.7
  22.7 0.7 collective-permute-start.9
  23.4 3.2 %collective-permute-done.10.refs_0_ = bf16[64,4096]{1,0:T(8,128)(2,1)S(1)} collective-permute-done((bf16[64,4096]{1,0:T(8,128)(2,1)S(1)}, bf16[64,4096]{1,0:T(8,128)(2,1)S(1)}, u32[]{:S(2)}, u32[]{:S(2)}) %collective-permute-start.10) | collective-permute-done | bytes 524320 | tf_op jit(solution)/shard_map/ppermute | solution.py:284
  26.6 0.3 shard_map.58.refs_2_.v_ref
  26.9 0.9 shard_map.56
  27.9 0.3 shard_map.59.refs_0_
  28.2 0.7 collective-permute-start.11
  28.9 0.9 shard_map.60
  30.1 0.7 collective-permute-start.12
  31.0 0.7 collective-permute-start.13
  32.0 0.7 collective-permute-start.14
  32.6 0.7 collective-permute-start.15
  33.3 0.7 collective-permute-start.16
  34.0 0.9 shard_map.62
  34.9 0.9 shard_map.64
  35.9 0.4 shard_map.66
  36.3 0.7 collective-permute-start.17
  37.3 0.7 collective-permute-start.18
  37.9 0.7 collective-permute-start.19
  38.6 0.7 collective-permute-start.20
  39.3 0.9 shard_map.67
  40.2 0.9 shard_map.68
  41.4 0.7 collective-permute-start.21
  42.4 0.8 collective-permute-start.22
  43.5 0.7 collective-permute-start.23
  44.2 0.7 collective-permute-start.24
  44.9 0.7 collective-permute-start.25
  45.6 0.9 shard_map.71
  46.5 0.9 shard_map.73
  47.7 0.7 collective-permute-start.26
  48.7 0.7 collective-permute-start.27
  49.6 0.7 collective-permute-start.28
  50.3 0.7 collective-permute-start.29
  51.0 0.7 collective-permute-start.30
  51.7 0.9 shard_map.76
  52.6 0.9 shard_map.78
  53.8 1.3 %collective-permute-start.31 = (bf16[32,2048]{1,0:T(8,128)(2,1)S(1)}, bf16[32,2048]{1,0:T(8,128)(2,1)S(1)}, u32[]{:S(2)}, u32[]{:S(2)}) collective-permute-start(bf16[32,2048]{1,0:T(8,128)(2,1)S(1)} %get-tuple-element.142.refs_0_), channel_id=1, source_target_pairs={{24,28},{25,29},{26,30},{27,31}} | collective-permute-start | bytes 393224 | tf_op jit(solution)/shard_map/ppermute | solution.py:284
  55.4 1.3 %collective-permute-start.32 = (bf16[32,2048]{1,0:T(8,128)(2,1)S(1)}, bf16[32,2048]{1,0:T(8,128)(2,1)S(1)}, u32[]{:S(2)}, u32[]{:S(2)}) collective-permute-start(bf16[32,2048]{1,0:T(8,128)(2,1)S(1)} %get-tuple-element.147.refs_1_), channel_id=1, source_target_pairs={{24,28},{25,29},{26,30},{27,31}} | collective-permute-start | bytes 393224 | tf_op jit(solution)/shard_map/ppermute | solution.py:284
  57.0 1.3 %collective-permute-start.33 = (bf16[32,128]{1,0:T(8,128)(2,1)S(1)}, bf16[32,128]{1,0:T(8,128)(2,1)S(1)}, u32[]{:S(2)}, u32[]{:S(2)}) collective-permute-start(bf16[32,128]{1,0:T(8,128)(2,1)S(1)} %shard_map.84), channel_id=1, source_target_pairs={{24,31},{25,30},{26,29},{27,28}} | collective-permute-start | bytes 24584 | tf_op jit(solution)/shard_map/ppermute | solution.py:284
  58.3 1.3 %collective-permute-start.34 = (bf16[32,128]{1,0:T(8,128)(2,1)S(1)}, bf16[32,128]{1,0:T(8,128)(2,1)S(1)}, u32[]{:S(2)}, u32[]{:S(2)}) collective-permute-start(bf16[32,128]{1,0:T(8,128)(2,1)S(1)} %shard_map.84), channel_id=1, source_target_pairs={{24,29},{25,28},{26,31},{27,30}} | collective-permute-start | bytes 24584 | tf_op jit(solution)/shard_map/ppermute | solution.py:284
  59.6 1.3 %collective-permute-start.35 = (bf16[32,128]{1,0:T(8,128)(2,1)S(1)}, bf16[32,128]{1,0:T(8,128)(2,1)S(1)}, u32[]{:S(2)}, u32[]{:S(2)}) collective-permute-start(bf16[32,128]{1,0:T(8,128)(2,1)S(1)} %shard_map.84), channel_id=1, source_target_pairs={{24,30},{25,31},{26,28},{27,29}} | collective-permute-start | bytes 24584 | tf_op jit(solution)/shard_map/ppermute | solution.py:284
  60.9 29.1 %collective-permute-done.31.front_ref = bf16[32,2048]{1,0:T(8,128)(2,1)S(1)} collective-permute-done((bf16[32,2048]{1,0:T(8,128)(2,1)S(1)}, bf16[32,2048]{1,0:T(8,128)(2,1)S(1)}, u32[]{:S(2)}, u32[]{:S(2)}) %collective-permute-start.31) | collective-permute-done | bytes 131104 | tf_op jit(solution)/shard_map/ppermute | solution.py:284
  90.0 0.9 shard_map.81
  90.9 0.7 collective-permute-done.32.front_ref
  91.6 0.9 shard_map.83
  92.5 1.9 %collective-permute-done.35.refs_7_ = bf16[32,128]{1,0:T(8,128)(2,1)S(1)} collective-permute-done((bf16[32,128]{1,0:T(8,128)(2,1)S(1)}, bf16[32,128]{1,0:T(8,128)(2,1)S(1)}, u32[]{:S(2)}, u32[]{:S(2)}) %collective-permute-start.35) | collective-permute-done | bytes 8224 | tf_op jit(solution)/shard_map/ppermute | solution.py:284
  94.4 1.1 %shard_map.85 = (bf16[32,4096]{1,0:T(8,128)(2,1)}, f32[32,128]{1,0:T(8,128)S(1)}) custom-call(f32[32,2048]{1,0:T(8,128)S(1)} %get-tuple-element.143.refs_0_, f32[32,2048]{1,0:T(8,128)S(1)} %get-tuple-element.149.refs_1_, f32[2,32,128]{2,1,0:T(8,128)S(1)} %get-tuple-element.148.refs_0_.refs_2_, ...), custom_call_target="tpu_custom_call", output_to_operand_aliasing={{1}: (4, {})} | custom-call | tf_op jit(solution)/shard_map/pallas_call | solution.py:30
  (58 shorter events, 4.5 us)
Async XLA Ops:
  0.0 9.9 %slice-start = ((s8[8388608]{0:T(1024)(128)(4,1)}), s8[4194304]{0:T(1024)(128)(4,1)S(1)}, s32[]{:S(2)}) async-start(s8[8388608]{0:T(1024)(128)(4,1)} %bitcast.8), calls=%async_computation | async-start | bytes 8388608
  1.6 14.9 %collective-permute-start.4 = (bf16[64,4096]{1,0:T(8,128)(2,1)S(1)}, bf16[64,4096]{1,0:T(8,128)(2,1)S(1)}, u32[]{:S(2)}, u32[]{:S(2)}) collective-permute-start(bf16[64,4096]{1,0:T(8,128)(2,1)S(1)} %bitcast.46), channel_id=1, source_target_pairs={{4,0},{5,1},{6,2},{7,3},{12,8},{13,9},{14,10},{15,11},{16,12},{17,... | collective-permute-start | bytes 1572872 | tf_op jit(solution)/shard_map/ppermute | solution.py:284
  4.2 5.7 %slice-start.1 = ((s8[8388608]{0:T(1024)(128)(4,1)}), s8[4194304]{0:T(1024)(128)(4,1)S(1)}, s32[]{:S(2)}) async-start(s8[8388608]{0:T(1024)(128)(4,1)} %bitcast.8), calls=%async_computation.1 | async-start | bytes 8388608
  4.2 5.7 %copy-start.1 = (bf16[1,4,64,4096]{3,2,1,0:T(8,128)(2,1)S(1)}, bf16[1,4,64,4096]{3,2,1,0:T(8,128)(2,1)}, u32[]{:S(2)}) copy-start(bf16[1,4,64,4096]{3,2,1,0:T(8,128)(2,1)} %param.6) | copy-start | bytes 6291460
  4.7 7.1 %collective-permute-start = (bf16[32,128]{1,0:T(8,128)(2,1)S(1)}, bf16[32,128]{1,0:T(8,128)(2,1)S(1)}, u32[]{:S(2)}, u32[]{:S(2)}) collective-permute-start(bf16[32,128]{1,0:T(8,128)(2,1)S(1)} %shard_map.48), channel_id=1, source_target_pairs={{0,1},{1,0},{2,3},{3,2},{4,5},{5,4},{6,7},{7,6},{8,9},{9,8},{10,11... | collective-permute-start | bytes 24584 | tf_op jit(solution)/shard_map/ppermute | solution.py:284
  4.8 7.1 %collective-permute-start.1 = (bf16[32,128]{1,0:T(8,128)(2,1)S(1)}, bf16[32,128]{1,0:T(8,128)(2,1)S(1)}, u32[]{:S(2)}, u32[]{:S(2)}) collective-permute-start(bf16[32,128]{1,0:T(8,128)(2,1)S(1)} %shard_map.48), channel_id=1, source_target_pairs={{0,2},{1,3},{2,0},{3,1},{4,6},{5,7},{6,4},{7,5},{8,10},{9,11},{10,... | collective-permute-start | bytes 24584 | tf_op jit(solution)/shard_map/ppermute | solution.py:284
  6.3 5.5 %collective-permute-start.2 = (bf16[32,128]{1,0:T(8,128)(2,1)S(1)}, bf16[32,128]{1,0:T(8,128)(2,1)S(1)}, u32[]{:S(2)}, u32[]{:S(2)}) collective-permute-start(bf16[32,128]{1,0:T(8,128)(2,1)S(1)} %shard_map.48), channel_id=1, source_target_pairs={{0,3},{1,2},{2,1},{3,0},{4,7},{5,6},{6,5},{7,4},{8,11},{9,10},{10,... | collective-permute-start | bytes 24584 | tf_op jit(solution)/shard_map/ppermute | solution.py:284
  6.6 20.0 %collective-permute-start.10 = (bf16[64,4096]{1,0:T(8,128)(2,1)S(1)}, bf16[64,4096]{1,0:T(8,128)(2,1)S(1)}, u32[]{:S(2)}, u32[]{:S(2)}) collective-permute-start(bf16[64,4096]{1,0:T(8,128)(2,1)S(1)} %bitcast.44), channel_id=1, source_target_pairs={{12,8},{13,9},{14,10},{15,11},{16,12},{17,13},{18,14},{19,15},{20,... | collective-permute-start | bytes 1572872 | tf_op jit(solution)/shard_map/ppermute | solution.py:284
  9.9 1.9 %copy-start = (bf16[1,4,64,4096]{3,2,1,0:T(8,128)(2,1)S(1)}, bf16[1,4,64,4096]{3,2,1,0:T(8,128)(2,1)}, u32[]{:S(2)}) copy-start(bf16[1,4,64,4096]{3,2,1,0:T(8,128)(2,1)} %param.7) | copy-start | bytes 6291460
  12.3 6.2 %collective-permute-start.3 = (bf16[32,4096]{1,0:T(8,128)(2,1)S(1)}, bf16[32,4096]{1,0:T(8,128)(2,1)S(1)}, u32[]{:S(2)}, u32[]{:S(2)}) collective-permute-start(bf16[32,4096]{1,0:T(8,128)(2,1)S(1)} %get-tuple-element.87.refs_1_), channel_id=1, source_target_pairs={{0,4},{1,5},{2,6},{3,7}} | collective-permute-start | bytes 786440 | tf_op jit(solution)/shard_map/ppermute | solution.py:284
  16.8 2.7 %collective-permute-start.5 = (bf16[32,128]{1,0:T(8,128)(2,1)S(1)}, bf16[32,128]{1,0:T(8,128)(2,1)S(1)}, u32[]{:S(2)}, u32[]{:S(2)}) collective-permute-start(bf16[32,128]{1,0:T(8,128)(2,1)S(1)} %shard_map.50.other_ref.refs_0_.refs_2_), channel_id=1, source_target_pairs={{0,6},{1,7},{2,4},{3,5}} | collective-permute-start | bytes 24584 | tf_op jit(solution)/shard_map/ppermute | solution.py:284
  17.8 4.7 %collective-permute-start.8 = (bf16[64,4096]{1,0:T(8,128)(2,1)S(1)}, bf16[64,4096]{1,0:T(8,128)(2,1)S(1)}, u32[]{:S(2)}, u32[]{:S(2)}) collective-permute-start(bf16[64,4096]{1,0:T(8,128)(2,1)S(1)} %get-tuple-element.101), channel_id=1, source_target_pairs={{8,4},{9,5},{10,6},{11,7}} | collective-permute-start | bytes 1572872 | tf_op jit(solution)/shard_map/ppermute | solution.py:284
  19.8 1.6 %collective-permute-start.6 = (bf16[32,128]{1,0:T(8,128)(2,1)S(1)}, bf16[32,128]{1,0:T(8,128)(2,1)S(1)}, u32[]{:S(2)}, u32[]{:S(2)}) collective-permute-start(bf16[32,128]{1,0:T(8,128)(2,1)S(1)} %shard_map.53.refs_0_), channel_id=1, source_target_pairs={{4,5},{5,4},{6,7},{7,6}} | collective-permute-start | bytes 24584 | tf_op jit(solution)/shard_map/ppermute | solution.py:284
  21.8 5.2 %collective-permute-start.7 = (bf16[32,4096]{1,0:T(8,128)(2,1)S(1)}, bf16[32,4096]{1,0:T(8,128)(2,1)S(1)}, u32[]{:S(2)}, u32[]{:S(2)}) collective-permute-start(bf16[32,4096]{1,0:T(8,128)(2,1)S(1)} %get-tuple-element.96.refs_1_), channel_id=1, source_target_pairs={{4,8},{5,9},{6,10},{7,11}} | collective-permute-start | bytes 786440 | tf_op jit(solution)/shard_map/ppermute | solution.py:284
  22.7 5.1 %collective-permute-start.9 = (bf16[32,128]{1,0:T(8,128)(2,1)S(1)}, bf16[32,128]{1,0:T(8,128)(2,1)S(1)}, u32[]{:S(2)}, u32[]{:S(2)}) collective-permute-start(bf16[32,128]{1,0:T(8,128)(2,1)S(1)} %shard_map.57), channel_id=1, source_target_pairs={{4,10},{5,11},{6,8},{7,9}} | collective-permute-start | bytes 24584 | tf_op jit(solution)/shard_map/ppermute | solution.py:284
  28.2 1.6 %collective-permute-start.11 = (bf16[32,128]{1,0:T(8,128)(2,1)S(1)}, bf16[32,128]{1,0:T(8,128)(2,1)S(1)}, u32[]{:S(2)}, u32[]{:S(2)}) collective-permute-start(bf16[32,128]{1,0:T(8,128)(2,1)S(1)} %shard_map.59.refs_0_), channel_id=1, source_target_pairs={{8,9},{9,8},{10,11},{11,10}} | collective-permute-start | bytes 24584 | tf_op jit(solution)/shard_map/ppermute | solution.py:284
  30.1 3.9 %collective-permute-start.12 = (bf16[32,2048]{1,0:T(8,128)(2,1)S(1)}, bf16[32,2048]{1,0:T(8,128)(2,1)S(1)}, u32[]{:S(2)}, u32[]{:S(2)}) collective-permute-start(bf16[32,2048]{1,0:T(8,128)(2,1)S(1)} %get-tuple-element.104.refs_0_), channel_id=1, source_target_pairs={{8,12},{9,13},{10,14},{11,15}} | collective-permute-start | bytes 393224 | tf_op jit(solution)/shard_map/ppermute | solution.py:284
  31.0 3.9 %collective-permute-start.13 = (bf16[32,2048]{1,0:T(8,128)(2,1)S(1)}, bf16[32,2048]{1,0:T(8,128)(2,1)S(1)}, u32[]{:S(2)}, u32[]{:S(2)}) collective-permute-start(bf16[32,2048]{1,0:T(8,128)(2,1)S(1)} %get-tuple-element.110.refs_1_), channel_id=1, source_target_pairs={{8,12},{9,13},{10,14},{11,15}} | collective-permute-start | bytes 393224 | tf_op jit(solution)/shard_map/ppermute | solution.py:284
  32.0 3.9 %collective-permute-start.14 = (bf16[32,128]{1,0:T(8,128)(2,1)S(1)}, bf16[32,128]{1,0:T(8,128)(2,1)S(1)}, u32[]{:S(2)}, u32[]{:S(2)}) collective-permute-start(bf16[32,128]{1,0:T(8,128)(2,1)S(1)} %shard_map.65), channel_id=1, source_target_pairs={{8,15},{9,14},{10,13},{11,12}} | collective-permute-start | bytes 24584 | tf_op jit(solution)/shard_map/ppermute | solution.py:284
  32.6 3.2 %collective-permute-start.15 = (bf16[32,128]{1,0:T(8,128)(2,1)S(1)}, bf16[32,128]{1,0:T(8,128)(2,1)S(1)}, u32[]{:S(2)}, u32[]{:S(2)}) collective-permute-start(bf16[32,128]{1,0:T(8,128)(2,1)S(1)} %shard_map.65), channel_id=1, source_target_pairs={{8,13},{9,12},{10,15},{11,14}} | collective-permute-start | bytes 24584 | tf_op jit(solution)/shard_map/ppermute | solution.py:284
  33.3 2.6 %collective-permute-start.16 = (bf16[32,128]{1,0:T(8,128)(2,1)S(1)}, bf16[32,128]{1,0:T(8,128)(2,1)S(1)}, u32[]{:S(2)}, u32[]{:S(2)}) collective-permute-start(bf16[32,128]{1,0:T(8,128)(2,1)S(1)} %shard_map.65), channel_id=1, source_target_pairs={{8,14},{9,15},{10,12},{11,13}} | collective-permute-start | bytes 24584 | tf_op jit(solution)/shard_map/ppermute | solution.py:284
  36.3 3.0 %collective-permute-start.17 = (bf16[32,4096]{1,0:T(8,128)(2,1)S(1)}, bf16[32,4096]{1,0:T(8,128)(2,1)S(1)}, u32[]{:S(2)}, u32[]{:S(2)}) collective-permute-start(bf16[32,4096]{1,0:T(8,128)(2,1)S(1)} %get-tuple-element.115.refs_0_), channel_id=1, source_target_pairs={{12,16},{13,17},{14,18},{15,19}} | collective-permute-start | bytes 786440 | tf_op jit(solution)/shard_map/ppermute | solution.py:284
  37.3 3.9 %collective-permute-start.18 = (bf16[32,128]{1,0:T(8,128)(2,1)S(1)}, bf16[32,128]{1,0:T(8,128)(2,1)S(1)}, u32[]{:S(2)}, u32[]{:S(2)}) collective-permute-start(bf16[32,128]{1,0:T(8,128)(2,1)S(1)} %shard_map.69), channel_id=1, source_target_pairs={{12,19},{13,18},{14,17},{15,16}} | collective-permute-start | bytes 24584 | tf_op jit(solution)/shard_map/ppermute | solution.py:284
  37.9 3.2 %collective-permute-start.19 = (bf16[32,128]{1,0:T(8,128)(2,1)S(1)}, bf16[32,128]{1,0:T(8,128)(2,1)S(1)}, u32[]{:S(2)}, u32[]{:S(2)}) collective-permute-start(bf16[32,128]{1,0:T(8,128)(2,1)S(1)} %shard_map.69), channel_id=1, source_target_pairs={{12,17},{13,16},{14,19},{15,18}} | collective-permute-start | bytes 24584 | tf_op jit(solution)/shard_map/ppermute | solution.py:284
  38.6 2.6 %collective-permute-start.20 = (bf16[32,128]{1,0:T(8,128)(2,1)S(1)}, bf16[32,128]{1,0:T(8,128)(2,1)S(1)}, u32[]{:S(2)}, u32[]{:S(2)}) collective-permute-start(bf16[32,128]{1,0:T(8,128)(2,1)S(1)} %shard_map.69), channel_id=1, source_target_pairs={{12,18},{13,19},{14,16},{15,17}} | collective-permute-start | bytes 24584 | tf_op jit(solution)/shard_map/ppermute | solution.py:284
  41.4 4.1 %collective-permute-start.21 = (bf16[32,2048]{1,0:T(8,128)(2,1)S(1)}, bf16[32,2048]{1,0:T(8,128)(2,1)S(1)}, u32[]{:S(2)}, u32[]{:S(2)}) collective-permute-start(bf16[32,2048]{1,0:T(8,128)(2,1)S(1)} %get-tuple-element.122.refs_0_), channel_id=1, source_target_pairs={{16,20},{17,21},{18,22},{19,23}} | collective-permute-start | bytes 393224 | tf_op jit(solution)/shard_map/ppermute | solution.py:284
  42.4 4.1 %collective-permute-start.22 = (bf16[32,2048]{1,0:T(8,128)(2,1)S(1)}, bf16[32,2048]{1,0:T(8,128)(2,1)S(1)}, u32[]{:S(2)}, u32[]{:S(2)}) collective-permute-start(bf16[32,2048]{1,0:T(8,128)(2,1)S(1)} %get-tuple-element.129.refs_1_), channel_id=1, source_target_pairs={{16,20},{17,21},{18,22},{19,23}} | collective-permute-start | bytes 393224 | tf_op jit(solution)/shard_map/ppermute | solution.py:284
  43.5 3.9 %collective-permute-start.23 = (bf16[32,128]{1,0:T(8,128)(2,1)S(1)}, bf16[32,128]{1,0:T(8,128)(2,1)S(1)}, u32[]{:S(2)}, u32[]{:S(2)}) collective-permute-start(bf16[32,128]{1,0:T(8,128)(2,1)S(1)} %shard_map.74), channel_id=1, source_target_pairs={{16,23},{17,22},{18,21},{19,20}} | collective-permute-start | bytes 24584 | tf_op jit(solution)/shard_map/ppermute | solution.py:284
  44.2 3.2 %collective-permute-start.24 = (bf16[32,128]{1,0:T(8,128)(2,1)S(1)}, bf16[32,128]{1,0:T(8,128)(2,1)S(1)}, u32[]{:S(2)}, u32[]{:S(2)}) collective-permute-start(bf16[32,128]{1,0:T(8,128)(2,1)S(1)} %shard_map.74), channel_id=1, source_target_pairs={{16,21},{17,20},{18,23},{19,22}} | collective-permute-start | bytes 24584 | tf_op jit(solution)/shard_map/ppermute | solution.py:284
  44.9 2.6 %collective-permute-start.25 = (bf16[32,128]{1,0:T(8,128)(2,1)S(1)}, bf16[32,128]{1,0:T(8,128)(2,1)S(1)}, u32[]{:S(2)}, u32[]{:S(2)}) collective-permute-start(bf16[32,128]{1,0:T(8,128)(2,1)S(1)} %shard_map.74), channel_id=1, source_target_pairs={{16,22},{17,23},{18,20},{19,21}} | collective-permute-start | bytes 24584 | tf_op jit(solution)/shard_map/ppermute | solution.py:284
  47.7 3.9 %collective-permute-start.26 = (bf16[32,2048]{1,0:T(8,128)(2,1)S(1)}, bf16[32,2048]{1,0:T(8,128)(2,1)S(1)}, u32[]{:S(2)}, u32[]{:S(2)}) collective-permute-start(bf16[32,2048]{1,0:T(8,128)(2,1)S(1)} %get-tuple-element.132.refs_0_), channel_id=1, source_target_pairs={{20,24},{21,25},{22,26},{23,27}} | collective-permute-start | bytes 393224 | tf_op jit(solution)/shard_map/ppermute | solution.py:284
  48.7 3.9 %collective-permute-start.27 = (bf16[32,2048]{1,0:T(8,128)(2,1)S(1)}, bf16[32,2048]{1,0:T(8,128)(2,1)S(1)}, u32[]{:S(2)}, u32[]{:S(2)}) collective-permute-start(bf16[32,2048]{1,0:T(8,128)(2,1)S(1)} %get-tuple-element.139.refs_1_), channel_id=1, source_target_pairs={{20,24},{21,25},{22,26},{23,27}} | collective-permute-start | bytes 393224 | tf_op jit(solution)/shard_map/ppermute | solution.py:284
  49.6 3.9 %collective-permute-start.28 = (bf16[32,128]{1,0:T(8,128)(2,1)S(1)}, bf16[32,128]{1,0:T(8,128)(2,1)S(1)}, u32[]{:S(2)}, u32[]{:S(2)}) collective-permute-start(bf16[32,128]{1,0:T(8,128)(2,1)S(1)} %shard_map.79), channel_id=1, source_target_pairs={{20,27},{21,26},{22,25},{23,24}} | collective-permute-start | bytes 24584 | tf_op jit(solution)/shard_map/ppermute | solution.py:284
  50.3 3.2 %collective-permute-start.29 = (bf16[32,128]{1,0:T(8,128)(2,1)S(1)}, bf16[32,128]{1,0:T(8,128)(2,1)S(1)}, u32[]{:S(2)}, u32[]{:S(2)}) collective-permute-start(bf16[32,128]{1,0:T(8,128)(2,1)S(1)} %shard_map.79), channel_id=1, source_target_pairs={{20,25},{21,24},{22,27},{23,26}} | collective-permute-start | bytes 24584 | tf_op jit(solution)/shard_map/ppermute | solution.py:284
  51.0 2.6 %collective-permute-start.30 = (bf16[32,128]{1,0:T(8,128)(2,1)S(1)}, bf16[32,128]{1,0:T(8,128)(2,1)S(1)}, u32[]{:S(2)}, u32[]{:S(2)}) collective-permute-start(bf16[32,128]{1,0:T(8,128)(2,1)S(1)} %shard_map.79), channel_id=1, source_target_pairs={{20,26},{21,27},{22,24},{23,25}} | collective-permute-start | bytes 24584 | tf_op jit(solution)/shard_map/ppermute | solution.py:284
  53.8 36.2 %collective-permute-start.31 = (bf16[32,2048]{1,0:T(8,128)(2,1)S(1)}, bf16[32,2048]{1,0:T(8,128)(2,1)S(1)}, u32[]{:S(2)}, u32[]{:S(2)}) collective-permute-start(bf16[32,2048]{1,0:T(8,128)(2,1)S(1)} %get-tuple-element.142.refs_0_), channel_id=1, source_target_pairs={{24,28},{25,29},{26,30},{27,31}} | collective-permute-start | bytes 393224 | tf_op jit(solution)/shard_map/ppermute | solution.py:284
  55.4 36.2 %collective-permute-start.32 = (bf16[32,2048]{1,0:T(8,128)(2,1)S(1)}, bf16[32,2048]{1,0:T(8,128)(2,1)S(1)}, u32[]{:S(2)}, u32[]{:S(2)}) collective-permute-start(bf16[32,2048]{1,0:T(8,128)(2,1)S(1)} %get-tuple-element.147.refs_1_), channel_id=1, source_target_pairs={{24,28},{25,29},{26,30},{27,31}} | collective-permute-start | bytes 393224 | tf_op jit(solution)/shard_map/ppermute | solution.py:284
  57.0 35.5 %collective-permute-start.33 = (bf16[32,128]{1,0:T(8,128)(2,1)S(1)}, bf16[32,128]{1,0:T(8,128)(2,1)S(1)}, u32[]{:S(2)}, u32[]{:S(2)}) collective-permute-start(bf16[32,128]{1,0:T(8,128)(2,1)S(1)} %shard_map.84), channel_id=1, source_target_pairs={{24,31},{25,30},{26,29},{27,28}} | collective-permute-start | bytes 24584 | tf_op jit(solution)/shard_map/ppermute | solution.py:284
  58.3 34.2 %collective-permute-start.34 = (bf16[32,128]{1,0:T(8,128)(2,1)S(1)}, bf16[32,128]{1,0:T(8,128)(2,1)S(1)}, u32[]{:S(2)}, u32[]{:S(2)}) collective-permute-start(bf16[32,128]{1,0:T(8,128)(2,1)S(1)} %shard_map.84), channel_id=1, source_target_pairs={{24,29},{25,28},{26,31},{27,30}} | collective-permute-start | bytes 24584 | tf_op jit(solution)/shard_map/ppermute | solution.py:284
  59.6 34.9 %collective-permute-start.35 = (bf16[32,128]{1,0:T(8,128)(2,1)S(1)}, bf16[32,128]{1,0:T(8,128)(2,1)S(1)}, u32[]{:S(2)}, u32[]{:S(2)}) collective-permute-start(bf16[32,128]{1,0:T(8,128)(2,1)S(1)} %shard_map.84), channel_id=1, source_target_pairs={{24,30},{25,31},{26,28},{27,29}} | collective-permute-start | bytes 24584 | tf_op jit(solution)/shard_map/ppermute | solution.py:284

commit v4 on v1

--- a/solution.py
+++ b/solution.py
@@ -208,13 +208,15 @@
     return call(functools.partial(near_kernel, span, start), outs, [w, front, leaf, near_v, *behind], {0: 0})
 
 
-def far_kernel(rank, size, spans, chosen, levels_of, *refs):
+def far_kernel(rank, size, spans, chosen, levels_of, sends, *refs):
     refs = list(refs)
+    p_out = refs.pop() if sends else None
     sum_refs = [refs.pop(0) for _ in chosen]
     p_refs = [refs.pop(0) for _ in spans]
     q_ref = refs.pop(0)
     part_refs = [refs.pop(0) for _ in levels_of]
     u_ref = refs.pop(0)
+    next_ref, earlier_ref = (refs.pop(0), refs.pop(0)) if sends else (None, None)
     out_ref, q_out = refs[:2]
     rows, far = q_ref.shape
     near = u_ref.shape[0] - far
@@ -250,14 +252,19 @@
             value = value + dot(swapped.astype(jnp.bfloat16), u_ref[far:, columns])
             out_ref[:, place : place + size] = value.astype(jnp.bfloat16)
             place += size
-
-
-def far_part(rank, size, spans, chosen, sums, projected, q, parts, levels_of, u, last):
-    args = [*[sums[i] for i in chosen], *projected, q, *parts, u]
+    if sends:
+        before = earlier_ref.shape[1]
+        total = dot(earlier_ref[...], next_ref[:before, :]) + dot(out_ref[...], next_ref[before:, :])
+        p_out[...] = total.astype(p_out.dtype)
+
+
+def far_part(rank, size, spans, chosen, sums, projected, q, parts, levels_of, u, last, sends=()):
+    args = [*[sums[i] for i in chosen], *projected, q, *parts, u, *sends]
     width = sum(sums[i].shape[1] for i in chosen)
     space = jax.ShapeDtypeStruct if last else pltpu.VMEM
     outs = [space((q.shape[0], width), jnp.bfloat16), pltpu.VMEM(q.shape, jnp.float32)]
-    kernel = functools.partial(far_kernel, rank, size, spans, chosen, tuple(levels_of) if parts else ())
+    outs += [pltpu.VMEM((q.shape[0], sends[0].shape[1]), jnp.bfloat16)] if sends else []
+    kernel = functools.partial(far_kernel, rank, size, spans, chosen, tuple(levels_of) if parts else (), len(sends) > 0)
     return call(kernel, outs, args, {len(chosen) + len(projected): 1})
 
 
@@ -329,13 +336,14 @@
         split = k >= IN_PLACE and k != WHOLE_HOP
         outs, front = [], []
         for chosen in [(i,) for i in every] if split else [every]:
-            out, q = far(chosen, sums, projected, q, [] if front else parts, levels_now, u, False)
+            sends = [turned, outs[0]] if outs else []
+            out, q, *p = far(chosen, sums, projected, q, [] if front else parts, levels_now, u, False, sends)
             outs.append(out)
             front.append(moved(out, [(k, k + 1)]))
         if k < IN_PLACE:
             p = project(whole, outs, [second], ranks)
         else:
-            p = project_turned(spans if split else whole, outs, turned)
+            p = p[0] if split else project_turned(whole, outs, turned)
         sent = relayed if k < IN_PLACE else offsets[::-1]
         parts = [moved(p, [(k, k + 1)], x) for x in sent]
 

time: 94.3 us -> 94.1 us (level)
    pallas_call x40 -> x36, Pallas kernels: 24 us -> 23.8 us  [call(): pl.pallas_call(kernel, out_shape=outs, in_specs=[remote if i in from_hbm...]
where the time goes in v4:
time: 94.1 us; the launch traced here: 93.5 us
  waiting for transfers between devices  37.1 us (39%)
  starting transfers between devices  31.8 us (34%)
  Pallas kernels  23.8 us (25%)
    ppermute x36, waiting for transfers between devices, moved(): return lax.ppermute(x, ('slab', 'hodlr'), route)  37.1 us
    ppermute x36, starting transfers between devices, moved(): return lax.ppermute(x, ('slab', 'hodlr'), route)  31.8 us
    pallas_call x36, Pallas kernels, call(): pl.pallas_call(kernel, out_shape=outs, in_specs=[remote if i in from_hbm...  23.8 us
  transfers between devices with their start and end apart: 36, of which 4 were waited for; matrix products, arithmetic and copies ran while one was open for 0% of the time, Pallas kernels for 21%

profile of v4, /device:TPU:26, one launch (start us, length us, event | category | flops | bytes accessed | tf_op | source)
XLA Modules:
  0.0 93.5 jit_solution(9001619060163648215)
XLA Ops:
  0.0 1.6 %shard_map.46 = (bf16[1,64,4096]{2,1,0:T(8,128)(2,1)S(1)}, bf16[1,64,4096]{2,1,0:T(8,128)(2,1)S(1)}, bf16[1,64,4096]{2,1,0:T(8,128)(2,1)S(1)}, bf16[32,2048]{1,0:T(8,128)(2,1)S(1)}, bf16[32,2048]{1,0:T(8,128)(2,1)S(1)}) custom-call(bf16[32,4096]{1,0:T(8,128)(2,1)} %bitcast.46, bf16[4,64,4096]{2,1,0:T(8,128)(2,1)} %bitcast.37), custom_call_target="tpu_custom_call" | custom-call | tf_op jit(solution)/shard_map/pallas_call | solution.py:30
  1.6 2.6 %collective-permute-start.4 = (bf16[64,4096]{1,0:T(8,128)(2,1)S(1)}, bf16[64,4096]{1,0:T(8,128)(2,1)S(1)}, u32[]{:S(2)}, u32[]{:S(2)}) collective-permute-start(bf16[64,4096]{1,0:T(8,128)(2,1)S(1)} %bitcast.45), channel_id=1, source_target_pairs={{4,0},{5,1},{6,2},{7,3},{12,8},{13,9},{14,10},{15,11},{16,12},{17,... | collective-permute-start | bytes 1572872 | tf_op jit(solution)/shard_map/ppermute | solution.py:285
  4.3 0.4 shard_map.48
  4.8 1.6 %collective-permute-start.1 = (bf16[32,128]{1,0:T(8,128)(2,1)S(1)}, bf16[32,128]{1,0:T(8,128)(2,1)S(1)}, u32[]{:S(2)}, u32[]{:S(2)}) collective-permute-start(bf16[32,128]{1,0:T(8,128)(2,1)S(1)} %shard_map.48), channel_id=1, source_target_pairs={{0,2},{1,3},{2,0},{3,1},{4,6},{5,7},{6,4},{7,5},{8,10},{9,11},{10,... | collective-permute-start | bytes 24584 | tf_op jit(solution)/shard_map/ppermute | solution.py:285
  6.6 3.3 %collective-permute-start.10 = (bf16[64,4096]{1,0:T(8,128)(2,1)S(1)}, bf16[64,4096]{1,0:T(8,128)(2,1)S(1)}, u32[]{:S(2)}, u32[]{:S(2)}) collective-permute-start(bf16[64,4096]{1,0:T(8,128)(2,1)S(1)} %bitcast.43), channel_id=1, source_target_pairs={{12,8},{13,9},{14,10},{15,11},{16,12},{17,13},{18,14},{19,15},{20,... | collective-permute-start | bytes 1572872 | tf_op jit(solution)/shard_map/ppermute | solution.py:285
  10.0 1.8 %shard_map.47 = (bf16[2,1024,256]{2,1,0:T(8,128)(2,1)S(1)}, f32[32,2048]{1,0:T(8,128)S(1)}, f32[32,2048]{1,0:T(8,128)S(1)}, f32[2,32,128]{2,1,0:T(8,128)S(1)}, f32[2,32,128]{2,1,0:T(8,128)S(1)}) custom-call(bf16[32,2048]{1,0:T(8,128)(2,1)S(1)} %get-tuple-element.82.refs_0_.refs_2_.w_ref, bf16[32,2048]{1,0:T(8,128)(2,1)S(1)} %get-tuple-element.83.refs_1_.refs_3_.w_ref, ...), custom_call_target="tpu_custom_call" | custom-call | tf_op jit(solution)/shard_map/pallas_call | solution.py:30
  11.8 0.4 shard_map.49
  12.2 0.7 collective-permute-start.3
  12.9 3.6 %collective-permute-done.4.refs_0_.refs_1_ = bf16[64,4096]{1,0:T(8,128)(2,1)S(1)} collective-permute-done((bf16[64,4096]{1,0:T(8,128)(2,1)S(1)}, bf16[64,4096]{1,0:T(8,128)(2,1)S(1)}, u32[]{:S(2)}, u32[]{:S(2)}) %collective-permute-start.4) | collective-permute-done | bytes 524320 | tf_op jit(solution)/shard_map/ppermute | solution.py:285
  16.8 0.7 collective-permute-start.5
  17.5 0.7 collective-permute-start.8
  18.2 0.9 shard_map.51
  19.1 0.3 shard_map.52.refs_0_
  19.5 0.7 collective-permute-start.6
  20.1 0.9 shard_map.53
  21.1 0.4 shard_map.54
  21.5 0.7 collective-permute-start.7
  22.4 0.7 collective-permute-start.9
  23.1 3.5 %collective-permute-done.10.refs_0_ = bf16[64,4096]{1,0:T(8,128)(2,1)S(1)} collective-permute-done((bf16[64,4096]{1,0:T(8,128)(2,1)S(1)}, bf16[64,4096]{1,0:T(8,128)(2,1)S(1)}, u32[]{:S(2)}, u32[]{:S(2)}) %collective-permute-start.10) | collective-permute-done | bytes 524320 | tf_op jit(solution)/shard_map/ppermute | solution.py:285
  26.9 0.9 shard_map.55
  28.2 0.7 collective-permute-start.11
  28.9 0.9 shard_map.60
  30.1 0.7 collective-permute-start.12
  30.7 0.5 shard_map.63
  31.2 0.7 collective-permute-start.13
  31.9 0.7 collective-permute-start.14
  32.6 0.7 collective-permute-start.15
  33.2 0.7 collective-permute-start.16
  33.9 0.9 shard_map.62
  34.8 0.9 shard_map.64
  35.8 0.4 shard_map.65
  36.2 0.7 collective-permute-start.17
  37.2 0.7 collective-permute-start.18
  37.8 0.7 collective-permute-start.19
  38.5 0.7 collective-permute-start.20
  39.2 0.9 shard_map.66
  40.1 0.9 shard_map.67
  41.3 0.7 collective-permute-start.21
  42.0 0.5 shard_map.71
  42.5 0.7 collective-permute-start.22
  43.2 0.7 collective-permute-start.23
  43.8 0.7 collective-permute-start.24
  44.5 0.8 collective-permute-start.25
  45.4 0.9 shard_map.70
  46.3 0.9 shard_map.72
  47.5 0.7 collective-permute-start.26
  48.2 0.5 shard_map.75
  48.7 0.7 collective-permute-start.27
  49.4 0.7 collective-permute-start.28
  50.0 0.7 collective-permute-start.29
  50.7 0.7 collective-permute-start.30
  51.4 0.9 shard_map.74
  52.3 0.9 shard_map.76
  53.5 1.3 %collective-permute-start.31 = (bf16[32,2048]{1,0:T(8,128)(2,1)S(1)}, bf16[32,2048]{1,0:T(8,128)(2,1)S(1)}, u32[]{:S(2)}, u32[]{:S(2)}) collective-permute-start(bf16[32,2048]{1,0:T(8,128)(2,1)S(1)} %get-tuple-element.147.refs_6_), channel_id=1, source_target_pairs={{24,28},{25,29},{26,30},{27,31}} | collective-permute-start | bytes 393224 | tf_op jit(solution)/shard_map/ppermute | solution.py:285
  54.8 0.5 shard_map.79
  55.3 1.3 %collective-permute-start.32 = (bf16[32,2048]{1,0:T(8,128)(2,1)S(1)}, bf16[32,2048]{1,0:T(8,128)(2,1)S(1)}, u32[]{:S(2)}, u32[]{:S(2)}) collective-permute-start(bf16[32,2048]{1,0:T(8,128)(2,1)S(1)} %get-tuple-element.152), channel_id=1, source_target_pairs={{24,28},{25,29},{26,30},{27,31}} | collective-permute-start | bytes 393224 | tf_op jit(solution)/shard_map/ppermute | solution.py:285
  56.6 1.3 %collective-permute-start.33 = (bf16[32,128]{1,0:T(8,128)(2,1)S(1)}, bf16[32,128]{1,0:T(8,128)(2,1)S(1)}, u32[]{:S(2)}, u32[]{:S(2)}) collective-permute-start(bf16[32,128]{1,0:T(8,128)(2,1)S(1)} %get-tuple-element.157), channel_id=1, source_target_pairs={{24,31},{25,30},{26,29},{27,28}} | collective-permute-start | bytes 24584 | tf_op jit(solution)/shard_map/ppermute | solution.py:285
  57.9 1.3 %collective-permute-start.34 = (bf16[32,128]{1,0:T(8,128)(2,1)S(1)}, bf16[32,128]{1,0:T(8,128)(2,1)S(1)}, u32[]{:S(2)}, u32[]{:S(2)}) collective-permute-start(bf16[32,128]{1,0:T(8,128)(2,1)S(1)} %get-tuple-element.157), channel_id=1, source_target_pairs={{24,30},{25,31},{26,28},{27,29}} | collective-permute-start | bytes 24584 | tf_op jit(solution)/shard_map/ppermute | solution.py:285
  59.2 1.3 %collective-permute-start.35 = (bf16[32,128]{1,0:T(8,128)(2,1)S(1)}, bf16[32,128]{1,0:T(8,128)(2,1)S(1)}, u32[]{:S(2)}, u32[]{:S(2)}) collective-permute-start(bf16[32,128]{1,0:T(8,128)(2,1)S(1)} %get-tuple-element.157), channel_id=1, source_target_pairs={{24,29},{25,28},{26,31},{27,30}} | collective-permute-start | bytes 24584 | tf_op jit(solution)/shard_map/ppermute | solution.py:285
  60.5 28.9 %collective-permute-done.31.front_ref = bf16[32,2048]{1,0:T(8,128)(2,1)S(1)} collective-permute-done((bf16[32,2048]{1,0:T(8,128)(2,1)S(1)}, bf16[32,2048]{1,0:T(8,128)(2,1)S(1)}, u32[]{:S(2)}, u32[]{:S(2)}) %collective-permute-start.31) | collective-permute-done | bytes 131104 | tf_op jit(solution)/shard_map/ppermute | solution.py:285
  89.4 0.9 shard_map.78
  90.3 1.1 %collective-permute-done.32.front_ref = bf16[32,2048]{1,0:T(8,128)(2,1)S(1)} collective-permute-done((bf16[32,2048]{1,0:T(8,128)(2,1)S(1)}, bf16[32,2048]{1,0:T(8,128)(2,1)S(1)}, u32[]{:S(2)}, u32[]{:S(2)}) %collective-permute-start.32) | collective-permute-done | bytes 131104 | tf_op jit(solution)/shard_map/ppermute | solution.py:285
  91.4 0.9 shard_map.80
  92.3 1.1 %shard_map.81 = (bf16[32,4096]{1,0:T(8,128)(2,1)}, f32[32,128]{1,0:T(8,128)S(1)}) custom-call(f32[32,2048]{1,0:T(8,128)S(1)} %get-tuple-element.148.refs_0_, f32[32,2048]{1,0:T(8,128)S(1)} %get-tuple-element.154.refs_1_, f32[2,32,128]{2,1,0:T(8,128)S(1)} %get-tuple-element.153.refs_0_.refs_2_, ...), custom_call_target="tpu_custom_call", output_to_operand_aliasing={{1}: (4, {})} | custom-call | tf_op jit(solution)/shard_map/pallas_call | solution.py:30
  (54 shorter events, 3.0 us)
Async XLA Ops:
  0.0 9.9 %slice-start = ((s8[8388608]{0:T(1024)(128)(4,1)}), s8[4194304]{0:T(1024)(128)(4,1)S(1)}, s32[]{:S(2)}) async-start(s8[8388608]{0:T(1024)(128)(4,1)} %bitcast.8), calls=%async_computation | async-start | bytes 8388608
  1.6 14.9 %collective-permute-start.4 = (bf16[64,4096]{1,0:T(8,128)(2,1)S(1)}, bf16[64,4096]{1,0:T(8,128)(2,1)S(1)}, u32[]{:S(2)}, u32[]{:S(2)}) collective-permute-start(bf16[64,4096]{1,0:T(8,128)(2,1)S(1)} %bitcast.45), channel_id=1, source_target_pairs={{4,0},{5,1},{6,2},{7,3},{12,8},{13,9},{14,10},{15,11},{16,12},{17,... | collective-permute-start | bytes 1572872 | tf_op jit(solution)/shard_map/ppermute | solution.py:285
  4.2 5.7 %slice-start.1 = ((s8[8388608]{0:T(1024)(128)(4,1)}), s8[4194304]{0:T(1024)(128)(4,1)S(1)}, s32[]{:S(2)}) async-start(s8[8388608]{0:T(1024)(128)(4,1)} %bitcast.8), calls=%async_computation.1 | async-start | bytes 8388608
  4.2 5.7 %copy-start.1 = (bf16[1,4,64,4096]{3,2,1,0:T(8,128)(2,1)S(1)}, bf16[1,4,64,4096]{3,2,1,0:T(8,128)(2,1)}, u32[]{:S(2)}) copy-start(bf16[1,4,64,4096]{3,2,1,0:T(8,128)(2,1)} %param.6) | copy-start | bytes 6291460
  4.7 7.1 %collective-permute-start = (bf16[32,128]{1,0:T(8,128)(2,1)S(1)}, bf16[32,128]{1,0:T(8,128)(2,1)S(1)}, u32[]{:S(2)}, u32[]{:S(2)}) collective-permute-start(bf16[32,128]{1,0:T(8,128)(2,1)S(1)} %shard_map.48), channel_id=1, source_target_pairs={{0,1},{1,0},{2,3},{3,2},{4,5},{5,4},{6,7},{7,6},{8,9},{9,8},{10,11... | collective-permute-start | bytes 24584 | tf_op jit(solution)/shard_map/ppermute | solution.py:285
  4.8 7.0 %collective-permute-start.1 = (bf16[32,128]{1,0:T(8,128)(2,1)S(1)}, bf16[32,128]{1,0:T(8,128)(2,1)S(1)}, u32[]{:S(2)}, u32[]{:S(2)}) collective-permute-start(bf16[32,128]{1,0:T(8,128)(2,1)S(1)} %shard_map.48), channel_id=1, source_target_pairs={{0,2},{1,3},{2,0},{3,1},{4,6},{5,7},{6,4},{7,5},{8,10},{9,11},{10,... | collective-permute-start | bytes 24584 | tf_op jit(solution)/shard_map/ppermute | solution.py:285
  6.3 5.4 %collective-permute-start.2 = (bf16[32,128]{1,0:T(8,128)(2,1)S(1)}, bf16[32,128]{1,0:T(8,128)(2,1)S(1)}, u32[]{:S(2)}, u32[]{:S(2)}) collective-permute-start(bf16[32,128]{1,0:T(8,128)(2,1)S(1)} %shard_map.48), channel_id=1, source_target_pairs={{0,3},{1,2},{2,1},{3,0},{4,7},{5,6},{6,5},{7,4},{8,11},{9,10},{10,... | collective-permute-start | bytes 24584 | tf_op jit(solution)/shard_map/ppermute | solution.py:285
  6.6 20.0 %collective-permute-start.10 = (bf16[64,4096]{1,0:T(8,128)(2,1)S(1)}, bf16[64,4096]{1,0:T(8,128)(2,1)S(1)}, u32[]{:S(2)}, u32[]{:S(2)}) collective-permute-start(bf16[64,4096]{1,0:T(8,128)(2,1)S(1)} %bitcast.43), channel_id=1, source_target_pairs={{12,8},{13,9},{14,10},{15,11},{16,12},{17,13},{18,14},{19,15},{20,... | collective-permute-start | bytes 1572872 | tf_op jit(solution)/shard_map/ppermute | solution.py:285
  9.9 1.9 %copy-start = (bf16[1,4,64,4096]{3,2,1,0:T(8,128)(2,1)S(1)}, bf16[1,4,64,4096]{3,2,1,0:T(8,128)(2,1)}, u32[]{:S(2)}) copy-start(bf16[1,4,64,4096]{3,2,1,0:T(8,128)(2,1)} %param.7) | copy-start | bytes 6291460
  12.2 5.9 %collective-permute-start.3 = (bf16[32,4096]{1,0:T(8,128)(2,1)S(1)}, bf16[32,4096]{1,0:T(8,128)(2,1)S(1)}, u32[]{:S(2)}, u32[]{:S(2)}) collective-permute-start(bf16[32,4096]{1,0:T(8,128)(2,1)S(1)} %get-tuple-element.90.refs_1_), channel_id=1, source_target_pairs={{0,4},{1,5},{2,6},{3,7}} | collective-permute-start | bytes 786440 | tf_op jit(solution)/shard_map/ppermute | solution.py:285
  16.8 2.3 %collective-permute-start.5 = (bf16[32,128]{1,0:T(8,128)(2,1)S(1)}, bf16[32,128]{1,0:T(8,128)(2,1)S(1)}, u32[]{:S(2)}, u32[]{:S(2)}) collective-permute-start(bf16[32,128]{1,0:T(8,128)(2,1)S(1)} %shard_map.50.refs_0_.refs_2_.other_ref), channel_id=1, source_target_pairs={{0,6},{1,7},{2,4},{3,5}} | collective-permute-start | bytes 24584 | tf_op jit(solution)/shard_map/ppermute | solution.py:285
  17.5 4.7 %collective-permute-start.8 = (bf16[64,4096]{1,0:T(8,128)(2,1)S(1)}, bf16[64,4096]{1,0:T(8,128)(2,1)S(1)}, u32[]{:S(2)}, u32[]{:S(2)}) collective-permute-start(bf16[64,4096]{1,0:T(8,128)(2,1)S(1)} %shard_map.56), channel_id=1, source_target_pairs={{8,4},{9,5},{10,6},{11,7}} | collective-permute-start | bytes 1572872 | tf_op jit(solution)/shard_map/ppermute | solution.py:285
  19.5 1.6 %collective-permute-start.6 = (bf16[32,128]{1,0:T(8,128)(2,1)S(1)}, bf16[32,128]{1,0:T(8,128)(2,1)S(1)}, u32[]{:S(2)}, u32[]{:S(2)}) collective-permute-start(bf16[32,128]{1,0:T(8,128)(2,1)S(1)} %shard_map.52.refs_0_), channel_id=1, source_target_pairs={{4,5},{5,4},{6,7},{7,6}} | collective-permute-start | bytes 24584 | tf_op jit(solution)/shard_map/ppermute | solution.py:285
  21.5 5.5 %collective-permute-start.7 = (bf16[32,4096]{1,0:T(8,128)(2,1)S(1)}, bf16[32,4096]{1,0:T(8,128)(2,1)S(1)}, u32[]{:S(2)}, u32[]{:S(2)}) collective-permute-start(bf16[32,4096]{1,0:T(8,128)(2,1)S(1)} %get-tuple-element.99.refs_1_), channel_id=1, source_target_pairs={{4,8},{5,9},{6,10},{7,11}} | collective-permute-start | bytes 786440 | tf_op jit(solution)/shard_map/ppermute | solution.py:285
  22.4 5.4 %collective-permute-start.9 = (bf16[32,128]{1,0:T(8,128)(2,1)S(1)}, bf16[32,128]{1,0:T(8,128)(2,1)S(1)}, u32[]{:S(2)}, u32[]{:S(2)}) collective-permute-start(bf16[32,128]{1,0:T(8,128)(2,1)S(1)} %shard_map.57), channel_id=1, source_target_pairs={{4,10},{5,11},{6,8},{7,9}} | collective-permute-start | bytes 24584 | tf_op jit(solution)/shard_map/ppermute | solution.py:285
  28.2 1.6 %collective-permute-start.11 = (bf16[32,128]{1,0:T(8,128)(2,1)S(1)}, bf16[32,128]{1,0:T(8,128)(2,1)S(1)}, u32[]{:S(2)}, u32[]{:S(2)}) collective-permute-start(bf16[32,128]{1,0:T(8,128)(2,1)S(1)} %shard_map.59.refs_0_), channel_id=1, source_target_pairs={{8,9},{9,8},{10,11},{11,10}} | collective-permute-start | bytes 24584 | tf_op jit(solution)/shard_map/ppermute | solution.py:285
  30.1 3.8 %collective-permute-start.12 = (bf16[32,2048]{1,0:T(8,128)(2,1)S(1)}, bf16[32,2048]{1,0:T(8,128)(2,1)S(1)}, u32[]{:S(2)}, u32[]{:S(2)}) collective-permute-start(bf16[32,2048]{1,0:T(8,128)(2,1)S(1)} %get-tuple-element.106.refs_6_), channel_id=1, source_target_pairs={{8,12},{9,13},{10,14},{11,15}} | collective-permute-start | bytes 393224 | tf_op jit(solution)/shard_map/ppermute | solution.py:285
  31.2 3.6 %collective-permute-start.13 = (bf16[32,2048]{1,0:T(8,128)(2,1)S(1)}, bf16[32,2048]{1,0:T(8,128)(2,1)S(1)}, u32[]{:S(2)}, u32[]{:S(2)}) collective-permute-start(bf16[32,2048]{1,0:T(8,128)(2,1)S(1)} %get-tuple-element.112), channel_id=1, source_target_pairs={{8,12},{9,13},{10,14},{11,15}} | collective-permute-start | bytes 393224 | tf_op jit(solution)/shard_map/ppermute | solution.py:285
  31.9 3.9 %collective-permute-start.14 = (bf16[32,128]{1,0:T(8,128)(2,1)S(1)}, bf16[32,128]{1,0:T(8,128)(2,1)S(1)}, u32[]{:S(2)}, u32[]{:S(2)}) collective-permute-start(bf16[32,128]{1,0:T(8,128)(2,1)S(1)} %get-tuple-element.117), channel_id=1, source_target_pairs={{8,15},{9,14},{10,13},{11,12}} | collective-permute-start | bytes 24584 | tf_op jit(solution)/shard_map/ppermute | solution.py:285
  32.6 3.2 %collective-permute-start.15 = (bf16[32,128]{1,0:T(8,128)(2,1)S(1)}, bf16[32,128]{1,0:T(8,128)(2,1)S(1)}, u32[]{:S(2)}, u32[]{:S(2)}) collective-permute-start(bf16[32,128]{1,0:T(8,128)(2,1)S(1)} %get-tuple-element.117), channel_id=1, source_target_pairs={{8,14},{9,15},{10,12},{11,13}} | collective-permute-start | bytes 24584 | tf_op jit(solution)/shard_map/ppermute | solution.py:285
  33.2 2.5 %collective-permute-start.16 = (bf16[32,128]{1,0:T(8,128)(2,1)S(1)}, bf16[32,128]{1,0:T(8,128)(2,1)S(1)}, u32[]{:S(2)}, u32[]{:S(2)}) collective-permute-start(bf16[32,128]{1,0:T(8,128)(2,1)S(1)} %get-tuple-element.117), channel_id=1, source_target_pairs={{8,13},{9,12},{10,15},{11,14}} | collective-permute-start | bytes 24584 | tf_op jit(solution)/shard_map/ppermute | solution.py:285
  36.2 3.0 %collective-permute-start.17 = (bf16[32,4096]{1,0:T(8,128)(2,1)S(1)}, bf16[32,4096]{1,0:T(8,128)(2,1)S(1)}, u32[]{:S(2)}, u32[]{:S(2)}) collective-permute-start(bf16[32,4096]{1,0:T(8,128)(2,1)S(1)} %get-tuple-element.118.refs_0_), channel_id=1, source_target_pairs={{12,16},{13,17},{14,18},{15,19}} | collective-permute-start | bytes 786440 | tf_op jit(solution)/shard_map/ppermute | solution.py:285
  37.2 3.9 %collective-permute-start.18 = (bf16[32,128]{1,0:T(8,128)(2,1)S(1)}, bf16[32,128]{1,0:T(8,128)(2,1)S(1)}, u32[]{:S(2)}, u32[]{:S(2)}) collective-permute-start(bf16[32,128]{1,0:T(8,128)(2,1)S(1)} %shard_map.68), channel_id=1, source_target_pairs={{12,19},{13,18},{14,17},{15,16}} | collective-permute-start | bytes 24584 | tf_op jit(solution)/shard_map/ppermute | solution.py:285
  37.8 3.2 %collective-permute-start.19 = (bf16[32,128]{1,0:T(8,128)(2,1)S(1)}, bf16[32,128]{1,0:T(8,128)(2,1)S(1)}, u32[]{:S(2)}, u32[]{:S(2)}) collective-permute-start(bf16[32,128]{1,0:T(8,128)(2,1)S(1)} %shard_map.68), channel_id=1, source_target_pairs={{12,18},{13,19},{14,16},{15,17}} | collective-permute-start | bytes 24584 | tf_op jit(solution)/shard_map/ppermute | solution.py:285
  38.5 2.5 %collective-permute-start.20 = (bf16[32,128]{1,0:T(8,128)(2,1)S(1)}, bf16[32,128]{1,0:T(8,128)(2,1)S(1)}, u32[]{:S(2)}, u32[]{:S(2)}) collective-permute-start(bf16[32,128]{1,0:T(8,128)(2,1)S(1)} %shard_map.68), channel_id=1, source_target_pairs={{12,17},{13,16},{14,19},{15,18}} | collective-permute-start | bytes 24584 | tf_op jit(solution)/shard_map/ppermute | solution.py:285
  41.3 4.0 %collective-permute-start.21 = (bf16[32,2048]{1,0:T(8,128)(2,1)S(1)}, bf16[32,2048]{1,0:T(8,128)(2,1)S(1)}, u32[]{:S(2)}, u32[]{:S(2)}) collective-permute-start(bf16[32,2048]{1,0:T(8,128)(2,1)S(1)} %get-tuple-element.125.refs_6_), channel_id=1, source_target_pairs={{16,20},{17,21},{18,22},{19,23}} | collective-permute-start | bytes 393224 | tf_op jit(solution)/shard_map/ppermute | solution.py:285
  42.5 3.8 %collective-permute-start.22 = (bf16[32,2048]{1,0:T(8,128)(2,1)S(1)}, bf16[32,2048]{1,0:T(8,128)(2,1)S(1)}, u32[]{:S(2)}, u32[]{:S(2)}) collective-permute-start(bf16[32,2048]{1,0:T(8,128)(2,1)S(1)} %get-tuple-element.132), channel_id=1, source_target_pairs={{16,20},{17,21},{18,22},{19,23}} | collective-permute-start | bytes 393224 | tf_op jit(solution)/shard_map/ppermute | solution.py:285
  43.2 4.0 %collective-permute-start.23 = (bf16[32,128]{1,0:T(8,128)(2,1)S(1)}, bf16[32,128]{1,0:T(8,128)(2,1)S(1)}, u32[]{:S(2)}, u32[]{:S(2)}) collective-permute-start(bf16[32,128]{1,0:T(8,128)(2,1)S(1)} %get-tuple-element.135), channel_id=1, source_target_pairs={{16,23},{17,22},{18,21},{19,20}} | collective-permute-start | bytes 24584 | tf_op jit(solution)/shard_map/ppermute | solution.py:285
  43.8 3.4 %collective-permute-start.24 = (bf16[32,128]{1,0:T(8,128)(2,1)S(1)}, bf16[32,128]{1,0:T(8,128)(2,1)S(1)}, u32[]{:S(2)}, u32[]{:S(2)}) collective-permute-start(bf16[32,128]{1,0:T(8,128)(2,1)S(1)} %get-tuple-element.135), channel_id=1, source_target_pairs={{16,22},{17,23},{18,20},{19,21}} | collective-permute-start | bytes 24584 | tf_op jit(solution)/shard_map/ppermute | solution.py:285
  44.5 2.7 %collective-permute-start.25 = (bf16[32,128]{1,0:T(8,128)(2,1)S(1)}, bf16[32,128]{1,0:T(8,128)(2,1)S(1)}, u32[]{:S(2)}, u32[]{:S(2)}) collective-permute-start(bf16[32,128]{1,0:T(8,128)(2,1)S(1)} %get-tuple-element.135), channel_id=1, source_target_pairs={{16,21},{17,20},{18,23},{19,22}} | collective-permute-start | bytes 24584 | tf_op jit(solution)/shard_map/ppermute | solution.py:285
  47.5 3.9 %collective-permute-start.26 = (bf16[32,2048]{1,0:T(8,128)(2,1)S(1)}, bf16[32,2048]{1,0:T(8,128)(2,1)S(1)}, u32[]{:S(2)}, u32[]{:S(2)}) collective-permute-start(bf16[32,2048]{1,0:T(8,128)(2,1)S(1)} %get-tuple-element.136.refs_6_), channel_id=1, source_target_pairs={{20,24},{21,25},{22,26},{23,27}} | collective-permute-start | bytes 393224 | tf_op jit(solution)/shard_map/ppermute | solution.py:285
  48.7 3.6 %collective-permute-start.27 = (bf16[32,2048]{1,0:T(8,128)(2,1)S(1)}, bf16[32,2048]{1,0:T(8,128)(2,1)S(1)}, u32[]{:S(2)}, u32[]{:S(2)}) collective-permute-start(bf16[32,2048]{1,0:T(8,128)(2,1)S(1)} %get-tuple-element.143), channel_id=1, source_target_pairs={{20,24},{21,25},{22,26},{23,27}} | collective-permute-start | bytes 393224 | tf_op jit(solution)/shard_map/ppermute | solution.py:285
  49.4 3.9 %collective-permute-start.28 = (bf16[32,128]{1,0:T(8,128)(2,1)S(1)}, bf16[32,128]{1,0:T(8,128)(2,1)S(1)}, u32[]{:S(2)}, u32[]{:S(2)}) collective-permute-start(bf16[32,128]{1,0:T(8,128)(2,1)S(1)} %get-tuple-element.146), channel_id=1, source_target_pairs={{20,27},{21,26},{22,25},{23,24}} | collective-permute-start | bytes 24584 | tf_op jit(solution)/shard_map/ppermute | solution.py:285
  50.0 3.2 %collective-permute-start.29 = (bf16[32,128]{1,0:T(8,128)(2,1)S(1)}, bf16[32,128]{1,0:T(8,128)(2,1)S(1)}, u32[]{:S(2)}, u32[]{:S(2)}) collective-permute-start(bf16[32,128]{1,0:T(8,128)(2,1)S(1)} %get-tuple-element.146), channel_id=1, source_target_pairs={{20,26},{21,27},{22,24},{23,25}} | collective-permute-start | bytes 24584 | tf_op jit(solution)/shard_map/ppermute | solution.py:285
  50.7 2.5 %collective-permute-start.30 = (bf16[32,128]{1,0:T(8,128)(2,1)S(1)}, bf16[32,128]{1,0:T(8,128)(2,1)S(1)}, u32[]{:S(2)}, u32[]{:S(2)}) collective-permute-start(bf16[32,128]{1,0:T(8,128)(2,1)S(1)} %get-tuple-element.146), channel_id=1, source_target_pairs={{20,25},{21,24},{22,27},{23,26}} | collective-permute-start | bytes 24584 | tf_op jit(solution)/shard_map/ppermute | solution.py:285
  53.5 35.9 %collective-permute-start.31 = (bf16[32,2048]{1,0:T(8,128)(2,1)S(1)}, bf16[32,2048]{1,0:T(8,128)(2,1)S(1)}, u32[]{:S(2)}, u32[]{:S(2)}) collective-permute-start(bf16[32,2048]{1,0:T(8,128)(2,1)S(1)} %get-tuple-element.147.refs_6_), channel_id=1, source_target_pairs={{24,28},{25,29},{26,30},{27,31}} | collective-permute-start | bytes 393224 | tf_op jit(solution)/shard_map/ppermute | solution.py:285
  55.3 36.1 %collective-permute-start.32 = (bf16[32,2048]{1,0:T(8,128)(2,1)S(1)}, bf16[32,2048]{1,0:T(8,128)(2,1)S(1)}, u32[]{:S(2)}, u32[]{:S(2)}) collective-permute-start(bf16[32,2048]{1,0:T(8,128)(2,1)S(1)} %get-tuple-element.152), channel_id=1, source_target_pairs={{24,28},{25,29},{26,30},{27,31}} | collective-permute-start | bytes 393224 | tf_op jit(solution)/shard_map/ppermute | solution.py:285
  56.6 35.7 %collective-permute-start.33 = (bf16[32,128]{1,0:T(8,128)(2,1)S(1)}, bf16[32,128]{1,0:T(8,128)(2,1)S(1)}, u32[]{:S(2)}, u32[]{:S(2)}) collective-permute-start(bf16[32,128]{1,0:T(8,128)(2,1)S(1)} %get-tuple-element.157), channel_id=1, source_target_pairs={{24,31},{25,30},{26,29},{27,28}} | collective-permute-start | bytes 24584 | tf_op jit(solution)/shard_map/ppermute | solution.py:285
  57.9 34.4 %collective-permute-start.34 = (bf16[32,128]{1,0:T(8,128)(2,1)S(1)}, bf16[32,128]{1,0:T(8,128)(2,1)S(1)}, u32[]{:S(2)}, u32[]{:S(2)}) collective-permute-start(bf16[32,128]{1,0:T(8,128)(2,1)S(1)} %get-tuple-element.157), channel_id=1, source_target_pairs={{24,30},{25,31},{26,28},{27,29}} | collective-permute-start | bytes 24584 | tf_op jit(solution)/shard_map/ppermute | solution.py:285
  59.2 33.1 %collective-permute-start.35 = (bf16[32,128]{1,0:T(8,128)(2,1)S(1)}, bf16[32,128]{1,0:T(8,128)(2,1)S(1)}, u32[]{:S(2)}, u32[]{:S(2)}) collective-permute-start(bf16[32,128]{1,0:T(8,128)(2,1)S(1)} %get-tuple-element.157), channel_id=1, source_target_pairs={{24,29},{25,28},{26,31},{27,30}} | collective-permute-start | bytes 24584 | tf_op jit(solution)/shard_map/ppermute | solution.py:285

commit v5 on v1

--- a/solution.py
+++ b/solution.py
@@ -10,7 +10,7 @@
 VMEM_LIMIT = 24 * 1024 * 1024
 FIRST_SHARE = 2
 IN_PLACE = 2
-WHOLE_HOP = 3
+WHOLE_HOP = 5
 OPEN_FLOPS = 4 * 10**9
 ROWS_TIMES_COLUMNS = (((1,), (0,)), ((), ()))
 ROWS_TIMES_ROWS = (((1,), (1,)), ((), ()))

time: 94.3 us -> 94.4 us (level)
  no operation moved by 1% of the time
where the time goes in v5:
time: 94.4 us; the launch traced here: 93.5 us
  waiting for transfers between devices  36.9 us (39%)
  starting transfers between devices  31.8 us (34%)
  Pallas kernels  24 us (25%)
    ppermute x36, waiting for transfers between devices, moved(): return lax.ppermute(x, ('slab', 'hodlr'), route)  36.9 us
    ppermute x36, starting transfers between devices, moved(): return lax.ppermute(x, ('slab', 'hodlr'), route)  31.8 us
    pallas_call x40, Pallas kernels, call(): pl.pallas_call(kernel, out_shape=outs, in_specs=[remote if i in from_hbm...  24 us
  transfers between devices with their start and end apart: 36, of which 4 were waited for; matrix products, arithmetic and copies ran while one was open for 0% of the time, Pallas kernels for 21%

profile of v5, /device:TPU:26, one launch (start us, length us, event | category | flops | bytes accessed | tf_op | source)
XLA Modules:
  0.0 93.5 jit_solution(15690688013668221662)
XLA Ops:
  0.0 1.6 %shard_map.46 = (bf16[1,64,4096]{2,1,0:T(8,128)(2,1)S(1)}, bf16[1,64,4096]{2,1,0:T(8,128)(2,1)S(1)}, bf16[1,64,4096]{2,1,0:T(8,128)(2,1)S(1)}, bf16[32,2048]{1,0:T(8,128)(2,1)S(1)}, bf16[32,2048]{1,0:T(8,128)(2,1)S(1)}) custom-call(bf16[32,4096]{1,0:T(8,128)(2,1)} %bitcast.46, bf16[4,64,4096]{2,1,0:T(8,128)(2,1)} %bitcast.37), custom_call_target="tpu_custom_call" | custom-call | tf_op jit(solution)/shard_map/pallas_call | solution.py:30
  1.6 2.6 %collective-permute-start.4 = (bf16[64,4096]{1,0:T(8,128)(2,1)S(1)}, bf16[64,4096]{1,0:T(8,128)(2,1)S(1)}, u32[]{:S(2)}, u32[]{:S(2)}) collective-permute-start(bf16[64,4096]{1,0:T(8,128)(2,1)S(1)} %bitcast.45), channel_id=1, source_target_pairs={{4,0},{5,1},{6,2},{7,3},{12,8},{13,9},{14,10},{15,11},{16,12},{17,... | collective-permute-start | bytes 1572872 | tf_op jit(solution)/shard_map/ppermute | solution.py:278
  4.3 0.4 shard_map.48
  4.8 1.6 %collective-permute-start.1 = (bf16[32,128]{1,0:T(8,128)(2,1)S(1)}, bf16[32,128]{1,0:T(8,128)(2,1)S(1)}, u32[]{:S(2)}, u32[]{:S(2)}) collective-permute-start(bf16[32,128]{1,0:T(8,128)(2,1)S(1)} %shard_map.48), channel_id=1, source_target_pairs={{0,2},{1,3},{2,0},{3,1},{4,6},{5,7},{6,4},{7,5},{8,10},{9,11},{10,... | collective-permute-start | bytes 24584 | tf_op jit(solution)/shard_map/ppermute | solution.py:278
  6.3 0.3 collective-permute-start.2
  6.6 3.3 %collective-permute-start.10 = (bf16[64,4096]{1,0:T(8,128)(2,1)S(1)}, bf16[64,4096]{1,0:T(8,128)(2,1)S(1)}, u32[]{:S(2)}, u32[]{:S(2)}) collective-permute-start(bf16[64,4096]{1,0:T(8,128)(2,1)S(1)} %bitcast.43), channel_id=1, source_target_pairs={{12,8},{13,9},{14,10},{15,11},{16,12},{17,13},{18,14},{19,15},{20,... | collective-permute-start | bytes 1572872 | tf_op jit(solution)/shard_map/ppermute | solution.py:278
  9.9 1.8 %shard_map.47 = (bf16[2,1024,256]{2,1,0:T(8,128)(2,1)S(1)}, f32[32,2048]{1,0:T(8,128)S(1)}, f32[32,2048]{1,0:T(8,128)S(1)}, f32[2,32,128]{2,1,0:T(8,128)S(1)}, f32[2,32,128]{2,1,0:T(8,128)S(1)}) custom-call(bf16[32,2048]{1,0:T(8,128)(2,1)S(1)} %get-tuple-element.78.refs_0_.refs_2_.w_ref, bf16[32,2048]{1,0:T(8,128)(2,1)S(1)} %get-tuple-element.79.refs_1_.refs_3_.w_ref, ...), custom_call_target="tpu_custom_call" | custom-call | tf_op jit(solution)/shard_map/pallas_call | solution.py:30
  11.8 0.4 shard_map.49
  12.2 0.7 collective-permute-start.3
  12.9 3.6 %collective-permute-done.4.refs_0_.refs_1_ = bf16[64,4096]{1,0:T(8,128)(2,1)S(1)} collective-permute-done((bf16[64,4096]{1,0:T(8,128)(2,1)S(1)}, bf16[64,4096]{1,0:T(8,128)(2,1)S(1)}, u32[]{:S(2)}, u32[]{:S(2)}) %collective-permute-start.4) | collective-permute-done | bytes 524320 | tf_op jit(solution)/shard_map/ppermute | solution.py:278
  16.8 0.7 collective-permute-start.5
  17.5 0.7 collective-permute-start.8
  18.2 0.9 shard_map.51
  19.1 0.3 shard_map.52.refs_0_
  19.5 0.7 collective-permute-start.6
  20.1 0.9 shard_map.53
  21.1 0.4 shard_map.54
  21.5 0.7 collective-permute-start.7
  22.4 0.7 collective-permute-start.9
  23.1 3.5 %collective-permute-done.10.refs_0_ = bf16[64,4096]{1,0:T(8,128)(2,1)S(1)} collective-permute-done((bf16[64,4096]{1,0:T(8,128)(2,1)S(1)}, bf16[64,4096]{1,0:T(8,128)(2,1)S(1)}, u32[]{:S(2)}, u32[]{:S(2)}) %collective-permute-start.10) | collective-permute-done | bytes 524320 | tf_op jit(solution)/shard_map/ppermute | solution.py:278
  26.6 0.3 shard_map.58.refs_2_.v_ref
  26.9 0.9 shard_map.55
  27.9 0.3 shard_map.59.refs_0_
  28.2 0.7 collective-permute-start.11
  28.9 0.9 shard_map.60
  30.1 0.7 collective-permute-start.12
  31.0 0.7 collective-permute-start.13
  32.0 0.7 collective-permute-start.14
  32.6 0.7 collective-permute-start.15
  33.3 0.7 collective-permute-start.16
  34.0 0.9 shard_map.62
  34.9 0.9 shard_map.64
  36.1 0.7 collective-permute-start.17
  37.1 0.7 collective-permute-start.18
  38.0 0.7 collective-permute-start.19
  38.7 0.7 collective-permute-start.20
  39.4 0.7 collective-permute-start.21
  40.1 0.9 shard_map.67
  41.0 0.9 shard_map.69
  42.2 0.7 collective-permute-start.22
  43.2 0.7 collective-permute-start.23
  44.1 0.7 collective-permute-start.24
  44.8 0.8 collective-permute-start.25
  45.6 0.7 collective-permute-start.26
  46.3 0.9 shard_map.72
  47.2 0.9 shard_map.74
  48.2 0.4 shard_map.76
  48.6 0.7 collective-permute-start.27
  49.3 0.3 shard_map.79
  49.6 0.7 collective-permute-start.28
  50.3 0.7 collective-permute-start.29
  50.9 0.7 collective-permute-start.30
  51.6 0.9 shard_map.77
  52.5 0.9 shard_map.78
  53.7 1.3 %collective-permute-start.31 = (bf16[32,2048]{1,0:T(8,128)(2,1)S(1)}, bf16[32,2048]{1,0:T(8,128)(2,1)S(1)}, u32[]{:S(2)}, u32[]{:S(2)}) collective-permute-start(bf16[32,2048]{1,0:T(8,128)(2,1)S(1)} %get-tuple-element.140.refs_0_), channel_id=1, source_target_pairs={{24,28},{25,29},{26,30},{27,31}} | collective-permute-start | bytes 393224 | tf_op jit(solution)/shard_map/ppermute | solution.py:278
  55.3 1.3 %collective-permute-start.32 = (bf16[32,2048]{1,0:T(8,128)(2,1)S(1)}, bf16[32,2048]{1,0:T(8,128)(2,1)S(1)}, u32[]{:S(2)}, u32[]{:S(2)}) collective-permute-start(bf16[32,2048]{1,0:T(8,128)(2,1)S(1)} %get-tuple-element.145.refs_1_), channel_id=1, source_target_pairs={{24,28},{25,29},{26,30},{27,31}} | collective-permute-start | bytes 393224 | tf_op jit(solution)/shard_map/ppermute | solution.py:278
  56.9 1.3 %collective-permute-start.33 = (bf16[32,128]{1,0:T(8,128)(2,1)S(1)}, bf16[32,128]{1,0:T(8,128)(2,1)S(1)}, u32[]{:S(2)}, u32[]{:S(2)}) collective-permute-start(bf16[32,128]{1,0:T(8,128)(2,1)S(1)} %shard_map.84), channel_id=1, source_target_pairs={{24,31},{25,30},{26,29},{27,28}} | collective-permute-start | bytes 24584 | tf_op jit(solution)/shard_map/ppermute | solution.py:278
  58.2 1.3 %collective-permute-start.34 = (bf16[32,128]{1,0:T(8,128)(2,1)S(1)}, bf16[32,128]{1,0:T(8,128)(2,1)S(1)}, u32[]{:S(2)}, u32[]{:S(2)}) collective-permute-start(bf16[32,128]{1,0:T(8,128)(2,1)S(1)} %shard_map.84), channel_id=1, source_target_pairs={{24,30},{25,31},{26,28},{27,29}} | collective-permute-start | bytes 24584 | tf_op jit(solution)/shard_map/ppermute | solution.py:278
  59.5 1.3 %collective-permute-start.35 = (bf16[32,128]{1,0:T(8,128)(2,1)S(1)}, bf16[32,128]{1,0:T(8,128)(2,1)S(1)}, u32[]{:S(2)}, u32[]{:S(2)}) collective-permute-start(bf16[32,128]{1,0:T(8,128)(2,1)S(1)} %shard_map.84), channel_id=1, source_target_pairs={{24,29},{25,28},{26,31},{27,30}} | collective-permute-start | bytes 24584 | tf_op jit(solution)/shard_map/ppermute | solution.py:278
  60.8 29.0 %collective-permute-done.31.front_ref = bf16[32,2048]{1,0:T(8,128)(2,1)S(1)} collective-permute-done((bf16[32,2048]{1,0:T(8,128)(2,1)S(1)}, bf16[32,2048]{1,0:T(8,128)(2,1)S(1)}, u32[]{:S(2)}, u32[]{:S(2)}) %collective-permute-start.31) | collective-permute-done | bytes 131104 | tf_op jit(solution)/shard_map/ppermute | solution.py:278
  89.7 0.9 shard_map.81
  90.7 0.7 collective-permute-done.32.front_ref
  91.4 0.9 shard_map.83
  92.3 1.1 %shard_map.85 = (bf16[32,4096]{1,0:T(8,128)(2,1)}, f32[32,128]{1,0:T(8,128)S(1)}) custom-call(f32[32,2048]{1,0:T(8,128)S(1)} %get-tuple-element.141.refs_0_, f32[32,2048]{1,0:T(8,128)S(1)} %get-tuple-element.147.refs_1_, f32[2,32,128]{2,1,0:T(8,128)S(1)} %get-tuple-element.146.refs_0_.refs_2_, ...), custom_call_target="tpu_custom_call", output_to_operand_aliasing={{1}: (4, {})} | custom-call | tf_op jit(solution)/shard_map/pallas_call | solution.py:30
  (58 shorter events, 4.0 us)
Async XLA Ops:
  0.0 9.9 %slice-start = ((s8[8388608]{0:T(1024)(128)(4,1)}), s8[4194304]{0:T(1024)(128)(4,1)S(1)}, s32[]{:S(2)}) async-start(s8[8388608]{0:T(1024)(128)(4,1)} %bitcast.8), calls=%async_computation | async-start | bytes 8388608
  1.6 14.9 %collective-permute-start.4 = (bf16[64,4096]{1,0:T(8,128)(2,1)S(1)}, bf16[64,4096]{1,0:T(8,128)(2,1)S(1)}, u32[]{:S(2)}, u32[]{:S(2)}) collective-permute-start(bf16[64,4096]{1,0:T(8,128)(2,1)S(1)} %bitcast.45), channel_id=1, source_target_pairs={{4,0},{5,1},{6,2},{7,3},{12,8},{13,9},{14,10},{15,11},{16,12},{17,... | collective-permute-start | bytes 1572872 | tf_op jit(solution)/shard_map/ppermute | solution.py:278
  4.2 5.7 %slice-start.1 = ((s8[8388608]{0:T(1024)(128)(4,1)}), s8[4194304]{0:T(1024)(128)(4,1)S(1)}, s32[]{:S(2)}) async-start(s8[8388608]{0:T(1024)(128)(4,1)} %bitcast.8), calls=%async_computation.1 | async-start | bytes 8388608
  4.2 5.7 %copy-start.1 = (bf16[1,4,64,4096]{3,2,1,0:T(8,128)(2,1)S(1)}, bf16[1,4,64,4096]{3,2,1,0:T(8,128)(2,1)}, u32[]{:S(2)}) copy-start(bf16[1,4,64,4096]{3,2,1,0:T(8,128)(2,1)} %param.6) | copy-start | bytes 6291460
  4.7 7.1 %collective-permute-start = (bf16[32,128]{1,0:T(8,128)(2,1)S(1)}, bf16[32,128]{1,0:T(8,128)(2,1)S(1)}, u32[]{:S(2)}, u32[]{:S(2)}) collective-permute-start(bf16[32,128]{1,0:T(8,128)(2,1)S(1)} %shard_map.48), channel_id=1, source_target_pairs={{0,1},{1,0},{2,3},{3,2},{4,5},{5,4},{6,7},{7,6},{8,9},{9,8},{10,11... | collective-permute-start | bytes 24584 | tf_op jit(solution)/shard_map/ppermute | solution.py:278
  4.8 7.0 %collective-permute-start.1 = (bf16[32,128]{1,0:T(8,128)(2,1)S(1)}, bf16[32,128]{1,0:T(8,128)(2,1)S(1)}, u32[]{:S(2)}, u32[]{:S(2)}) collective-permute-start(bf16[32,128]{1,0:T(8,128)(2,1)S(1)} %shard_map.48), channel_id=1, source_target_pairs={{0,2},{1,3},{2,0},{3,1},{4,6},{5,7},{6,4},{7,5},{8,10},{9,11},{10,... | collective-permute-start | bytes 24584 | tf_op jit(solution)/shard_map/ppermute | solution.py:278
  6.3 5.4 %collective-permute-start.2 = (bf16[32,128]{1,0:T(8,128)(2,1)S(1)}, bf16[32,128]{1,0:T(8,128)(2,1)S(1)}, u32[]{:S(2)}, u32[]{:S(2)}) collective-permute-start(bf16[32,128]{1,0:T(8,128)(2,1)S(1)} %shard_map.48), channel_id=1, source_target_pairs={{0,3},{1,2},{2,1},{3,0},{4,7},{5,6},{6,5},{7,4},{8,11},{9,10},{10,... | collective-permute-start | bytes 24584 | tf_op jit(solution)/shard_map/ppermute | solution.py:278
  6.6 20.0 %collective-permute-start.10 = (bf16[64,4096]{1,0:T(8,128)(2,1)S(1)}, bf16[64,4096]{1,0:T(8,128)(2,1)S(1)}, u32[]{:S(2)}, u32[]{:S(2)}) collective-permute-start(bf16[64,4096]{1,0:T(8,128)(2,1)S(1)} %bitcast.43), channel_id=1, source_target_pairs={{12,8},{13,9},{14,10},{15,11},{16,12},{17,13},{18,14},{19,15},{20,... | collective-permute-start | bytes 1572872 | tf_op jit(solution)/shard_map/ppermute | solution.py:278
  9.9 1.9 %copy-start = (bf16[1,4,64,4096]{3,2,1,0:T(8,128)(2,1)S(1)}, bf16[1,4,64,4096]{3,2,1,0:T(8,128)(2,1)}, u32[]{:S(2)}) copy-start(bf16[1,4,64,4096]{3,2,1,0:T(8,128)(2,1)} %param.7) | copy-start | bytes 6291460
  12.2 6.0 %collective-permute-start.3 = (bf16[32,4096]{1,0:T(8,128)(2,1)S(1)}, bf16[32,4096]{1,0:T(8,128)(2,1)S(1)}, u32[]{:S(2)}, u32[]{:S(2)}) collective-permute-start(bf16[32,4096]{1,0:T(8,128)(2,1)S(1)} %get-tuple-element.86.refs_1_), channel_id=1, source_target_pairs={{0,4},{1,5},{2,6},{3,7}} | collective-permute-start | bytes 786440 | tf_op jit(solution)/shard_map/ppermute | solution.py:278
  16.8 2.4 %collective-permute-start.5 = (bf16[32,128]{1,0:T(8,128)(2,1)S(1)}, bf16[32,128]{1,0:T(8,128)(2,1)S(1)}, u32[]{:S(2)}, u32[]{:S(2)}) collective-permute-start(bf16[32,128]{1,0:T(8,128)(2,1)S(1)} %shard_map.50.refs_0_.refs_2_.other_ref), channel_id=1, source_target_pairs={{0,6},{1,7},{2,4},{3,5}} | collective-permute-start | bytes 24584 | tf_op jit(solution)/shard_map/ppermute | solution.py:278
  17.5 4.7 %collective-permute-start.8 = (bf16[64,4096]{1,0:T(8,128)(2,1)S(1)}, bf16[64,4096]{1,0:T(8,128)(2,1)S(1)}, u32[]{:S(2)}, u32[]{:S(2)}) collective-permute-start(bf16[64,4096]{1,0:T(8,128)(2,1)S(1)} %shard_map.56), channel_id=1, source_target_pairs={{8,4},{9,5},{10,6},{11,7}} | collective-permute-start | bytes 1572872 | tf_op jit(solution)/shard_map/ppermute | solution.py:278
  19.5 1.6 %collective-permute-start.6 = (bf16[32,128]{1,0:T(8,128)(2,1)S(1)}, bf16[32,128]{1,0:T(8,128)(2,1)S(1)}, u32[]{:S(2)}, u32[]{:S(2)}) collective-permute-start(bf16[32,128]{1,0:T(8,128)(2,1)S(1)} %shard_map.52.refs_0_), channel_id=1, source_target_pairs={{4,5},{5,4},{6,7},{7,6}} | collective-permute-start | bytes 24584 | tf_op jit(solution)/shard_map/ppermute | solution.py:278
  21.5 5.5 %collective-permute-start.7 = (bf16[32,4096]{1,0:T(8,128)(2,1)S(1)}, bf16[32,4096]{1,0:T(8,128)(2,1)S(1)}, u32[]{:S(2)}, u32[]{:S(2)}) collective-permute-start(bf16[32,4096]{1,0:T(8,128)(2,1)S(1)} %get-tuple-element.95.refs_1_), channel_id=1, source_target_pairs={{4,8},{5,9},{6,10},{7,11}} | collective-permute-start | bytes 786440 | tf_op jit(solution)/shard_map/ppermute | solution.py:278
  22.4 5.4 %collective-permute-start.9 = (bf16[32,128]{1,0:T(8,128)(2,1)S(1)}, bf16[32,128]{1,0:T(8,128)(2,1)S(1)}, u32[]{:S(2)}, u32[]{:S(2)}) collective-permute-start(bf16[32,128]{1,0:T(8,128)(2,1)S(1)} %shard_map.57), channel_id=1, source_target_pairs={{4,10},{5,11},{6,8},{7,9}} | collective-permute-start | bytes 24584 | tf_op jit(solution)/shard_map/ppermute | solution.py:278
  28.2 1.6 %collective-permute-start.11 = (bf16[32,128]{1,0:T(8,128)(2,1)S(1)}, bf16[32,128]{1,0:T(8,128)(2,1)S(1)}, u32[]{:S(2)}, u32[]{:S(2)}) collective-permute-start(bf16[32,128]{1,0:T(8,128)(2,1)S(1)} %shard_map.59.refs_0_), channel_id=1, source_target_pairs={{8,9},{9,8},{10,11},{11,10}} | collective-permute-start | bytes 24584 | tf_op jit(solution)/shard_map/ppermute | solution.py:278
  30.1 3.9 %collective-permute-start.12 = (bf16[32,2048]{1,0:T(8,128)(2,1)S(1)}, bf16[32,2048]{1,0:T(8,128)(2,1)S(1)}, u32[]{:S(2)}, u32[]{:S(2)}) collective-permute-start(bf16[32,2048]{1,0:T(8,128)(2,1)S(1)} %get-tuple-element.102.refs_0_), channel_id=1, source_target_pairs={{8,12},{9,13},{10,14},{11,15}} | collective-permute-start | bytes 393224 | tf_op jit(solution)/shard_map/ppermute | solution.py:278
  31.0 3.9 %collective-permute-start.13 = (bf16[32,2048]{1,0:T(8,128)(2,1)S(1)}, bf16[32,2048]{1,0:T(8,128)(2,1)S(1)}, u32[]{:S(2)}, u32[]{:S(2)}) collective-permute-start(bf16[32,2048]{1,0:T(8,128)(2,1)S(1)} %get-tuple-element.109.refs_1_), channel_id=1, source_target_pairs={{8,12},{9,13},{10,14},{11,15}} | collective-permute-start | bytes 393224 | tf_op jit(solution)/shard_map/ppermute | solution.py:278
  32.0 3.9 %collective-permute-start.14 = (bf16[32,128]{1,0:T(8,128)(2,1)S(1)}, bf16[32,128]{1,0:T(8,128)(2,1)S(1)}, u32[]{:S(2)}, u32[]{:S(2)}) collective-permute-start(bf16[32,128]{1,0:T(8,128)(2,1)S(1)} %shard_map.65), channel_id=1, source_target_pairs={{8,15},{9,14},{10,13},{11,12}} | collective-permute-start | bytes 24584 | tf_op jit(solution)/shard_map/ppermute | solution.py:278
  32.6 3.2 %collective-permute-start.15 = (bf16[32,128]{1,0:T(8,128)(2,1)S(1)}, bf16[32,128]{1,0:T(8,128)(2,1)S(1)}, u32[]{:S(2)}, u32[]{:S(2)}) collective-permute-start(bf16[32,128]{1,0:T(8,128)(2,1)S(1)} %shard_map.65), channel_id=1, source_target_pairs={{8,14},{9,15},{10,12},{11,13}} | collective-permute-start | bytes 24584 | tf_op jit(solution)/shard_map/ppermute | solution.py:278
  33.3 2.5 %collective-permute-start.16 = (bf16[32,128]{1,0:T(8,128)(2,1)S(1)}, bf16[32,128]{1,0:T(8,128)(2,1)S(1)}, u32[]{:S(2)}, u32[]{:S(2)}) collective-permute-start(bf16[32,128]{1,0:T(8,128)(2,1)S(1)} %shard_map.65), channel_id=1, source_target_pairs={{8,13},{9,12},{10,15},{11,14}} | collective-permute-start | bytes 24584 | tf_op jit(solution)/shard_map/ppermute | solution.py:278
  36.1 3.9 %collective-permute-start.17 = (bf16[32,2048]{1,0:T(8,128)(2,1)S(1)}, bf16[32,2048]{1,0:T(8,128)(2,1)S(1)}, u32[]{:S(2)}, u32[]{:S(2)}) collective-permute-start(bf16[32,2048]{1,0:T(8,128)(2,1)S(1)} %get-tuple-element.112.refs_0_), channel_id=1, source_target_pairs={{12,16},{13,17},{14,18},{15,19}} | collective-permute-start | bytes 393224 | tf_op jit(solution)/shard_map/ppermute | solution.py:278
  37.1 3.9 %collective-permute-start.18 = (bf16[32,2048]{1,0:T(8,128)(2,1)S(1)}, bf16[32,2048]{1,0:T(8,128)(2,1)S(1)}, u32[]{:S(2)}, u32[]{:S(2)}) collective-permute-start(bf16[32,2048]{1,0:T(8,128)(2,1)S(1)} %get-tuple-element.119.refs_1_), channel_id=1, source_target_pairs={{12,16},{13,17},{14,18},{15,19}} | collective-permute-start | bytes 393224 | tf_op jit(solution)/shard_map/ppermute | solution.py:278
  38.0 3.9 %collective-permute-start.19 = (bf16[32,128]{1,0:T(8,128)(2,1)S(1)}, bf16[32,128]{1,0:T(8,128)(2,1)S(1)}, u32[]{:S(2)}, u32[]{:S(2)}) collective-permute-start(bf16[32,128]{1,0:T(8,128)(2,1)S(1)} %shard_map.70), channel_id=1, source_target_pairs={{12,19},{13,18},{14,17},{15,16}} | collective-permute-start | bytes 24584 | tf_op jit(solution)/shard_map/ppermute | solution.py:278
  38.7 3.2 %collective-permute-start.20 = (bf16[32,128]{1,0:T(8,128)(2,1)S(1)}, bf16[32,128]{1,0:T(8,128)(2,1)S(1)}, u32[]{:S(2)}, u32[]{:S(2)}) collective-permute-start(bf16[32,128]{1,0:T(8,128)(2,1)S(1)} %shard_map.70), channel_id=1, source_target_pairs={{12,18},{13,19},{14,16},{15,17}} | collective-permute-start | bytes 24584 | tf_op jit(solution)/shard_map/ppermute | solution.py:278
  39.4 2.5 %collective-permute-start.21 = (bf16[32,128]{1,0:T(8,128)(2,1)S(1)}, bf16[32,128]{1,0:T(8,128)(2,1)S(1)}, u32[]{:S(2)}, u32[]{:S(2)}) collective-permute-start(bf16[32,128]{1,0:T(8,128)(2,1)S(1)} %shard_map.70), channel_id=1, source_target_pairs={{12,17},{13,16},{14,19},{15,18}} | collective-permute-start | bytes 24584 | tf_op jit(solution)/shard_map/ppermute | solution.py:278
  42.2 4.1 %collective-permute-start.22 = (bf16[32,2048]{1,0:T(8,128)(2,1)S(1)}, bf16[32,2048]{1,0:T(8,128)(2,1)S(1)}, u32[]{:S(2)}, u32[]{:S(2)}) collective-permute-start(bf16[32,2048]{1,0:T(8,128)(2,1)S(1)} %get-tuple-element.122.refs_0_), channel_id=1, source_target_pairs={{16,20},{17,21},{18,22},{19,23}} | collective-permute-start | bytes 393224 | tf_op jit(solution)/shard_map/ppermute | solution.py:278
  43.2 4.1 %collective-permute-start.23 = (bf16[32,2048]{1,0:T(8,128)(2,1)S(1)}, bf16[32,2048]{1,0:T(8,128)(2,1)S(1)}, u32[]{:S(2)}, u32[]{:S(2)}) collective-permute-start(bf16[32,2048]{1,0:T(8,128)(2,1)S(1)} %get-tuple-element.128.refs_1_), channel_id=1, source_target_pairs={{16,20},{17,21},{18,22},{19,23}} | collective-permute-start | bytes 393224 | tf_op jit(solution)/shard_map/ppermute | solution.py:278
  44.1 4.0 %collective-permute-start.24 = (bf16[32,128]{1,0:T(8,128)(2,1)S(1)}, bf16[32,128]{1,0:T(8,128)(2,1)S(1)}, u32[]{:S(2)}, u32[]{:S(2)}) collective-permute-start(bf16[32,128]{1,0:T(8,128)(2,1)S(1)} %shard_map.75), channel_id=1, source_target_pairs={{16,23},{17,22},{18,21},{19,20}} | collective-permute-start | bytes 24584 | tf_op jit(solution)/shard_map/ppermute | solution.py:278
  44.8 3.4 %collective-permute-start.25 = (bf16[32,128]{1,0:T(8,128)(2,1)S(1)}, bf16[32,128]{1,0:T(8,128)(2,1)S(1)}, u32[]{:S(2)}, u32[]{:S(2)}) collective-permute-start(bf16[32,128]{1,0:T(8,128)(2,1)S(1)} %shard_map.75), channel_id=1, source_target_pairs={{16,22},{17,23},{18,20},{19,21}} | collective-permute-start | bytes 24584 | tf_op jit(solution)/shard_map/ppermute | solution.py:278
  45.6 2.5 %collective-permute-start.26 = (bf16[32,128]{1,0:T(8,128)(2,1)S(1)}, bf16[32,128]{1,0:T(8,128)(2,1)S(1)}, u32[]{:S(2)}, u32[]{:S(2)}) collective-permute-start(bf16[32,128]{1,0:T(8,128)(2,1)S(1)} %shard_map.75), channel_id=1, source_target_pairs={{16,21},{17,20},{18,23},{19,22}} | collective-permute-start | bytes 24584 | tf_op jit(solution)/shard_map/ppermute | solution.py:278
  48.6 3.0 %collective-permute-start.27 = (bf16[32,4096]{1,0:T(8,128)(2,1)S(1)}, bf16[32,4096]{1,0:T(8,128)(2,1)S(1)}, u32[]{:S(2)}, u32[]{:S(2)}) collective-permute-start(bf16[32,4096]{1,0:T(8,128)(2,1)S(1)} %get-tuple-element.133.refs_0_), channel_id=1, source_target_pairs={{20,24},{21,25},{22,26},{23,27}} | collective-permute-start | bytes 786440 | tf_op jit(solution)/shard_map/ppermute | solution.py:278
  49.6 3.9 %collective-permute-start.28 = (bf16[32,128]{1,0:T(8,128)(2,1)S(1)}, bf16[32,128]{1,0:T(8,128)(2,1)S(1)}, u32[]{:S(2)}, u32[]{:S(2)}) collective-permute-start(bf16[32,128]{1,0:T(8,128)(2,1)S(1)} %shard_map.79), channel_id=1, source_target_pairs={{20,27},{21,26},{22,25},{23,24}} | collective-permute-start | bytes 24584 | tf_op jit(solution)/shard_map/ppermute | solution.py:278
  50.3 3.2 %collective-permute-start.29 = (bf16[32,128]{1,0:T(8,128)(2,1)S(1)}, bf16[32,128]{1,0:T(8,128)(2,1)S(1)}, u32[]{:S(2)}, u32[]{:S(2)}) collective-permute-start(bf16[32,128]{1,0:T(8,128)(2,1)S(1)} %shard_map.79), channel_id=1, source_target_pairs={{20,26},{21,27},{22,24},{23,25}} | collective-permute-start | bytes 24584 | tf_op jit(solution)/shard_map/ppermute | solution.py:278
  50.9 2.5 %collective-permute-start.30 = (bf16[32,128]{1,0:T(8,128)(2,1)S(1)}, bf16[32,128]{1,0:T(8,128)(2,1)S(1)}, u32[]{:S(2)}, u32[]{:S(2)}) collective-permute-start(bf16[32,128]{1,0:T(8,128)(2,1)S(1)} %shard_map.79), channel_id=1, source_target_pairs={{20,25},{21,24},{22,27},{23,26}} | collective-permute-start | bytes 24584 | tf_op jit(solution)/shard_map/ppermute | solution.py:278
  53.7 36.0 %collective-permute-start.31 = (bf16[32,2048]{1,0:T(8,128)(2,1)S(1)}, bf16[32,2048]{1,0:T(8,128)(2,1)S(1)}, u32[]{:S(2)}, u32[]{:S(2)}) collective-permute-start(bf16[32,2048]{1,0:T(8,128)(2,1)S(1)} %get-tuple-element.140.refs_0_), channel_id=1, source_target_pairs={{24,28},{25,29},{26,30},{27,31}} | collective-permute-start | bytes 393224 | tf_op jit(solution)/shard_map/ppermute | solution.py:278
  55.3 36.1 %collective-permute-start.32 = (bf16[32,2048]{1,0:T(8,128)(2,1)S(1)}, bf16[32,2048]{1,0:T(8,128)(2,1)S(1)}, u32[]{:S(2)}, u32[]{:S(2)}) collective-permute-start(bf16[32,2048]{1,0:T(8,128)(2,1)S(1)} %get-tuple-element.145.refs_1_), channel_id=1, source_target_pairs={{24,28},{25,29},{26,30},{27,31}} | collective-permute-start | bytes 393224 | tf_op jit(solution)/shard_map/ppermute | solution.py:278
  56.9 35.4 %collective-permute-start.33 = (bf16[32,128]{1,0:T(8,128)(2,1)S(1)}, bf16[32,128]{1,0:T(8,128)(2,1)S(1)}, u32[]{:S(2)}, u32[]{:S(2)}) collective-permute-start(bf16[32,128]{1,0:T(8,128)(2,1)S(1)} %shard_map.84), channel_id=1, source_target_pairs={{24,31},{25,30},{26,29},{27,28}} | collective-permute-start | bytes 24584 | tf_op jit(solution)/shard_map/ppermute | solution.py:278
  58.2 34.1 %collective-permute-start.34 = (bf16[32,128]{1,0:T(8,128)(2,1)S(1)}, bf16[32,128]{1,0:T(8,128)(2,1)S(1)}, u32[]{:S(2)}, u32[]{:S(2)}) collective-permute-start(bf16[32,128]{1,0:T(8,128)(2,1)S(1)} %shard_map.84), channel_id=1, source_target_pairs={{24,30},{25,31},{26,28},{27,29}} | collective-permute-start | bytes 24584 | tf_op jit(solution)/shard_map/ppermute | solution.py:278
  59.5 32.8 %collective-permute-start.35 = (bf16[32,128]{1,0:T(8,128)(2,1)S(1)}, bf16[32,128]{1,0:T(8,128)(2,1)S(1)}, u32[]{:S(2)}, u32[]{:S(2)}) collective-permute-start(bf16[32,128]{1,0:T(8,128)(2,1)S(1)} %shard_map.84), channel_id=1, source_target_pairs={{24,29},{25,28},{26,31},{27,30}} | collective-permute-start | bytes 24584 | tf_op jit(solution)/shard_map/ppermute | solution.py:278
